TPU v7x, 32 devices: a whole 2x2x4 slice. The times are simulated.
32 devices in a mesh: fsdp: 4 (over x, core), ctx: 8 (over z, y).
Axes of the slice: x: 2, y: 2, z: 4, core: 2. Of those that a mesh axis runs over, the one named last changes fastest.
Arguments:
- tokens: bfloat16 [5120, 2048], P(('fsdp', 'ctx')), may hold values from -6 to 6
- first_gain: bfloat16 [2048], P('fsdp'), may hold values from 0.099609375 to 1.8984375
- query_weight: bfloat16 [2048, 2048], P('fsdp'), may hold values from -0.125 to 0.125
- key_matrix: bfloat16 [2048, 512], P('fsdp'), may hold values from -0.125 to 0.125
- value_matrix: bfloat16 [2048, 512], P('fsdp'), may hold values from -0.125 to 0.125
- out_weight: bfloat16 [2048, 2048], P('fsdp'), may hold values from -1 to 1
- second_gain: bfloat16 [2048], P('fsdp'), may hold values from 0.099609375 to 1.8984375
- gate_weight: bfloat16 [2048, 8192], P('fsdp'), may hold values from -0.125 to 0.125
- up_weight: bfloat16 [2048, 8192], P('fsdp'), may hold values from -0.125 to 0.125
- down_weight: bfloat16 [8192, 2048], P('fsdp'), may hold values from -0.0625 to 0.0625
- lengths: int32 [4, 4], P('fsdp'), may hold values from 1 to 1024, as said below
- block_order: int32 [16], replicated, may hold values from 0 to 15, as said below
- cotangent: bfloat16 [5120, 2048], P(('fsdp', 'ctx')), may hold values from -6 to 6
Outputs:
- layer_out: bfloat16 [5120, 2048], P(('fsdp', 'ctx'))
- tokens_grad: float32 [5120, 2048], P(('fsdp', 'ctx'))
- first_gain_grad: float32 [2048], P(('fsdp', 'ctx'))
- query_grad: float32 [2048, 2048], P(('fsdp', 'ctx'))
- key_grad: float32 [2048, 512], P(('fsdp', 'ctx'))
- value_grad: float32 [2048, 512], P(('fsdp', 'ctx'))
- out_grad: float32 [2048, 2048], P(('fsdp', 'ctx'))
- second_gain_grad: float32 [2048], P(('fsdp', 'ctx'))
- gate_grad: float32 [2048, 8192], P(('fsdp', 'ctx'))
- up_grad: float32 [2048, 8192], P(('fsdp', 'ctx'))
- down_grad: float32 [8192, 2048], P(('fsdp', 'ctx'))
Inputs may be any that keep to these rules, and one draw needn't show every extreme that they name: Each row holds the lengths of the 4 sequences packed one after another in one group; they sum to 1280, and the first is exactly 1024, the longest. `block_order`: A permutation of the 16 blocks in which entry 2c is below 8 and entry 2c + 1 equals 15 minus entry 2c.
All inputs are finite; a program needn't handle non-finite values.
Results may differ from a plain program's by a relative error of at most 0.02.
Values may be sent and summed in bfloat16 or wider, within the bound.
No kernel may reach another device: no remote copies, remote signals or barrier semaphores. Data moves between devices by JAX's collectives and lax.ppermute only.
A program may use at most 576 MiB of HBM per device.

v0:
```python
import math

import jax
import jax.numpy as jnp
from jax import lax
from jax.sharding import PartitionSpec as P

QUERY_HEADS = 32
KEY_VALUE_HEADS = 8
HEAD_SIZE = 64


NORM_EPS = 1e-05
ROPE_BASE = 500000.0
MASKED_SCORE = -1e30


def as_sent(value):

    def short(part):
        return part.astype(jnp.bfloat16) if part.dtype == jnp.float32 else part

    return jax.tree.map(short, value)


def rope_tables(position):
    freqs = ROPE_BASE ** (-(jnp.arange(HEAD_SIZE // 2, dtype=jnp.float32) * 2.0 / HEAD_SIZE))
    angle = position.astype(jnp.float32)[:, None] * freqs[None, :]
    return (jnp.cos(angle)[:, None, :], jnp.sin(angle)[:, None, :])


def apply_rotary(rotated_in, cosine_table, sine_values):
    half_size = rotated_in.shape[-1] // 2
    first_half = rotated_in[..., :half_size]
    second_half = rotated_in[..., half_size:]
    return jnp.concatenate(
        [
            first_half * cosine_table - second_half * sine_values,
            second_half * cosine_table + first_half * sine_values,
        ],
        axis=-1,
    )


def packed_rows(order_part, block_rows):
    offsets = jnp.arange(block_rows, dtype=jnp.int32)
    return (order_part[:, None] * block_rows + offsets[None, :]).reshape(-1)


def sequence_place(packed, seq_lengths):
    seq_ends = jnp.cumsum(seq_lengths)
    seq_starts = seq_ends - seq_lengths
    seq_ids = jnp.sum((packed[:, None] >= seq_ends[None, :]).astype(jnp.int32), axis=1)
    onehot_seq = (
        seq_ids[:, None] == jnp.arange(seq_lengths.shape[0], dtype=jnp.int32)[None, :]
    ).astype(jnp.int32)
    return (seq_ids, packed - jnp.sum(onehot_seq * seq_starts[None, :], axis=1))


def rms_scale(value_rows):
    return lax.rsqrt(jnp.mean(value_rows * value_rows, axis=-1, keepdims=True) + NORM_EPS)


def norm_back(grad_normed, normed, inverse):
    return inverse * (grad_normed - normed * jnp.mean(grad_normed * normed, axis=-1, keepdims=True))


def matrix_product(left_in, right_in):
    return jnp.dot(left_in, right_in, preferred_element_type=jnp.float32)


def matmul_nt(left_in, right_in):
    return lax.dot_general(
        left_in, right_in, (((1,), (1,)), ((), ())), preferred_element_type=jnp.float32
    )


def matmul_tn(left_in, right_in):
    return lax.dot_general(
        left_in, right_in, (((0,), (0,)), ((), ())), preferred_element_type=jnp.float32
    )


def fetch_front(first_gain, query_weight, key_matrix, value_matrix):
    return (
        lax.all_gather(first_gain, "fsdp", axis=0, tiled=True),
        lax.all_gather(query_weight, "fsdp", axis=0, tiled=True),
        lax.all_gather(key_matrix, "fsdp", axis=0, tiled=True),
        lax.all_gather(value_matrix, "fsdp", axis=0, tiled=True),
    )


def fetch_middle(out_weight, second_gain, gate_weight, up_weight):
    return (
        lax.all_gather(out_weight, "fsdp", axis=0, tiled=True),
        lax.all_gather(second_gain, "fsdp", axis=0, tiled=True),
        lax.all_gather(gate_weight, "fsdp", axis=0, tiled=True),
        lax.all_gather(up_weight, "fsdp", axis=0, tiled=True),
    )


def fetch_down(down_weight):
    return lax.all_gather(down_weight, "fsdp", axis=0, tiled=True)


def reduce_small(terms):
    within = jax.tree.map(
        lambda part: part.astype(jnp.float32),
        lax.psum_scatter(as_sent(terms), "fsdp", scatter_dimension=0, tiled=True),
    )
    return jax.tree.map(
        lambda part: part.astype(jnp.float32),
        lax.psum_scatter(as_sent(within), "ctx", scatter_dimension=0, tiled=True),
    )


def reduce_large(left_in, right_in):
    within = lax.psum_scatter(
        matmul_tn(left_in, right_in).astype(jnp.bfloat16), "fsdp", scatter_dimension=0, tiled=True
    )
    return lax.psum_scatter(within, "ctx", scatter_dimension=0, tiled=True).astype(jnp.float32)


def body(
    tokens,
    first_gain,
    query_weight,
    key_matrix,
    value_matrix,
    out_weight,
    second_gain,
    gate_weight,
    up_weight,
    down_weight,
    lengths,
    block_order,
    cotangent,
):
    token_rows = tokens.shape[0]
    block_rows = token_rows // 2
    kv_width = key_matrix.shape[1]
    heads_per_group = QUERY_HEADS // KEY_VALUE_HEADS
    score_scale = 1.0 / math.sqrt(HEAD_SIZE)
    ctx_index = lax.axis_index("ctx")
    own_blocks = lax.dynamic_slice_in_dim(block_order, 2 * ctx_index, 2)
    packed_query = packed_rows(own_blocks, block_rows)
    packed_key = packed_rows(block_order, block_rows)
    seq_query, position = sequence_place(packed_query, lengths[0])
    seq_key = sequence_place(packed_key, lengths[0])[0]
    allowed = (seq_query[:, None] == seq_key[None, :]) & (
        packed_key[None, :] <= packed_query[:, None]
    )
    cosine_table, sine_values = rope_tables(position)
    front_weights_full = fetch_front(first_gain, query_weight, key_matrix, value_matrix)
    gain_one = front_weights_full[0].astype(jnp.float32)
    inputs_f = tokens.astype(jnp.float32)
    inverse_one = rms_scale(inputs_f)
    normed_one = inputs_f * inverse_one
    first_hidden = (normed_one * gain_one).astype(jnp.bfloat16)
    query_pre = matrix_product(first_hidden, front_weights_full[1]).reshape(
        token_rows, QUERY_HEADS, HEAD_SIZE
    )
    key_before_rotary = matrix_product(first_hidden, front_weights_full[2]).reshape(
        token_rows, KEY_VALUE_HEADS, HEAD_SIZE
    )
    query_rows = apply_rotary(query_pre, cosine_table, sine_values).astype(jnp.bfloat16)
    key_row_matrix = (
        apply_rotary(key_before_rotary, cosine_table, sine_values)
        .astype(jnp.bfloat16)
        .reshape(token_rows, kv_width)
    )
    value_rows = matrix_product(first_hidden, front_weights_full[3]).astype(jnp.bfloat16)
    gathered_keys, gathered_values = (
        lax.all_gather(key_row_matrix, "ctx", axis=0, tiled=True),
        lax.all_gather(value_rows, "ctx", axis=0, tiled=True),
    )
    key_total_count = gathered_keys.shape[0]
    query_head_rows = query_rows.reshape(
        token_rows, KEY_VALUE_HEADS, heads_per_group, HEAD_SIZE
    ).transpose(1, 0, 2, 3)
    key_head_rows = gathered_keys.reshape(key_total_count, KEY_VALUE_HEADS, HEAD_SIZE).transpose(
        1, 0, 2
    )
    value_head_rows = gathered_values.reshape(
        key_total_count, KEY_VALUE_HEADS, HEAD_SIZE
    ).transpose(1, 0, 2)

    def head_forward(head_args):
        head_query, head_key, head_value = head_args
        raw_scores = jnp.einsum(
            "qrd,td->qrt", head_query, head_key, preferred_element_type=jnp.float32
        )
        scores = jnp.where(allowed[:, None, :], raw_scores * score_scale, MASKED_SCORE)
        row_peak = jnp.max(scores, axis=-1, keepdims=True)
        expd_rows = jnp.exp(scores - row_peak)
        row_total = jnp.sum(expd_rows, axis=-1, keepdims=True)
        weights = (expd_rows / row_total).astype(jnp.bfloat16)
        mixed_rows = jnp.einsum(
            "qrt,td->qrd", weights, head_value, preferred_element_type=jnp.float32
        )
        return (mixed_rows, (row_peak + jnp.log(row_total))[..., 0])

    head_out, head_lse = lax.map(head_forward, (query_head_rows, key_head_rows, value_head_rows))
    attended = (
        head_out.transpose(1, 0, 2, 3)
        .reshape(token_rows, QUERY_HEADS * HEAD_SIZE)
        .astype(jnp.bfloat16)
    )
    middle_full = fetch_middle(out_weight, second_gain, gate_weight, up_weight)
    residual = inputs_f + matrix_product(attended, middle_full[0])
    inverse_two = rms_scale(residual)
    normed_two = residual * inverse_two
    gain_two = middle_full[1].astype(jnp.float32)
    hidden_two = (normed_two * gain_two).astype(jnp.bfloat16)
    gate_proj = matrix_product(hidden_two, middle_full[2])
    up_proj = matrix_product(hidden_two, middle_full[3])
    gate_sig = jax.nn.sigmoid(gate_proj)
    activated = (gate_proj * gate_sig * up_proj).astype(jnp.bfloat16)
    down_full = fetch_down(down_weight)
    layer_out = (residual + matrix_product(activated, down_full)).astype(jnp.bfloat16)
    grad_outf = cotangent.astype(jnp.float32)
    down_full = fetch_down(down_weight)
    down_grad = reduce_large(activated, cotangent)
    grad_act = matmul_nt(cotangent, down_full)
    grad_gate = (grad_act * up_proj * gate_sig * (1.0 + gate_proj * (1.0 - gate_sig))).astype(
        jnp.bfloat16
    )
    grad_up = (grad_act * gate_proj * gate_sig).astype(jnp.bfloat16)
    middle_full = fetch_middle(out_weight, second_gain, gate_weight, up_weight)
    gate_grad = reduce_large(hidden_two, grad_gate)
    up_grad = reduce_large(hidden_two, grad_up)
    grad_hidden_two = matmul_nt(grad_gate, middle_full[2]) + matmul_nt(grad_up, middle_full[3])
    gain_two_term = jnp.sum(grad_hidden_two * normed_two, axis=0)
    grad_residual = grad_outf + norm_back(grad_hidden_two * gain_two, normed_two, inverse_two)
    grad_branch = grad_residual.astype(jnp.bfloat16)
    out_term = matmul_tn(attended, grad_branch)
    out_grad, second_gain_grad = reduce_small((out_term, gain_two_term))
    attended_gradient = matmul_nt(grad_branch, middle_full[0]).astype(jnp.bfloat16)
    head_gradients = attended_gradient.reshape(
        token_rows, KEY_VALUE_HEADS, heads_per_group, HEAD_SIZE
    ).transpose(1, 0, 2, 3)

    def head_backward(head_args):
        head_query, head_key, head_value, head_grad, head_logsum = head_args
        raw_scores = jnp.einsum(
            "qrd,td->qrt", head_query, head_key, preferred_element_type=jnp.float32
        )
        scores = jnp.where(allowed[:, None, :], raw_scores * score_scale, MASKED_SCORE)
        prob_rows = jnp.exp(scores - head_logsum[..., None])
        grad_probs = jnp.einsum(
            "qrd,td->qrt", head_grad, head_value, preferred_element_type=jnp.float32
        )
        row_dot = jnp.sum(prob_rows * grad_probs, axis=-1, keepdims=True)
        grad_scores = (prob_rows * (grad_probs - row_dot) * score_scale).astype(jnp.bfloat16)
        grad_query_head = jnp.einsum(
            "qrt,td->qrd", grad_scores, head_key, preferred_element_type=jnp.float32
        )
        grad_key_head = jnp.einsum(
            "qrt,qrd->td", grad_scores, head_query, preferred_element_type=jnp.float32
        )
        grad_value_head = jnp.einsum(
            "qrt,qrd->td",
            prob_rows.astype(jnp.bfloat16),
            head_grad,
            preferred_element_type=jnp.float32,
        )
        return (grad_query_head, grad_key_head, grad_value_head)

    grad_q_heads, grad_k_heads, grad_v_heads = lax.map(
        head_backward, (query_head_rows, key_head_rows, value_head_rows, head_gradients, head_lse)
    )
    grad_key_part = grad_k_heads.transpose(1, 0, 2).reshape(key_total_count, kv_width)
    grad_value_part = grad_v_heads.transpose(1, 0, 2).reshape(key_total_count, kv_width)
    local_key_gradient, grad_value_own = (
        lax.psum_scatter(grad_key_part, "ctx", scatter_dimension=0, tiled=True),
        lax.psum_scatter(grad_value_part, "ctx", scatter_dimension=0, tiled=True),
    )
    grad_query_rows = grad_q_heads.transpose(1, 0, 2, 3).reshape(token_rows, QUERY_HEADS, HEAD_SIZE)
    grad_query = (
        apply_rotary(grad_query_rows, cosine_table, -sine_values)
        .astype(jnp.bfloat16)
        .reshape(token_rows, QUERY_HEADS * HEAD_SIZE)
    )
    grad_key = (
        apply_rotary(
            local_key_gradient.reshape(token_rows, KEY_VALUE_HEADS, HEAD_SIZE),
            cosine_table,
            -sine_values,
        )
        .astype(jnp.bfloat16)
        .reshape(token_rows, kv_width)
    )
    grad_value = grad_value_own.astype(jnp.bfloat16)
    front_weights_full = fetch_front(first_gain, query_weight, key_matrix, value_matrix)
    grad_hidden_one = (
        matmul_nt(grad_query, front_weights_full[1])
        + matmul_nt(grad_key, front_weights_full[2])
        + matmul_nt(grad_value, front_weights_full[3])
    )
    gain_one_term = jnp.sum(grad_hidden_one * normed_one, axis=0)
    tokens_grad = grad_residual + norm_back(grad_hidden_one * gain_one, normed_one, inverse_one)
    query_term = matmul_tn(first_hidden, grad_query)
    key_term = matmul_tn(first_hidden, grad_key)
    value_term = matmul_tn(first_hidden, grad_value)
    first_gain_grad, query_grad, key_grad, value_grad = reduce_small(
        (gain_one_term, query_term, key_term, value_term)
    )
    return (
        layer_out,
        tokens_grad,
        first_gain_grad,
        query_grad,
        key_grad,
        value_grad,
        out_grad,
        second_gain_grad,
        gate_grad,
        up_grad,
        down_grad,
    )


def solution(mesh):
    placed = (
        P(("fsdp", "ctx"), None),
        P("fsdp"),
        P("fsdp", None),
        P("fsdp", None),
        P("fsdp", None),
        P("fsdp", None),
        P("fsdp"),
        P("fsdp", None),
        P("fsdp", None),
        P("fsdp", None),
        P("fsdp", None),
        P(),
        P(("fsdp", "ctx"), None),
    )
    return jax.shard_map(
        body,
        mesh=mesh,
        in_specs=placed,
        out_specs=(
            P(("fsdp", "ctx"), None),
            P(("fsdp", "ctx"), None),
            P(("fsdp", "ctx")),
            P(("fsdp", "ctx"), None),
            P(("fsdp", "ctx"), None),
            P(("fsdp", "ctx"), None),
            P(("fsdp", "ctx"), None),
            P(("fsdp", "ctx")),
            P(("fsdp", "ctx"), None),
            P(("fsdp", "ctx"), None),
            P(("fsdp", "ctx"), None),
        ),
        check_vma=False,
    )
```

profile of v0, /device:TPU:0, one launch (start us, length us, event | category | flops | bytes accessed | tf_op | source)
XLA Modules:
  0.0 2891.1 jit_solution(7711629399974170317)
XLA Ops:
  38.9 20.2 all-gather.18.cloned.1.call-done
  72.6 31.1 %all-gather.16.cloned.1.call-done = bf16[1280,512]{1,0:T(8,128)(2,1)} async-done(((bf16[160,512]{1,0:T(8,128)(2,1)}), bf16[1280,512]{1,0:T(8,128)(2,1)}) %all-gather.16.cloned.1.call-update) | async-done | bytes 1310736 | tf_op jit(solution)/shard_map/all_gather | solution.py:174
  106.3 40.5 %all-gather.20.cloned.1.call-done = bf16[1280,512]{1,0:T(8,128)(2,1)} async-done(((bf16[160,512]{1,0:T(8,128)(2,1)}), bf16[1280,512]{1,0:T(8,128)(2,1)}) %all-gather.20.cloned.1.call-update) | async-done | bytes 1310736 | tf_op jit(solution)/shard_map/all_gather | solution.py:175
  149.2 55.9 %all-gather.12.cloned.1.call-done = bf16[2048,2048]{1,0:T(8,128)(2,1)} async-done(((bf16[512,2048]{1,0:T(8,128)(2,1)}), bf16[2048,2048]{1,0:T(8,128)(2,1)}) %all-gather.12.cloned.1.call-update) | async-done | bytes 8388624 | tf_op jit(solution)/shard_map/all_gather | solution.py:87
  221.3 46.5 %while.30 = (s32[]{:T(128)}, bf16[8,160,4,64]{1,3,2,0:T(8,128)(2,1)S(1)}, f32[8,160,4]{1,2,0:T(4,128)}, bf16[8,160,4,64]{1,3,2,0:T(8,128)(2,1)S(1)}, bf16[8,1280...) while((s32[]{:T(128)}, ...), condition=%wide.region_8.9_spmd.clone.clone, body=%wide.region_5.8_spmd.clone.sunk.clone | while | flops 216882560 | bytes 10999665 | solution.py:203
  274.0 194.0 %all-gather.24.cloned.1.call-done = bf16[2048,8192]{1,0:T(8,128)(2,1)} async-done(((bf16[512,8192]{1,0:T(8,128)(2,1)}), bf16[2048,8192]{1,0:T(8,128)(2,1)}) %all-gather.24.cloned.1.call-update) | async-done | bytes 33554448 | tf_op jit(solution)/shard_map/all_gather | solution.py:97
  487.7 183.5 %all-gather.26.cloned.1.call-done = bf16[2048,8192]{1,0:T(8,128)(2,1)} async-done(((bf16[512,8192]{1,0:T(8,128)(2,1)}), bf16[2048,8192]{1,0:T(8,128)(2,1)}) %all-gather.26.cloned.1.call-update) | async-done | bytes 33554448 | tf_op jit(solution)/shard_map/all_gather | solution.py:98
  691.0 183.3 %all-gather.28.cloned.1.call-done = bf16[8192,2048]{1,0:T(8,128)(2,1)} async-done(((bf16[2048,2048]{1,0:T(8,128)(2,1)}), bf16[8192,2048]{1,0:T(8,128)(2,1)}) %all-gather.28.cloned.1.call-update) | async-done | bytes 33554448 | tf_op jit(solution)/shard_map/all_gather | solution.py:103
  874.3 22.3 multiply_convert_fusion
  941.7 138.7 %while.31 = (s32[]{:T(128)}, f32[8,160,4,64]{1,3,2,0:T(8,128)}, f32[8,1280,64]{1,2,0:T(8,128)}, f32[8,1280,64]{1,2,0:T(8,128)}, bf16[8,160,4,64]{1,3,2,0:T(8,128...) while((s32[]{:T(128)}, f32[8,160,4,64]{1,3,2,0:T(8,128)}, ...), condition=%wide.region_13.14_spmd.clone.clone, body=%wide.region_11.13_spmd.clone.sunk.clone | while | flops 536375040 | bytes 38412168 | solution.py:269
  1087.5 66.8 %reduce-scatter.25.cloned.1.call-done = f32[160,512]{1,0:T(8,128)} async-done(((f32[1280,512]{1,0:T(8,128)}), f32[160,512]{1,0:T(8,128)}) %reduce-scatter.25.cloned.1.call-update) | async-done | bytes 327696 | tf_op jit(solution)/shard_map/reduce_scatter | solution.py:275
  1158.5 68.6 %reduce-scatter.49.cloned.1.call-done = f32[160,512]{1,0:T(8,128)} async-done(((f32[1280,512]{1,0:T(8,128)}), f32[160,512]{1,0:T(8,128)}) %reduce-scatter.49.cloned.1.call-update) | async-done | bytes 327696
  1301.6 67.7 %reduce-scatter.27.cloned.1.call-done = bf16[512,2048]{1,0:T(8,128)(2,1)} async-done(((bf16[2048,2048]{1,0:T(8,128)(2,1)}), bf16[512,2048]{1,0:T(8,128)(2,1)}) %reduce-scatter.27.cloned.1.call-update) | async-done | bytes 2097168 | tf_op jit(solution)/shard_map/reduce_scatter | solution.py:109
  1369.4 74.3 %reduce-scatter.39.cloned.1.call-done = bf16[512,2048]{1,0:T(8,128)(2,1)} async-done(((bf16[2048,2048]{1,0:T(8,128)(2,1)}), bf16[512,2048]{1,0:T(8,128)(2,1)}) %reduce-scatter.39.cloned.1.call-update) | async-done | bytes 2097168 | tf_op jit(solution)/shard_map/reduce_scatter | solution.py:109
  1443.7 237.3 %reduce-scatter.51.cloned.1.call-done = bf16[512,8192]{1,0:T(8,128)(2,1)} async-done(((bf16[2048,8192]{1,0:T(8,128)(2,1)}), bf16[512,8192]{1,0:T(8,128)(2,1)}) %reduce-scatter.51.cloned.1.call-update) | async-done | bytes 8388624
  1681.1 237.3 %reduce-scatter.53.cloned.1.call-done = bf16[512,8192]{1,0:T(8,128)(2,1)} async-done(((bf16[2048,8192]{1,0:T(8,128)(2,1)}), bf16[512,8192]{1,0:T(8,128)(2,1)}) %reduce-scatter.53.cloned.1.call-update) | async-done | bytes 8388624
  1918.4 237.3 %reduce-scatter.55.cloned.1.call-done = bf16[2048,2048]{1,0:T(8,128)(2,1)} async-done(((bf16[8192,2048]{1,0:T(8,128)(2,1)}), bf16[2048,2048]{1,0:T(8,128)(2,1)}) %reduce-scatter.55.cloned.1.call-update) | async-done | bytes 8388624
  2189.7 21.6 all-reduce.7
  2222.5 63.0 %reduce-scatter.37.cloned.1.call-done = bf16[64,512]{1,0:T(8,128)(2,1)} async-done(((bf16[512,512]{1,0:T(8,128)(2,1)}), bf16[64,512]{1,0:T(8,128)(2,1)}) %reduce-scatter.37.cloned.1.call-update) | async-done | bytes 65552 | tf_op jit(solution)/shard_map/reduce_scatter | solution.py:113
  2287.0 68.7 %reduce-scatter.29.cloned.1.call-done = bf16[64,2048]{1,0:T(8,128)(2,1)} async-done(((bf16[512,2048]{1,0:T(8,128)(2,1)}), bf16[64,2048]{1,0:T(8,128)(2,1)}) %reduce-scatter.29.cloned.1.call-update) | async-done | bytes 262160 | tf_op jit(solution)/shard_map/reduce_scatter | solution.py:113
  2357.5 68.7 %reduce-scatter.41.cloned.1.call-done = bf16[64,2048]{1,0:T(8,128)(2,1)} async-done(((bf16[512,2048]{1,0:T(8,128)(2,1)}), bf16[64,2048]{1,0:T(8,128)(2,1)}) %reduce-scatter.41.cloned.1.call-update) | async-done | bytes 262160 | tf_op jit(solution)/shard_map/reduce_scatter | solution.py:113
  2428.1 149.9 %reduce-scatter.43.cloned.1.call-done = bf16[64,8192]{1,0:T(8,128)(2,1)} async-done(((bf16[512,8192]{1,0:T(8,128)(2,1)}), bf16[64,8192]{1,0:T(8,128)(2,1)}) %reduce-scatter.43.cloned.1.call-update) | async-done | bytes 1048592 | tf_op jit(solution)/shard_map/reduce_scatter | solution.py:121
  2580.6 149.3 %reduce-scatter.45.cloned.1.call-done = bf16[64,8192]{1,0:T(8,128)(2,1)} async-done(((bf16[512,8192]{1,0:T(8,128)(2,1)}), bf16[64,8192]{1,0:T(8,128)(2,1)}) %reduce-scatter.45.cloned.1.call-update) | async-done | bytes 1048592 | tf_op jit(solution)/shard_map/reduce_scatter | solution.py:121
  2732.6 149.0 %reduce-scatter.47.cloned.1.call-done = bf16[256,2048]{1,0:T(8,128)(2,1)} async-done(((bf16[2048,2048]{1,0:T(8,128)(2,1)}), bf16[256,2048]{1,0:T(8,128)(2,1)}) %reduce-scatter.47.cloned.1.call-update) | async-done | bytes 1048592 | tf_op jit(solution)/shard_map/reduce_scatter | solution.py:121
  (322 shorter events, 484.5 us)
Async XLA Ops:
  7.9 51.2 %all-gather.18.cloned.1.call-start = ((), (), s32[]{:S(2)}) async-start(), calls=%async_computation.19 | async-start | bytes 2621440 | tf_op jit(solution)/shard_map/all_gather | solution.py:89
  8.7 95.0 %all-gather.16.cloned.1.call-start = ((), (), s32[]{:S(2)}) async-start(), calls=%async_computation.18 | async-start | bytes 1474560 | tf_op jit(solution)/shard_map/all_gather | solution.py:174
  38.9 107.9 %all-gather.20.cloned.1.call-start = ((), (), s32[]{:S(2)}) async-start(), calls=%async_computation.20 | async-start | bytes 1474560 | tf_op jit(solution)/shard_map/all_gather | solution.py:175
  61.9 143.2 %all-gather.12.cloned.1.call-start = ((), (), s32[]{:S(2)}) async-start(), calls=%async_computation.16 | async-start | bytes 10485760 | tf_op jit(solution)/shard_map/all_gather | solution.py:87
  62.5 205.2 %all-gather.22.cloned.1.call-start = ((), (), s32[]{:S(2)}) async-start(), calls=%async_computation.21 | async-start | bytes 10485760 | tf_op jit(solution)/shard_map/all_gather | solution.py:95
  63.1 404.9 %all-gather.24.cloned.1.call-start = ((), (), s32[]{:S(2)}) async-start(), calls=%async_computation.22 | async-start | bytes 41943040 | tf_op jit(solution)/shard_map/all_gather | solution.py:97
  63.9 607.3 %all-gather.26.cloned.1.call-start = ((), (), s32[]{:S(2)}) async-start(), calls=%async_computation.23 | async-start | bytes 41943040 | tf_op jit(solution)/shard_map/all_gather | solution.py:98
  64.6 809.7 %all-gather.28.cloned.1.call-start = ((), (), s32[]{:S(2)}) async-start(), calls=%async_computation.24 | async-start | bytes 41943040 | tf_op jit(solution)/shard_map/all_gather | solution.py:103
  65.4 1088.9 %reduce-scatter.25.cloned.1.call-start = ((), (), s32[]{:S(2)}) async-start(), calls=%async_computation.25 | async-start | bytes 2949120 | tf_op jit(solution)/shard_map/reduce_scatter | solution.py:275
  1083.6 143.4 %reduce-scatter.49.cloned.1.call-start = ((), (), s32[]{:S(2)}) async-start(), calls=%async_computation.37 | async-start | bytes 2949120
  1087.5 212.8 %reduce-scatter.31.cloned.1.call-start = ((), (), s32[]{:S(2)}) async-start(), calls=%async_computation.28 | async-start | bytes 2621440 | tf_op jit(solution)/shard_map/reduce_scatter | solution.py:109
  1158.4 142.6 %reduce-scatter.35.cloned.1.call-start = ((), (), s32[]{:S(2)}) async-start(), calls=%async_computation.30 | async-start | bytes 2621440 | tf_op jit(solution)/shard_map/reduce_scatter | solution.py:109
  1230.4 138.9 %reduce-scatter.27.cloned.1.call-start = ((), (), s32[]{:S(2)}) async-start(), calls=%async_computation.26 | async-start | bytes 10485760 | tf_op jit(solution)/shard_map/reduce_scatter | solution.py:109
  1243.4 200.3 %reduce-scatter.39.cloned.1.call-start = ((), (), s32[]{:S(2)}) async-start(), calls=%async_computation.32 | async-start | bytes 10485760 | tf_op jit(solution)/shard_map/reduce_scatter | solution.py:109
  1250.6 430.4 %reduce-scatter.51.cloned.1.call-start = ((), (), s32[]{:S(2)}) async-start(), calls=%async_computation.38 | async-start | bytes 41943040
  1267.2 651.1 %reduce-scatter.53.cloned.1.call-start = ((), (), s32[]{:S(2)}) async-start(), calls=%async_computation.39 | async-start | bytes 41943040
  1283.4 872.2 %reduce-scatter.55.cloned.1.call-start = ((), (), s32[]{:S(2)}) async-start(), calls=%async_computation.40 | async-start | bytes 41943040
  1300.2 920.7 %reduce-scatter.33.cloned.1.call-start = ((), (), s32[]{:S(2)}) async-start(), calls=%async_computation.29 | async-start | bytes 589824 | tf_op jit(solution)/shard_map/reduce_scatter | solution.py:113
  1301.0 984.5 %reduce-scatter.37.cloned.1.call-start = ((), (), s32[]{:S(2)}) async-start(), calls=%async_computation.31 | async-start | bytes 589824 | tf_op jit(solution)/shard_map/reduce_scatter | solution.py:113
  1301.6 1054.2 %reduce-scatter.29.cloned.1.call-start = ((), (), s32[]{:S(2)}) async-start(), calls=%async_computation.27 | async-start | bytes 2359296 | tf_op jit(solution)/shard_map/reduce_scatter | solution.py:113
  1369.3 1056.9 %reduce-scatter.41.cloned.1.call-start = ((), (), s32[]{:S(2)}) async-start(), calls=%async_computation.33 | async-start | bytes 2359296 | tf_op jit(solution)/shard_map/reduce_scatter | solution.py:113
  1443.7 1134.3 %reduce-scatter.43.cloned.1.call-start = ((), (), s32[]{:S(2)}) async-start(), calls=%async_computation.34 | async-start | bytes 9437184 | tf_op jit(solution)/shard_map/reduce_scatter | solution.py:121
  1681.0 1048.9 %reduce-scatter.45.cloned.1.call-start = ((), (), s32[]{:S(2)}) async-start(), calls=%async_computation.35 | async-start | bytes 9437184 | tf_op jit(solution)/shard_map/reduce_scatter | solution.py:121
  1918.3 963.3 %reduce-scatter.47.cloned.1.call-start = ((), (), s32[]{:S(2)}) async-start(), calls=%async_computation.36 | async-start | bytes 9437184 | tf_op jit(solution)/shard_map/reduce_scatter | solution.py:121
  (42 other events, 2560.6 us)
Sparse Core Ops, SparseCore 0:
  9.6 25.2 all-gather.13
  61.9 41.7 all-gather.15
  106.3 40.4 all-gather.19
  148.2 56.9 all-gather.11
  206.6 58.2 all-gather.21
  266.5 201.5 all-gather.23
  469.6 201.5 all-gather.25
  672.7 201.5 all-gather.27
  1083.7 70.5 reduce-scatter.24
  1157.8 69.1 reduce-scatter.48
  1230.0 30.3 reduce-scatter.30
  1263.7 31.4 reduce-scatter.34
  1297.6 71.6 reduce-scatter.26
  1371.9 71.6 reduce-scatter.38
  1446.1 234.8 reduce-scatter.50
  1683.4 234.8 reduce-scatter.52
  1920.7 234.8 reduce-scatter.54
  2159.0 61.9 reduce-scatter.32
  2224.5 60.9 reduce-scatter.36
  2289.1 66.6 reduce-scatter.28
  2359.3 66.9 reduce-scatter.40
  2429.9 147.9 reduce-scatter.42
  2581.9 147.9 reduce-scatter.44
  2733.5 147.9 reduce-scatter.46
  (1 shorter events, 22.6 us)
where the time goes:
time: 2900 us; the launch traced here: 2890 us
  waiting for transfers between devices  2370 us (82%)
  matrix products  367 us (13%)
  other arithmetic  51.3 us (2%)
  local copies, waits for them, and re-layouts  42.5 us (1%)
  blocking collectives  39.1 us (1%)
    unnamed x29, waiting for transfers between devices  786 us
    reduce_scatter x3, waiting for transfers between devices, reduce_large(): lax.psum_scatter(within, 'ctx', scatter_dimension=0, tiled=True)  448 us
    reduce_scatter x4, waiting for transfers between devices, reduce_small(): lax.psum_scatter(as_sent(within), 'ctx', scatter_dimension=0, tiled=True)  207 us
    all_gather x1, waiting for transfers between devices, fetch_middle(): lax.all_gather(gate_weight, 'fsdp', axis=0, tiled=True)  194 us
    all_gather x1, waiting for transfers between devices, fetch_middle(): lax.all_gather(up_weight, 'fsdp', axis=0, tiled=True)  184 us
    all_gather x1, waiting for transfers between devices, fetch_down(): return lax.all_gather(down_weight, 'fsdp', axis=0, tiled=True)  183 us
    reduce_scatter x4, waiting for transfers between devices, reduce_small(): lax.psum_scatter(as_sent(terms), 'fsdp', scatter_dimension=0, tiled=True)  142 us
    dot_general x7, matrix products, matmul_nt(): lax.dot_general(left_in, right_in, (((1,), (1,)), ((), ())), preferred_el...  73.6 us
  transfers between devices with their start and end apart: 25, of which 22 were waited for; matrix products, arithmetic and copies ran while one was open for 8% of the time, Pallas kernels for 0%

commit v1 on v0

v1 whole, which is shorter than its diff:
```python
import math

import jax
import jax.numpy as jnp
from jax import lax
from jax.sharding import PartitionSpec as P

QUERY_HEADS = 32
KEY_VALUE_HEADS = 8
HEAD_SIZE = 64

NORM_EPS = 1e-05
ROPE_BASE = 500000.0
MASKED_SCORE = -1e30
BF = jnp.bfloat16
F32 = jnp.float32


def rope_tables(position):
    freqs = ROPE_BASE ** (-(jnp.arange(HEAD_SIZE // 2, dtype=F32) * 2.0 / HEAD_SIZE))
    angle = position.astype(F32)[:, None] * freqs[None, :]
    return (jnp.cos(angle)[:, None, :], jnp.sin(angle)[:, None, :])


def apply_rotary(rotated_in, cosine_table, sine_values):
    half_size = rotated_in.shape[-1] // 2
    first_half = rotated_in[..., :half_size]
    second_half = rotated_in[..., half_size:]
    return jnp.concatenate(
        [
            first_half * cosine_table - second_half * sine_values,
            second_half * cosine_table + first_half * sine_values,
        ],
        axis=-1,
    )


def packed_rows(order_part, block_rows):
    offsets = jnp.arange(block_rows, dtype=jnp.int32)
    return (order_part[:, None] * block_rows + offsets[None, :]).reshape(-1)


def sequence_place(packed, seq_lengths):
    seq_ends = jnp.cumsum(seq_lengths)
    seq_starts = seq_ends - seq_lengths
    seq_ids = jnp.sum((packed[:, None] >= seq_ends[None, :]).astype(jnp.int32), axis=1)
    onehot_seq = (
        seq_ids[:, None] == jnp.arange(seq_lengths.shape[0], dtype=jnp.int32)[None, :]
    ).astype(jnp.int32)
    return (seq_ids, packed - jnp.sum(onehot_seq * seq_starts[None, :], axis=1))


def rms_scale(value_rows):
    return lax.rsqrt(jnp.mean(value_rows * value_rows, axis=-1, keepdims=True) + NORM_EPS)


def norm_back(grad_normed, normed, inverse):
    return inverse * (grad_normed - normed * jnp.mean(grad_normed * normed, axis=-1, keepdims=True))


def mm(left_in, right_in):
    return jnp.dot(left_in, right_in, preferred_element_type=F32)


def mm_nt(left_in, right_in):
    return lax.dot_general(left_in, right_in, (((1,), (1,)), ((), ())), preferred_element_type=F32)


def mm_tn(left_in, right_in):
    return lax.dot_general(left_in, right_in, (((0,), (0,)), ((), ())), preferred_element_type=F32)


def swap_fsdp(value, d):
    return lax.ppermute(value, "fsdp", [(i, i ^ d) for i in range(4)])


def gather_fsdp(shard):
    across = swap_fsdp(shard, 2)
    return [shard, swap_fsdp(shard, 1), across, swap_fsdp(across, 1)]


def xor_blocks(value, f, axis):
    size = value.shape[axis] // 4
    return jnp.concatenate(
        [lax.dynamic_slice_in_dim(value, (f ^ d) * size, size, axis) for d in range(4)], axis=axis
    )


def swap_cols(value, d, parts):
    width = value.shape[1] // (4 * parts)
    return jnp.concatenate(
        [
            value[:, (p * 4 + (e ^ d)) * width : (p * 4 + (e ^ d) + 1) * width]
            for p in range(parts)
            for e in range(4)
        ],
        axis=1,
    )


def scatter_fsdp(term, fix):
    size = term.shape[0] // 4
    blocks = [term[d * size : (d + 1) * size] for d in range(4)]
    got = swap_fsdp(jnp.concatenate([blocks[1], blocks[3]], axis=0).astype(BF), 1)
    own = blocks[0] + fix(got[:size], 1).astype(F32)
    other = blocks[2] + fix(got[size:], 1).astype(F32)
    return own + fix(swap_fsdp(other.astype(BF), 2), 2).astype(F32)


def ring_index(place, n):
    place = place % n
    return jnp.where(place < n // 2, 2 * place, 2 * (n - 1 - place) + 1)


def ring_shift(value, step, n):
    order = list(range(0, n, 2)) + list(range(n - 1, 0, -2))
    return lax.ppermute(value, "ctx", [(order[i], order[(i + step) % n]) for i in range(n)])


def ring_gather(own, n):
    half, width = n // 2, own.shape[1] // 2
    chunks = {0: own}
    right = left = own
    for step in range(1, half):
        right = ring_shift(right, 1, n)
        left = ring_shift(left, -1, n)
        chunks[-step], chunks[step] = right, left
    chunks[half] = jnp.concatenate(
        [ring_shift(right[:, :width], 1, n), ring_shift(left[:, width:], -1, n)], axis=1
    )
    return chunks


def ring_scatter(contrib, n):
    half = n // 2
    far = contrib(half)
    width = far.shape[1] // 2
    from_left = ring_shift(far[:, :width].astype(BF), 1, n)
    from_right = ring_shift(far[:, width:].astype(BF), -1, n)
    pad = ((0, 0), (0, width))
    from_left = jnp.pad(from_left, pad)
    from_right = jnp.pad(from_right, pad[:1] + (pad[1][::-1],))
    for step in range(half - 1, 0, -1):
        from_left = ring_shift((contrib(step) + from_left.astype(F32)).astype(BF), 1, n)
        from_right = ring_shift((contrib(-step) + from_right.astype(F32)).astype(BF), -1, n)
    return contrib(0) + from_left.astype(F32) + from_right.astype(F32)


def reduce_gain(term):
    within = lax.psum_scatter(term.astype(BF), "fsdp", scatter_dimension=0, tiled=True)
    return lax.psum_scatter(within, "ctx", scatter_dimension=0, tiled=True).astype(F32)


def body(
    n,
    tokens,
    first_gain,
    query_weight,
    key_matrix,
    value_matrix,
    out_weight,
    second_gain,
    gate_weight,
    up_weight,
    down_weight,
    lengths,
    block_order,
    cotangent,
):
    token_rows, model = tokens.shape
    block_rows = token_rows // 2
    kv_width = key_matrix.shape[1]
    heads_per_group = QUERY_HEADS // KEY_VALUE_HEADS
    score_scale = 1.0 / math.sqrt(HEAD_SIZE)
    c = lax.axis_index("ctx")
    f = lax.axis_index("fsdp")
    place = jnp.where(c % 2 == 0, c // 2, n - 1 - c // 2)
    rel = list(range(-(n // 2 - 1), n // 2 + 1))
    owners = ring_index(place + jnp.asarray(rel, jnp.int32), n)

    own_blocks = lax.dynamic_slice_in_dim(block_order, 2 * c, 2)
    key_blocks = jnp.take(block_order.reshape(n, 2), owners, axis=0).reshape(-1)
    packed_query = packed_rows(own_blocks, block_rows)
    packed_key = packed_rows(key_blocks, block_rows)
    seq_query, position = sequence_place(packed_query, lengths[0])
    seq_key = sequence_place(packed_key, lengths[0])[0]
    allowed = (seq_query[:, None] == seq_key[None, :]) & (
        packed_key[None, :] <= packed_query[:, None]
    )
    cosine_table, sine_values = rope_tables(position)

    kv_rows = gather_fsdp(jnp.concatenate([key_matrix, value_matrix], axis=1))
    query_rows_w = gather_fsdp(query_weight)
    gains = jnp.stack([first_gain, second_gain])
    gains_x = jnp.concatenate(gather_fsdp(gains), axis=1).astype(F32)
    gain_one, gain_two = gains_x[0], gains_x[1]
    weight_kv = jnp.concatenate(kv_rows, axis=0)
    weight_q = jnp.concatenate(query_rows_w, axis=0)
    weight_o = jnp.concatenate(gather_fsdp(out_weight), axis=0)

    units = gate_weight.shape[1] // (4 * n)
    span = gate_weight.shape[1] // 4

    def own_units(weight):
        return [
            lax.dynamic_slice_in_dim(weight, (f ^ e) * span + c * units, units, 1)
            for e in range(4)
        ]

    gate_up_own = jnp.concatenate(own_units(gate_weight) + own_units(up_weight), axis=1)
    gate_up = jnp.concatenate(
        [swap_cols(part, d, 2) for d, part in enumerate(gather_fsdp(gate_up_own))], axis=0
    )
    down = jnp.concatenate(
        gather_fsdp(lax.dynamic_slice_in_dim(down_weight, c * units, units, 0)), axis=0
    )
    grad_out_all = ring_gather(cotangent, n)

    inputs_f = tokens.astype(F32)
    inverse_one = rms_scale(inputs_f)
    normed_one = xor_blocks(inputs_f * inverse_one, f, 1)
    first_hidden = (normed_one * gain_one).astype(BF)
    kv_pre = mm(first_hidden, weight_kv)
    key_before_rotary = kv_pre[:, :kv_width].reshape(token_rows, KEY_VALUE_HEADS, HEAD_SIZE)
    key_row_matrix = (
        apply_rotary(key_before_rotary, cosine_table, sine_values)
        .astype(BF)
        .reshape(token_rows, kv_width)
    )
    value_rows = kv_pre[:, kv_width:].astype(BF)
    kv_all = ring_gather(jnp.concatenate([key_row_matrix, value_rows], axis=1), n)
    kv_all = jnp.concatenate([kv_all[r] for r in rel], axis=0)
    query_pre = mm(first_hidden, weight_q).reshape(token_rows, QUERY_HEADS, HEAD_SIZE)
    query_rows = apply_rotary(query_pre, cosine_table, sine_values).astype(BF)
    key_total_count = kv_all.shape[0]
    query_head_rows = query_rows.reshape(
        token_rows, KEY_VALUE_HEADS, heads_per_group, HEAD_SIZE
    ).transpose(1, 0, 2, 3)
    key_head_rows = (
        kv_all[:, :kv_width]
        .reshape(key_total_count, KEY_VALUE_HEADS, HEAD_SIZE)
        .transpose(1, 0, 2)
    )
    value_head_rows = (
        kv_all[:, kv_width:]
        .reshape(key_total_count, KEY_VALUE_HEADS, HEAD_SIZE)
        .transpose(1, 0, 2)
    )

    def head_forward(head_args):
        head_query, head_key, head_value = head_args
        raw_scores = jnp.einsum("qrd,td->qrt", head_query, head_key, preferred_element_type=F32)
        scores = jnp.where(allowed[:, None, :], raw_scores * score_scale, MASKED_SCORE)
        row_peak = jnp.max(scores, axis=-1, keepdims=True)
        expd_rows = jnp.exp(scores - row_peak)
        row_total = jnp.sum(expd_rows, axis=-1, keepdims=True)
        weights = (expd_rows / row_total).astype(BF)
        mixed_rows = jnp.einsum("qrt,td->qrd", weights, head_value, preferred_element_type=F32)
        return (mixed_rows, (row_peak + jnp.log(row_total))[..., 0])

    head_out, head_lse = lax.map(head_forward, (query_head_rows, key_head_rows, value_head_rows))
    attended = (
        head_out.transpose(1, 0, 2, 3).reshape(token_rows, QUERY_HEADS * HEAD_SIZE).astype(BF)
    )
    attended = xor_blocks(attended, f, 1)
    residual = inputs_f + mm(attended, weight_o)
    inverse_two = rms_scale(residual)
    normed_two = xor_blocks(residual * inverse_two, f, 1)
    hidden_two = (normed_two * gain_two).astype(BF)

    hidden_all = ring_gather(hidden_two, n)
    width = 4 * units
    activated, grad_gate_up = {}, {}
    for r in sorted(rel, key=abs):
        gate_up_proj = mm(hidden_all[r], gate_up)
        gate_proj, up_proj = gate_up_proj[:, :width], gate_up_proj[:, width:]
        gate_sig = jax.nn.sigmoid(gate_proj)
        activated[r] = (gate_proj * gate_sig * up_proj).astype(BF)
        grad_act = mm_nt(grad_out_all[r], down)
        grad_gate = grad_act * up_proj * gate_sig * (1.0 + gate_proj * (1.0 - gate_sig))
        grad_up = grad_act * gate_proj * gate_sig
        grad_gate_up[r] = jnp.concatenate([grad_gate, grad_up], axis=1).astype(BF)
    grad_hidden_two = ring_scatter(lambda r: mm_nt(grad_gate_up[r], gate_up), n)
    layer_out = (residual + ring_scatter(lambda r: mm(activated[r], down), n)).astype(BF)

    activated_rows = jnp.concatenate([activated[r] for r in rel], axis=0)
    grad_out_rows = jnp.concatenate([grad_out_all[r] for r in rel], axis=0)
    hidden_rows = jnp.concatenate([hidden_all[r] for r in rel], axis=0)
    grad_gate_up_rows = jnp.concatenate([grad_gate_up[r] for r in rel], axis=0)
    down_grad = scatter_fsdp(mm_tn(activated_rows, grad_out_rows), lambda value, d: value)
    down_grad = down_grad.astype(BF).astype(F32)
    gate_up_grad = scatter_fsdp(
        mm_tn(hidden_rows, grad_gate_up_rows), lambda value, d: swap_cols(value, d, 2)
    ).astype(BF)
    own_rows = gate_up_grad.shape[0] // n
    gate_up_grad = lax.all_to_all(
        gate_up_grad.reshape(n, own_rows, 2 * width), "ctx", 0, 0, tiled=False
    )
    gate_up_grad = gate_up_grad.reshape(n, own_rows, 2, 4, units).transpose(2, 1, 3, 0, 4)
    gate_up_grad = xor_blocks(gate_up_grad, f, 2).reshape(2, own_rows, 4 * n * units).astype(F32)
    gate_grad, up_grad = gate_up_grad[0], gate_up_grad[1]

    grad_normed_two = grad_hidden_two * gain_two
    gain_two_term = jnp.sum(grad_hidden_two * normed_two, axis=0)
    grad_residual = cotangent.astype(F32) + xor_blocks(
        norm_back(grad_normed_two, normed_two, inverse_two), f, 1
    )
    grad_branch = grad_residual.astype(BF)

    def reduce_rows(term):
        within = scatter_fsdp(term, lambda value, d: value)
        rows = within.shape[0] // n

        def contrib(r):
            start = ring_index(place + r, n) * rows
            return lax.dynamic_slice_in_dim(within, start, rows, 0)

        return ring_scatter(contrib, n)

    out_grad = reduce_rows(mm_tn(attended, grad_branch))
    second_gain_grad = reduce_gain(xor_blocks(gain_two_term, f, 0))
    attended_gradient = xor_blocks(mm_nt(grad_branch, weight_o), f, 1).astype(BF)
    head_gradients = attended_gradient.reshape(
        token_rows, KEY_VALUE_HEADS, heads_per_group, HEAD_SIZE
    ).transpose(1, 0, 2, 3)

    def head_backward(head_args):
        head_query, head_key, head_value, head_grad, head_logsum = head_args
        raw_scores = jnp.einsum("qrd,td->qrt", head_query, head_key, preferred_element_type=F32)
        scores = jnp.where(allowed[:, None, :], raw_scores * score_scale, MASKED_SCORE)
        prob_rows = jnp.exp(scores - head_logsum[..., None])
        grad_probs = jnp.einsum("qrd,td->qrt", head_grad, head_value, preferred_element_type=F32)
        row_dot = jnp.sum(prob_rows * grad_probs, axis=-1, keepdims=True)
        grad_scores = (prob_rows * (grad_probs - row_dot) * score_scale).astype(BF)
        grad_query_head = jnp.einsum(
            "qrt,td->qrd", grad_scores, head_key, preferred_element_type=F32
        )
        grad_key_head = jnp.einsum(
            "qrt,qrd->td", grad_scores, head_query, preferred_element_type=F32
        )
        grad_value_head = jnp.einsum(
            "qrt,qrd->td", prob_rows.astype(BF), head_grad, preferred_element_type=F32
        )
        return (grad_query_head, grad_key_head, grad_value_head)

    grad_q_heads, grad_k_heads, grad_v_heads = lax.map(
        head_backward, (query_head_rows, key_head_rows, value_head_rows, head_gradients, head_lse)
    )
    grad_key_part = grad_k_heads.transpose(1, 0, 2).reshape(key_total_count, kv_width)
    grad_value_part = grad_v_heads.transpose(1, 0, 2).reshape(key_total_count, kv_width)
    grad_kv_part = jnp.concatenate([grad_key_part, grad_value_part], axis=1)
    grad_query_rows = grad_q_heads.transpose(1, 0, 2, 3).reshape(token_rows, QUERY_HEADS, HEAD_SIZE)
    grad_query = (
        apply_rotary(grad_query_rows, cosine_table, -sine_values)
        .astype(BF)
        .reshape(token_rows, QUERY_HEADS * HEAD_SIZE)
    )
    query_grad = reduce_rows(mm_tn(first_hidden, grad_query))

    def kv_contrib(r):
        start = rel.index(r) * token_rows
        return grad_kv_part[start : start + token_rows]

    grad_kv = ring_scatter(kv_contrib, n)
    grad_key = (
        apply_rotary(
            grad_kv[:, :kv_width].reshape(token_rows, KEY_VALUE_HEADS, HEAD_SIZE),
            cosine_table,
            -sine_values,
        )
        .astype(BF)
        .reshape(token_rows, kv_width)
    )
    grad_kv_pre = jnp.concatenate([grad_key, grad_kv[:, kv_width:].astype(BF)], axis=1)
    kv_grad = reduce_rows(mm_tn(first_hidden, grad_kv_pre))
    grad_hidden_one = mm_nt(grad_query, weight_q) + mm_nt(grad_kv_pre, weight_kv)
    gain_one_term = jnp.sum(grad_hidden_one * normed_one, axis=0)
    first_gain_grad = reduce_gain(xor_blocks(gain_one_term, f, 0))
    tokens_grad = grad_residual + xor_blocks(
        norm_back(grad_hidden_one * gain_one, normed_one, inverse_one), f, 1
    )
    return (
        layer_out,
        tokens_grad,
        first_gain_grad,
        query_grad,
        kv_grad[:, :kv_width],
        kv_grad[:, kv_width:],
        out_grad,
        second_gain_grad,
        gate_grad,
        up_grad,
        down_grad,
    )


def solution(mesh):
    rows, vector = P(("fsdp", "ctx"), None), P(("fsdp", "ctx"))
    weight = P("fsdp", None)

    def layer(*arrays):
        return body(mesh.shape["ctx"], *arrays)

    return jax.shard_map(
        layer,
        mesh=mesh,
        in_specs=(
            rows, P("fsdp"), weight, weight, weight, weight, P("fsdp"), weight, weight, weight,
            weight, P(), rows,
        ),
        out_specs=(rows, rows, vector, rows, rows, rows, rows, vector, rows, rows, rows),
        check_vma=False,
    )
```

time: 2900 us -> 1140 us (0.39)
  waiting for transfers between devices: 2370 us -> 401 us
  local copies, waits for them, and re-layouts: 42.5 us -> 161 us
  starting transfers between devices: 0.99 us -> 90.8 us
  other arithmetic: 51.3 us -> 131 us
  matrix products: 367 us -> 306 us
    reduce_scatter x12 -> x0, waiting for transfers between devices: 864 us -> none  [the longest x3 448 us: reduce_large(): lax.psum_scatter(within, 'ctx', scatter_dimension=0, tiled=True)]
    unnamed x29 -> x0, waiting for transfers between devices: 786 us -> none
    all_gather x9 -> x0, waiting for transfers between devices: 723 us -> none  [the longest x1 194 us: fetch_middle(): lax.all_gather(gate_weight, 'fsdp', axis=0, tiled=True)]
    ppermute x0 -> x100, waiting for transfers between devices: none -> 401 us  [the longest x28 247 us: swap_fsdp(): return lax.ppermute(value, 'fsdp', [(i, i ^ d) for i in range(4)])]
    ppermute x0 -> x100, starting transfers between devices: none -> 86.4 us  [the longest x72 72.9 us: ring_shift(): lax.ppermute(value, 'ctx', [(order[i], order[(i + step) % n]) for i in ra...]
    unnamed x90 -> x359, local copies, waits for them, and re-layouts: 14 us -> 83.1 us
    dot_general x69 -> x91, matrix products: 331 us -> 270 us  [the longest x19 55.2 us: mm_nt(): lax.dot_general(left_in, right_in, (((1,), (1,)), ((), ())), preferred_el...]
    concatenate x0 -> x13, other arithmetic: none -> 52.2 us  [the longest x1 35.4 us: body(): jnp.concatenate([swap_cols(part, d, 2) for d, part in enumerate(gather_fs...]
  transfers between devices with their start and end apart: 25 -> 101, of which waited for: 22 -> 37; matrix products, arithmetic and copies ran while one was open for 8% -> 52% of each run, Pallas kernels for 0% -> 0%
where the time goes in v1:
time: 1140 us; the launch traced here: 1120 us
  waiting for transfers between devices  401 us (35%)
  matrix products  306 us (27%)
  local copies, waits for them, and re-layouts  161 us (14%)
  other arithmetic  131 us (11%)
  starting transfers between devices  90.8 us (8%)
  blocking collectives  28 us (2%)
    ppermute x28, waiting for transfers between devices, swap_fsdp(): return lax.ppermute(value, 'fsdp', [(i, i ^ d) for i in range(4)])  247 us
    ppermute x72, waiting for transfers between devices, ring_shift(): lax.ppermute(value, 'ctx', [(order[i], order[(i + step) % n]) for i in ra...  154 us
    unnamed x359, local copies, waits for them, and re-layouts  83.1 us
    ppermute x72, starting transfers between devices, ring_shift(): lax.ppermute(value, 'ctx', [(order[i], order[(i + step) % n]) for i in ra...  72.9 us
    dot_general x19, matrix products, mm_nt(): lax.dot_general(left_in, right_in, (((1,), (1,)), ((), ())), preferred_el...  55.2 us
    dot_general x5, matrix products, mm_tn(): lax.dot_general(left_in, right_in, (((0,), (0,)), ((), ())), preferred_el...  53.2 us
    dot_general x19, matrix products, mm(): return jnp.dot(left_in, right_in, preferred_element_type=F32)  38.5 us
    dot_general x8, matrix products, head_backward(): jnp.einsum('qrt,td->qrd', grad_scores, head_key, preferred_element_type=F32)  36.5 us
  transfers between devices with their start and end apart: 101, of which 37 were waited for; matrix products, arithmetic and copies ran while one was open for 52% of the time, Pallas kernels for 0%

profile of v1, /device:TPU:0, one launch (start us, length us, event | category | flops | bytes accessed | tf_op | source)
XLA Modules:
  0.0 1123.3 jit_solution(11877490407273136201)
XLA Ops:
  40.5 7.6 collective-permute-done.46
  49.9 15.2 %collective-permute-done.7 = bf16[512,1024]{1,0:T(8,128)(2,1)S(1)} collective-permute-done((bf16[512,1024]{1,0:T(8,128)(2,1)}, bf16[512,1024]{1,0:T(8,128)(2,1)S(1)}, u32[]{:S(2)}, u32[]{:S(2)}) %collective-permute-start.7) | collective-permute-done | bytes 1048608 | tf_op jit(solution)/shard_map/ppermute | solution.py:74
  74.9 7.5 collective-permute-done.44
  100.9 97.8 %collective-permute-done.24 = bf16[256,2048]{1,0:T(8,128)(2,1)} collective-permute-done((bf16[256,2048]{1,0:T(8,128)(2,1)S(1)}, bf16[256,2048]{1,0:T(8,128)(2,1)}, u32[]{:S(2)}, u32[]{:S(2)}) %collective-permute-start.24) | collective-permute-done | bytes 1048608 | tf_op jit(solution)/shard_map/ppermute | solution.py:74
  213.7 7.5 pad_maximum_fusion.2
  221.9 19.9 %collective-permute-done.21 = bf16[512,2048]{1,0:T(8,128)(2,1)} collective-permute-done((bf16[512,2048]{1,0:T(8,128)(2,1)}, bf16[512,2048]{1,0:T(8,128)(2,1)}, u32[]{:S(2)}, u32[]{:S(2)}) %collective-permute-start.21) | collective-permute-done | bytes 2097184 | tf_op jit(solution)/shard_map/ppermute | solution.py:74
  296.8 41.1 %while.30 = (s32[]{:T(128)}, bf16[8,160,4,64]{1,3,2,0:T(8,128)(2,1)S(1)}, f32[8,160,4]{1,2,0:T(4,128)}, bf16[8,160,4,64]{1,3,2,0:T(8,128)(2,1)S(1)}, bf16[8,1280...) while((s32[]{:T(128)}, ...), condition=%wide.region_8.9_spmd.clone.clone, body=%wide.region_5.8_spmd.clone.sunk.clone | while | flops 216882560 | bytes 10999665 | solution.py:261
  359.5 35.4 %pad_maximum_fusion = bf16[2048,2048]{1,0:T(8,128)(2,1)S(1)} fusion(bf16[512,2048]{1,0:T(8,128)(2,1)S(1)} %slice_dynamic-update-slice_fusion.16, bf16[512,512]{1,0:T(8,128)(2,1)S(1)} %copy-done.50, bf16[512,512]{1,0:T(8,128)(2,1)S(1)} %copy-done.51, bf16[512,512]{1,0:T(8,128)(2,1)S(1)} %copy-done.52, bf16[512,512]{1,0:T(8,128)(2,1)S(1)} %copy-done.49, ...), kind=kLoop, calls=%fused_computation.80 | loop fusion | flops 58720256 | bytes 16777216 | tf_op jit(solution)/shard_map/concatenate | solution.py:211
  464.3 19.3 %fusion.181 = (bf16[2048,2048]{1,0:T(8,128)(2,1)}, f32[2048,2048]{1,0:T(8,128)}) fusion(bf16[1280,2048]{1,0:T(8,128)(2,1)} %constant_dynamic-update-slice_fusion.41, bf16[1280,2048]{1,0:T(8,128)(2,1)} %fusion.129), kind=kOutput, calls=%fused_computation.493 | convolution fusion | flops 10741612544 | bytes 35651584 | tf_op jit(solution)/shard_map/dot_general | solution.py:70
  489.0 10.3 fusion.182
  525.0 9.0 collective-permute-done.55
  551.5 10.2 collective-permute-done.56
  576.9 15.4 %collective-permute-done.57 = bf16[160,2048]{1,0:T(8,128)(2,1)S(1)} collective-permute-done((bf16[160,2048]{1,0:T(8,128)(2,1)S(1)}, bf16[160,2048]{1,0:T(8,128)(2,1)S(1)}, u32[]{:S(2)}, u32[]{:S(2)}) %collective-permute-start.57) | collective-permute-done | bytes 655392 | tf_op jit(solution)/shard_map/ppermute | solution.py:117
  603.2 10.8 fusion.180
  615.8 138.1 %while.31 = (s32[]{:T(128)}, f32[8,160,4,64]{1,3,2,0:T(8,128)}, f32[8,1280,64]{1,2,0:T(8,128)}, f32[8,1280,64]{1,2,0:T(8,128)}, bf16[8,160,4,64]{1,3,2,0:T(8,128...) while((s32[]{:T(128)}, f32[8,160,4,64]{1,3,2,0:T(8,128)}, ...), condition=%wide.region_13.14_spmd.clone.clone, body=%wide.region_11.13_spmd.clone.sunk.clone | while | flops 536375040 | bytes 38412168 | solution.py:346
  766.0 8.2 fusion.178
  783.8 7.3 collective-permute-done.59
  796.9 9.0 collective-permute-done.63
  809.2 10.6 collective-permute-done.64
  855.5 21.9 %all-reduce.16 = (bf16[512]{0:T(512)(128)(2,1)S(1)}, bf16[512]{0:T(512)(128)(2,1)S(1)}) all-reduce(bf16[512]{0:T(512)(128)(2,1)S(1)} %dynamic-slice.17, bf16[512]{0:T(512)(128)(2,1)S(1)} %dynamic-slice.21), channel_id=3, replica_groups=mesh['fsdp'=4,'ctx'=8] {'ctx'}, use_global_device_ids=true, to_apply=%region_17.18.clone | all-reduce | flops 1024 | bytes 4096
  892.6 15.1 %collective-permute-done.77 = bf16[512,1024]{1,0:T(8,128)(2,1)S(1)} collective-permute-done((bf16[512,1024]{1,0:T(8,128)(2,1)S(1)}, bf16[512,1024]{1,0:T(8,128)(2,1)S(1)}, u32[]{:S(2)}, u32[]{:S(2)}) %collective-permute-start.77) | collective-permute-done | bytes 1048608 | tf_op jit(solution)/shard_map/ppermute | solution.py:74
  935.1 31.0 %collective-permute-done.97 = bf16[512,2048]{1,0:T(8,128)(2,1)S(1)} collective-permute-done((bf16[512,2048]{1,0:T(8,128)(2,1)S(1)}, bf16[512,2048]{1,0:T(8,128)(2,1)S(1)}, u32[]{:S(2)}, u32[]{:S(2)}) %collective-permute-start.97) | collective-permute-done | bytes 2097184 | tf_op jit(solution)/shard_map/ppermute | solution.py:74
  976.5 34.6 %collective-permute-done.67 = bf16[512,2048]{1,0:T(8,128)(2,1)} collective-permute-done((bf16[512,2048]{1,0:T(8,128)(2,1)}, bf16[512,2048]{1,0:T(8,128)(2,1)}, u32[]{:S(2)}, u32[]{:S(2)}) %collective-permute-start.67) | collective-permute-done | bytes 2097184 | tf_op jit(solution)/shard_map/ppermute | solution.py:74
  1015.5 33.2 %collective-permute-done.87 = bf16[512,2048]{1,0:T(8,128)(2,1)} collective-permute-done((bf16[512,2048]{1,0:T(8,128)(2,1)}, bf16[512,2048]{1,0:T(8,128)(2,1)}, u32[]{:S(2)}, u32[]{:S(2)}) %collective-permute-start.87) | collective-permute-done | bytes 2097184 | tf_op jit(solution)/shard_map/ppermute | solution.py:74
  (862 shorter events, 680.9 us)
Async XLA Ops:
  7.1 87.6 %collective-permute-start.17 = (bf16[512,2048]{1,0:T(8,128)(2,1)}, bf16[512,2048]{1,0:T(8,128)(2,1)}, u32[]{:S(2)}, u32[]{:S(2)}) collective-permute-start(bf16[512,2048]{1,0:T(8,128)(2,1)} %param.23), channel_id=1, source_target_pairs={{0,8},{8,0},{16,24},{24,16},{1,9},{9,1},{17,25},{25,17},{2,10},{10... | collective-permute-start | bytes 6291464 | tf_op jit(solution)/shard_map/ppermute | solution.py:74
  82.4 116.3 %collective-permute-start.18 = (bf16[512,2048]{1,0:T(8,128)(2,1)}, bf16[512,2048]{1,0:T(8,128)(2,1)}, u32[]{:S(2)}, u32[]{:S(2)}) collective-permute-start(bf16[512,2048]{1,0:T(8,128)(2,1)} %param.23), channel_id=1, source_target_pairs={{0,16},{8,24},{16,0},{24,8},{1,17},{9,25},{17,1},{25,9},{2,18},{10... | collective-permute-start | bytes 6291464 | tf_op jit(solution)/shard_map/ppermute | solution.py:74
  85.3 117.9 %collective-permute-start.3 = (bf16[512,2048]{1,0:T(8,128)(2,1)}, bf16[512,2048]{1,0:T(8,128)(2,1)}, u32[]{:S(2)}, u32[]{:S(2)}) collective-permute-start(bf16[512,2048]{1,0:T(8,128)(2,1)} %param.20), channel_id=1, source_target_pairs={{0,8},{8,0},{16,24},{24,16},{1,9},{9,1},{17,25},{25,17},{2,10},{10... | collective-permute-start | bytes 6291464 | tf_op jit(solution)/shard_map/ppermute | solution.py:74
  85.3 121.6 %collective-permute-start.4 = (bf16[512,2048]{1,0:T(8,128)(2,1)}, bf16[512,2048]{1,0:T(8,128)(2,1)}, u32[]{:S(2)}, u32[]{:S(2)}) collective-permute-start(bf16[512,2048]{1,0:T(8,128)(2,1)} %param.20), channel_id=1, source_target_pairs={{0,16},{8,24},{16,0},{24,8},{1,17},{9,25},{17,1},{25,9},{2,18},{10... | collective-permute-start | bytes 6291464 | tf_op jit(solution)/shard_map/ppermute | solution.py:74
  88.6 110.1 %collective-permute-start.24 = (bf16[256,2048]{1,0:T(8,128)(2,1)S(1)}, bf16[256,2048]{1,0:T(8,128)(2,1)}, u32[]{:S(2)}, u32[]{:S(2)}) collective-permute-start(bf16[256,2048]{1,0:T(8,128)(2,1)S(1)} %constant_dynamic-slice_fusion.12), channel_id=1, source_target_pairs={{0,16},{8,24},{16,0},{24,8},{1,17},{9,25},{17,1},{25,9},{2,18},{10... | collective-permute-start | bytes 3145736 | tf_op jit(solution)/shard_map/ppermute | solution.py:74
  94.8 147.1 %collective-permute-start.21 = (bf16[512,2048]{1,0:T(8,128)(2,1)}, bf16[512,2048]{1,0:T(8,128)(2,1)}, u32[]{:S(2)}, u32[]{:S(2)}) collective-permute-start(bf16[512,2048]{1,0:T(8,128)(2,1)} %dynamic-slice_dynamic-update-slice_fusion), channel_id=1, source_target_pairs={{0,16},{8,24},{16,0},{24,8},{1,17},{9,25},{17,1},{25,9},{2,18},{10... | collective-permute-start | bytes 6291464 | tf_op jit(solution)/shard_map/ppermute | solution.py:74
  203.2 55.2 %collective-permute-start.49 = (bf16[160,1024]{1,0:T(8,128)(2,1)S(1)}, bf16[160,1024]{1,0:T(8,128)(2,1)S(1)}, u32[]{:S(2)}, u32[]{:S(2)}) collective-permute-start(bf16[160,1024]{1,0:T(8,128)(2,1)S(1)} %copy-done.119), channel_id=1, source_target_pairs={{0,1},{2,0},{4,2},{6,4},{7,6},{5,7},{3,5},{1,3},{8,9},{10,8},{12,1... | collective-permute-start | bytes 983048 | tf_op jit(solution)/shard_map/ppermute | solution.py:117
  206.9 50.7 %collective-permute-start.48 = (bf16[160,1024]{1,0:T(8,128)(2,1)S(1)}, bf16[160,1024]{1,0:T(8,128)(2,1)S(1)}, u32[]{:S(2)}, u32[]{:S(2)}) collective-permute-start(bf16[160,1024]{1,0:T(8,128)(2,1)S(1)} %copy-done.120), channel_id=1, source_target_pairs={{0,2},{2,4},{4,6},{6,7},{7,5},{5,3},{3,1},{1,0},{8,10},{10,12},{12... | collective-permute-start | bytes 983048 | tf_op jit(solution)/shard_map/ppermute | solution.py:117
  257.6 80.2 %collective-permute-start.19 = (bf16[512,2048]{1,0:T(8,128)(2,1)}, bf16[512,2048]{1,0:T(8,128)(2,1)}, u32[]{:S(2)}, u32[]{:S(2)}) collective-permute-start(bf16[512,2048]{1,0:T(8,128)(2,1)} %collective-permute-done.18), channel_id=1, source_target_pairs={{0,8},{8,0},{16,24},{24,16},{1,9},{9,1},{17,25},{25,17},{2,10},{10... | collective-permute-start | bytes 6291464 | tf_op jit(solution)/shard_map/ppermute | solution.py:74
  258.5 93.1 %collective-permute-start.22 = (bf16[512,2048]{1,0:T(8,128)(2,1)}, bf16[512,2048]{1,0:T(8,128)(2,1)}, u32[]{:S(2)}, u32[]{:S(2)}) collective-permute-start(bf16[512,2048]{1,0:T(8,128)(2,1)} %collective-permute-done.21), channel_id=1, source_target_pairs={{0,8},{8,0},{16,24},{24,16},{1,9},{9,1},{17,25},{25,17},{2,10},{10... | collective-permute-start | bytes 6291464 | tf_op jit(solution)/shard_map/ppermute | solution.py:74
  349.0 49.9 %collective-permute-start.29 = (bf16[160,2048]{1,0:T(8,128)(2,1)S(1)}, bf16[160,2048]{1,0:T(8,128)(2,1)S(1)}, u32[]{:S(2)}, u32[]{:S(2)}) collective-permute-start(bf16[160,2048]{1,0:T(8,128)(2,1)S(1)} %multiply_convert_fusion), channel_id=1, source_target_pairs={{0,2},{2,4},{4,6},{6,7},{7,5},{5,3},{3,1},{1,0},{8,10},{10,12},{12... | collective-permute-start | bytes 1966088 | tf_op jit(solution)/shard_map/ppermute | solution.py:117
  350.7 51.6 %collective-permute-start.26 = (bf16[160,2048]{1,0:T(8,128)(2,1)S(1)}, bf16[160,2048]{1,0:T(8,128)(2,1)S(1)}, u32[]{:S(2)}, u32[]{:S(2)}) collective-permute-start(bf16[160,2048]{1,0:T(8,128)(2,1)S(1)} %multiply_convert_fusion), channel_id=1, source_target_pairs={{0,1},{2,0},{4,2},{6,4},{7,6},{5,7},{3,5},{1,3},{8,9},{10,8},{12,1... | collective-permute-start | bytes 1966088 | tf_op jit(solution)/shard_map/ppermute | solution.py:117
  452.1 50.2 %collective-permute-start.34 = (bf16[160,1024]{1,0:T(8,128)(2,1)S(1)}, bf16[160,1024]{1,0:T(8,128)(2,1)}, u32[]{:S(2)}, u32[]{:S(2)}) collective-permute-start(bf16[160,1024]{1,0:T(8,128)(2,1)S(1)} %get-tuple-element.342), channel_id=1, source_target_pairs={{0,2},{2,4},{4,6},{6,7},{7,5},{5,3},{3,1},{1,0},{8,10},{10,12},{12... | collective-permute-start | bytes 983048 | tf_op jit(solution)/shard_map/ppermute | solution.py:117
  459.7 50.9 %collective-permute-start.50 = (bf16[160,1024]{1,0:T(8,128)(2,1)}, bf16[160,1024]{1,0:T(8,128)(2,1)}, u32[]{:S(2)}, u32[]{:S(2)}) collective-permute-start(bf16[160,1024]{1,0:T(8,128)(2,1)} %get-tuple-element.340), channel_id=1, source_target_pairs={{0,2},{2,4},{4,6},{6,7},{7,5},{5,3},{3,1},{1,0},{8,10},{10,12},{12... | collective-permute-start | bytes 983048 | tf_op jit(solution)/shard_map/ppermute | solution.py:117
  489.0 393.3 %collective-permute-start.96 = (bf16[1024,2048]{1,0:T(8,128)(2,1)}, bf16[1024,2048]{1,0:T(8,128)(2,1)}, u32[]{:S(2)}, u32[]{:S(2)}) collective-permute-start(bf16[1024,2048]{1,0:T(8,128)(2,1)} %pad_maximum_fusion.5), channel_id=1, source_target_pairs={{0,8},{8,0},{16,24},{24,16},{1,9},{9,1},{17,25},{25,17},{2,10},{10... | collective-permute-start | bytes 12582920 | tf_op jit(solution)/shard_map/ppermute | solution.py:74
  499.8 72.0 %collective-permute-start.98 = (bf16[512,2048]{1,0:T(8,128)(2,1)S(1)}, bf16[512,2048]{1,0:T(8,128)(2,1)S(1)}, u32[]{:S(2)}, u32[]{:S(2)}) collective-permute-start(bf16[512,2048]{1,0:T(8,128)(2,1)S(1)} %pad_maximum_fusion.7), channel_id=1, source_target_pairs={{0,8},{8,0},{16,24},{24,16},{1,9},{9,1},{17,25},{25,17},{2,10},{10... | collective-permute-start | bytes 6291464 | tf_op jit(solution)/shard_map/ppermute | solution.py:74
  561.7 229.8 %collective-permute-start.41 = (bf16[160,2048]{1,0:T(8,128)(2,1)}, bf16[160,2048]{1,0:T(8,128)(2,1)}, u32[]{:S(2)}, u32[]{:S(2)}) collective-permute-start(bf16[160,2048]{1,0:T(8,128)(2,1)} %fusion.86), channel_id=1, source_target_pairs={{0,1},{2,0},{4,2},{6,4},{7,6},{5,7},{3,5},{1,3},{8,9},{10,8},{12,1... | collective-permute-start | bytes 1966088 | tf_op jit(solution)/shard_map/ppermute | solution.py:117
  571.7 220.1 %collective-permute-start.37 = (bf16[160,2048]{1,0:T(8,128)(2,1)}, bf16[160,2048]{1,0:T(8,128)(2,1)}, u32[]{:S(2)}, u32[]{:S(2)}) collective-permute-start(bf16[160,2048]{1,0:T(8,128)(2,1)} %fusion.83), channel_id=1, source_target_pairs={{0,2},{2,4},{4,6},{6,7},{7,5},{5,3},{3,1},{1,0},{8,10},{10,12},{12... | collective-permute-start | bytes 1966088 | tf_op jit(solution)/shard_map/ppermute | solution.py:117
  791.1 129.6 %collective-permute-start.66 = (bf16[1024,2048]{1,0:T(8,128)(2,1)}, bf16[1024,2048]{1,0:T(8,128)(2,1)}, u32[]{:S(2)}, u32[]{:S(2)}) collective-permute-start(bf16[1024,2048]{1,0:T(8,128)(2,1)} %pad_maximum_fusion.3), channel_id=1, source_target_pairs={{0,8},{8,0},{16,24},{24,16},{1,9},{9,1},{17,25},{25,17},{2,10},{10... | collective-permute-start | bytes 12582920 | tf_op jit(solution)/shard_map/ppermute | solution.py:74
  809.2 120.2 %collective-permute-start.86 = (bf16[1024,2048]{1,0:T(8,128)(2,1)}, bf16[1024,2048]{1,0:T(8,128)(2,1)}, u32[]{:S(2)}, u32[]{:S(2)}) collective-permute-start(bf16[1024,2048]{1,0:T(8,128)(2,1)} %pad_maximum_fusion.4), channel_id=1, source_target_pairs={{0,8},{8,0},{16,24},{24,16},{1,9},{9,1},{17,25},{25,17},{2,10},{10... | collective-permute-start | bytes 12582920 | tf_op jit(solution)/shard_map/ppermute | solution.py:74
  917.4 48.6 %collective-permute-start.97 = (bf16[512,2048]{1,0:T(8,128)(2,1)S(1)}, bf16[512,2048]{1,0:T(8,128)(2,1)S(1)}, u32[]{:S(2)}, u32[]{:S(2)}) collective-permute-start(bf16[512,2048]{1,0:T(8,128)(2,1)S(1)} %fusion.66), channel_id=1, source_target_pairs={{0,16},{8,24},{16,0},{24,8},{1,17},{9,25},{17,1},{25,9},{2,18},{10... | collective-permute-start | bytes 6291464 | tf_op jit(solution)/shard_map/ppermute | solution.py:74
  925.6 85.4 %collective-permute-start.67 = (bf16[512,2048]{1,0:T(8,128)(2,1)}, bf16[512,2048]{1,0:T(8,128)(2,1)}, u32[]{:S(2)}, u32[]{:S(2)}) collective-permute-start(bf16[512,2048]{1,0:T(8,128)(2,1)} %fusion.71), channel_id=1, source_target_pairs={{0,16},{8,24},{16,0},{24,8},{1,17},{9,25},{17,1},{25,9},{2,18},{10... | collective-permute-start | bytes 6291464 | tf_op jit(solution)/shard_map/ppermute | solution.py:74
  934.4 114.3 %collective-permute-start.87 = (bf16[512,2048]{1,0:T(8,128)(2,1)}, bf16[512,2048]{1,0:T(8,128)(2,1)}, u32[]{:S(2)}, u32[]{:S(2)}) collective-permute-start(bf16[512,2048]{1,0:T(8,128)(2,1)} %fusion.69), channel_id=1, source_target_pairs={{0,16},{8,24},{16,0},{24,8},{1,17},{9,25},{17,1},{25,9},{2,18},{10... | collective-permute-start | bytes 6291464 | tf_op jit(solution)/shard_map/ppermute | solution.py:74
  972.0 130.3 %all-to-all-start = ((bf16[8,64,2048]{2,1,0:T(8,128)(2,1)}), bf16[8,64,2048]{2,1,0:T(8,128)(2,1)}, u32[]{:S(2)}, u32[]{:S(2)}) async-start(bf16[8,64,2048]{2,1,0:T(8,128)(2,1)} %bitcast.40), calls=%async_computation | async-start | bytes 4194304 | tf_op jit(solution)/shard_map/all_to_all | solution.py:296
  (225 other events, 3435.5 us)

commit v2 on v1

v2 whole, which is shorter than its diff:
```python
import functools

import jax
import jax.numpy as jnp
from jax import lax
from jax.experimental import pallas as pl
from jax.experimental.pallas import tpu as pltpu
from jax.sharding import PartitionSpec as P

HEAD = 64
NORM_EPS = 1e-05
ROPE_BASE = 500000.0
MASKED = -1e30
VARIANTS = 5
BF = jnp.bfloat16
F32 = jnp.float32
MIB = 2**20


def dot(a, b):
    return jnp.dot(a, b, preferred_element_type=F32)


def dot_nt(a, b):
    return lax.dot_general(a, b, (((1,), (1,)), ((), ())), preferred_element_type=F32)


def fill_bias(sc, bias, own, block, ends_at, ends):
    for j in range(2):
        place = sc[own + j] * block + lax.broadcasted_iota(jnp.int32, bias.shape[1:], 0)
        key = lax.broadcasted_iota(jnp.int32, bias.shape[1:], 1)
        start = jnp.zeros_like(place)
        for s in range(ends):
            end = sc[ends_at + s]
            start = jnp.where(place >= end, end, start)
        bias[j] = jnp.where((key >= start) & (key <= place), 0.0, MASKED)


def fill_keys(sc, chunks, keys, values, block, blocks_at):
    for r, chunk in enumerate(chunks):
        for j in range(2):
            at = pl.multiple_of(sc[blocks_at + 2 * r + j] * block, 16)
            part = chunk[j * block : (j + 1) * block, :]
            for g in range(2):
                keys[g, pl.ds(at, block), :] = part[:, g * HEAD : (g + 1) * HEAD]
                values[g, pl.ds(at, block), :] = part[:, 2 * HEAD + g * HEAD : 2 * HEAD + (g + 1) * HEAD]


def split_heads(ref, out, block, group):
    for g in range(2):
        for j in range(2):
            for h in range(group):
                lane = (g * group + h) * HEAD
                out[g, j, h * block : (h + 1) * block, :] = ref[
                    j * block : (j + 1) * block, lane : lane + HEAD
                ]


def join_heads(out, block, group):
    rows = []
    for j in range(2):
        rows.append(
            jnp.concatenate(
                [out[g, j, h * block : (h + 1) * block, :] for g in range(2) for h in range(group)],
                axis=1,
            )
        )
    return jnp.concatenate(rows, axis=0)


def visible(sc, own, j, block, step):
    return (sc[own + j] * block + block - 1) // step + 1


def forward_kernel(n, group, ends, sc, q_ref, *rest):
    chunks, (o_ref, lse_ref), (bias, keys, values, queries, outs) = (
        rest[:n],
        rest[n : n + 2],
        rest[n + 2 :],
    )
    block = q_ref.shape[0] // 2
    total = keys.shape[1]
    step = total // VARIANTS
    pair = pl.program_id(0)

    @pl.when(pair == 0)
    def _():
        fill_bias(sc, bias, 1, block, 3 + 2 * n, ends)
        lse_ref[...] = jnp.zeros_like(lse_ref)

    fill_keys(sc, chunks, keys, values, block, 3)
    split_heads(q_ref, queries, block, group)

    def one(g, j, length):
        scores = dot_nt(queries[g, j], keys[g, :length, :])
        scores = (scores.reshape(group, block, length) + bias[j, :, :length][None]).reshape(
            group * block, length
        )
        peak = jnp.max(scores, axis=-1, keepdims=True)
        expd = jnp.exp(scores - peak)
        row_total = jnp.sum(expd, axis=-1, keepdims=True)
        mixed = dot(expd.astype(BF), values[g, :length, :])
        outs[g, j] = mixed / row_total
        lse = peak + jnp.log(row_total)
        lane = lax.broadcasted_iota(jnp.int32, (block, lse_ref.shape[1]), 1)
        rows = pl.ds(pl.multiple_of(j * block, 16), block)
        kept = lse_ref[rows, :]
        for h in range(group):
            kept = jnp.where(
                lane == (pair * 2 + g) * group + h, lse[h * block : (h + 1) * block], kept
            )
        lse_ref[rows, :] = kept

    def both(at, carry):
        g, j = at // 2, at % 2
        count = visible(sc, 1, j, block, step)
        for v in range(1, VARIANTS + 1):
            pl.when(count == v)(functools.partial(one, g, j, v * step))
        return carry

    lax.fori_loop(0, 4, both, 0)
    o_ref[...] = join_heads(outs, block, group).astype(o_ref.dtype)


def attention_forward(scalars, queries, chunks, ends):
    n = len(chunks)
    rows, width = queries.shape
    group = width // HEAD // 8
    block, total = rows // 2, rows * n
    pairs = 4
    return pl.pallas_call(
        functools.partial(forward_kernel, n, group, ends),
        grid_spec=pltpu.PrefetchScalarGridSpec(
            num_scalar_prefetch=1,
            grid=(pairs,),
            in_specs=[pl.BlockSpec((rows, width // pairs), lambda p, sc: (0, p))]
            + [pl.BlockSpec((rows, 4 * HEAD), lambda p, sc: (0, p))] * n,
            out_specs=[
                pl.BlockSpec((rows, width // pairs), lambda p, sc: (0, p ^ sc[0])),
                pl.BlockSpec((rows, 128), lambda p, sc: (0, 0)),
            ],
            scratch_shapes=[
                pltpu.VMEM((2, block, total), F32),
                pltpu.VMEM((2, total, HEAD), BF),
                pltpu.VMEM((2, total, HEAD), BF),
                pltpu.VMEM((2, 2, group * block, HEAD), BF),
                pltpu.VMEM((2, 2, group * block, HEAD), F32),
            ],
        ),
        out_shape=[
            jax.ShapeDtypeStruct((rows, width), BF),
            jax.ShapeDtypeStruct((rows, 128), F32),
        ],
        compiler_params=pltpu.CompilerParams(vmem_limit_bytes=48 * 2**20),
        cost_estimate=cost(18),
        name="attention_forward",
    )(scalars, queries, *chunks)


def backward_kernel(n, group, ends, first, sc, q_ref, do_ref, lse_ref, cos_ref, sin_ref, *rest):
    chunks, (dq_ref, dkv_ref), scratch = rest[:n], rest[n : n + 2], rest[n + 2 :]
    bias, keys, values, queries, grads, outs, dkeys, dvalues, flat = scratch
    block = q_ref.shape[0] // 2
    total = keys.shape[1]
    step = total // VARIANTS
    pair = pl.program_id(0) + first

    @pl.when(pair == first)
    def _():
        fill_bias(sc, bias, 1, block, 3 + 2 * n, ends)

    fill_keys(sc, chunks, keys, values, block, 3)
    split_heads(q_ref, queries, block, group)
    split_heads(do_ref, grads, block, group)
    dkeys[...] = jnp.zeros_like(dkeys)
    dvalues[...] = jnp.zeros_like(dvalues)

    def one(g, j, length):
        query, grad = queries[g, j], grads[g, j]
        key, value = keys[g, :length, :], values[g, :length, :]
        rows = pl.ds(pl.multiple_of(j * block, 16), block)
        kept = lse_ref[rows, :]
        lane = lax.broadcasted_iota(jnp.int32, kept.shape, 1)
        lse = jnp.concatenate(
            [
                jnp.sum(
                    jnp.where(lane == (pair * 2 + g) * group + h, kept, 0.0), axis=1, keepdims=True
                )
                for h in range(group)
            ],
            axis=0,
        )
        scores = dot_nt(query, key)
        scores = (scores.reshape(group, block, length) + bias[j, :, :length][None]).reshape(
            group * block, length
        )
        prob = jnp.exp(scores - lse)
        dprob = dot_nt(grad, value)
        weighted = prob * dprob
        row_dot = jnp.sum(weighted, axis=-1, keepdims=True)
        dscore = (weighted - prob * row_dot).astype(BF)
        outs[g, j] = dot(dscore, key)
        dkeys[g, :, :length] += dot(query.T, dscore)
        dvalues[g, :, :length] += dot(grad.T, prob.astype(BF))

    def both(at, carry):
        g, j = at // 2, at % 2
        count = visible(sc, 1, j, block, step)
        for v in range(1, VARIANTS + 1):
            pl.when(count == v)(functools.partial(one, g, j, v * step))
        return carry

    lax.fori_loop(0, 4, both, 0)
    dq = join_heads(outs, block, group) * (1.0 / 8.0)
    cosine, sine = cos_ref[...], sin_ref[...]
    low = lax.broadcasted_iota(jnp.int32, cosine.shape, 1) % HEAD < HEAD // 2
    for t in range(dq.shape[1] // 128):
        part = dq[:, t * 128 : (t + 1) * 128]
        turned = jnp.where(low, pltpu.roll(part, 96, 1), pltpu.roll(part, 32, 1))
        dq_ref[:, t * 128 : (t + 1) * 128] = (part * cosine - turned * sine).astype(dq_ref.dtype)
    flat[:, : 2 * HEAD] = jnp.concatenate([dkeys[0], dkeys[1]], axis=0).T
    flat[:, 2 * HEAD :] = jnp.concatenate([dvalues[0], dvalues[1]], axis=0).T
    for r in range(2 * n):
        at = pl.multiple_of(sc[3 + r] * block, 16)
        dkv_ref[r * block : (r + 1) * block, :] = flat[pl.ds(at, block), :].astype(dkv_ref.dtype)


def attention_backward(scalars, queries, grads, lse, cosine, sine, chunks, ends, pairs):
    n = len(chunks)
    rows, width = queries.shape
    group = width // HEAD // 8
    block, total = rows // 2, rows * n
    first, steps = pairs
    whole = pl.BlockSpec((rows, 128), lambda p, sc: (0, 0))
    wide = pl.BlockSpec((rows, width // 4), lambda p, sc: (0, p + first))
    return pl.pallas_call(
        functools.partial(backward_kernel, n, group, ends, first),
        grid_spec=pltpu.PrefetchScalarGridSpec(
            num_scalar_prefetch=1,
            grid=(steps,),
            in_specs=[
                wide,
                pl.BlockSpec((rows, width // 4), lambda p, sc: (0, (p + first) ^ sc[0])),
                whole,
                whole,
                whole,
            ]
            + [pl.BlockSpec((rows, 4 * HEAD), lambda p, sc: (0, p + first))] * n,
            out_specs=[
                pl.BlockSpec((rows, width // 4), lambda p, sc: (0, p)),
                pl.BlockSpec((total, 4 * HEAD), lambda p, sc: (0, p)),
            ],
            scratch_shapes=[
                pltpu.VMEM((2, block, total), F32),
                pltpu.VMEM((2, total, HEAD), BF),
                pltpu.VMEM((2, total, HEAD), BF),
                pltpu.VMEM((2, 2, group * block, HEAD), BF),
                pltpu.VMEM((2, 2, group * block, HEAD), BF),
                pltpu.VMEM((2, 2, group * block, HEAD), F32),
                pltpu.VMEM((2, HEAD, total), F32),
                pltpu.VMEM((2, HEAD, total), F32),
                pltpu.VMEM((total, 4 * HEAD), F32),
            ],
        ),
        out_shape=[
            jax.ShapeDtypeStruct((rows, steps * width // 4), BF),
            jax.ShapeDtypeStruct((total, steps * 4 * HEAD), BF),
        ],
        compiler_params=pltpu.CompilerParams(vmem_limit_bytes=56 * 2**20),
        cost_estimate=cost(26),
        name="attention_backward",
    )(scalars, queries, grads, lse, cosine, sine, *chunks)


def params(mib):
    return pltpu.CompilerParams(vmem_limit_bytes=mib * MIB)


def cost(micros):
    return pl.CostEstimate(flops=int(micros * 1e7), bytes_accessed=0, transcendentals=0)


def row_scale(values):
    return lax.rsqrt(jnp.mean(values * values, axis=-1, keepdims=True) + NORM_EPS)


def quarter(f, d, size):
    return pl.ds(pl.multiple_of((f ^ d) * size, size), size)


def norm_kernel(f_ref, x_ref, gain_ref, h_ref):
    inverse = row_scale(x_ref[...].astype(F32))
    size = x_ref.shape[1] // 4
    for d in range(4):
        part = x_ref[:, quarter(f_ref[0], d, size)].astype(F32) * inverse
        h_ref[:, d * size : (d + 1) * size] = (
            part * gain_ref[:, d * size : (d + 1) * size]
        ).astype(BF)


def smem():
    return pl.BlockSpec(memory_space=pltpu.SMEM)


def vmem():
    return pl.BlockSpec(memory_space=pltpu.VMEM)


def norm_rows(scalars, rows, gain):
    return pl.pallas_call(
        norm_kernel,
        in_specs=[smem(), vmem(), vmem()],
        out_specs=vmem(),
        out_shape=jax.ShapeDtypeStruct(rows.shape, BF),
        compiler_params=params(32),
        cost_estimate=cost(1),
        name="norm_rows",
    )(scalars, rows, gain)


def project_kernel(scale, turned_tiles, x_ref, cos_ref, sin_ref, *refs):
    weights, out_ref = refs[:-1], refs[-1]
    size = x_ref.shape[1] // 4
    parts = []
    for at in range(0, len(weights), 4):
        parts.append(
            sum(
                dot(x_ref[:, d * size : (d + 1) * size], w[...])
                for d, w in enumerate(weights[at : at + 4])
            )
        )
    cosine, sine = cos_ref[...], sin_ref[...]
    low = lax.broadcasted_iota(jnp.int32, cosine.shape, 1) % HEAD < HEAD // 2
    tiles = [p[:, t * 128 : (t + 1) * 128] for p in parts for t in range(p.shape[1] // 128)]
    for t, part in enumerate(tiles):
        if t < turned_tiles:
            turned = jnp.where(low, pltpu.roll(part, 96, 1), pltpu.roll(part, 32, 1))
            part = part * cosine + turned * sine
        part = part.astype(BF)
        if scale != 1.0:
            part = (part.astype(F32) * scale).astype(BF)
        out_ref[:, t * 128 : (t + 1) * 128] = part


def project(rows, cosine, sine, weights, turned_tiles, scale, micros):
    count, depth = rows.shape
    size, width = weights[0][0].shape
    part = 256 // len(weights)
    whole = lambda a: pl.BlockSpec(a.shape, lambda j: (0, 0))
    return pl.pallas_call(
        functools.partial(project_kernel, scale, turned_tiles),
        grid=(width // part,),
        in_specs=[whole(rows), whole(cosine), whole(sine)]
        + [pl.BlockSpec((size, part), lambda j: (0, j))] * (4 * len(weights)),
        out_specs=pl.BlockSpec((count, 256), lambda j: (0, j)),
        out_shape=jax.ShapeDtypeStruct((count, width * len(weights)), BF),
        compiler_params=params(32),
        cost_estimate=cost(micros),
        name="project",
    )(rows, cosine, sine, *[w for shards in weights for w in shards])


def out_kernel(f_ref, o_ref, x_ref, gain_ref, w0, w1, w2, w3, r_ref, h_ref):
    size = o_ref.shape[1] // 4
    tile = w0.shape[1]
    total = sum(
        dot(o_ref[:, d * size : (d + 1) * size], w[...]) for d, w in enumerate((w0, w1, w2, w3))
    )
    at = pl.ds(pl.multiple_of(pl.program_id(0) * tile, tile), tile)
    r_ref[:, at] = x_ref[:, at].astype(F32) + total

    @pl.when(pl.program_id(0) == pl.num_programs(0) - 1)
    def _():
        norm_kernel(f_ref, r_ref, gain_ref, h_ref)


def out_project(scalars, mixed, tokens, gain, weights):
    count, depth = mixed.shape
    size, width = weights[0].shape
    whole = lambda a: pl.BlockSpec(a.shape, lambda j: (0, 0))
    return pl.pallas_call(
        out_kernel,
        grid=(width // 256,),
        in_specs=[smem(), whole(mixed), whole(tokens), whole(gain)]
        + [pl.BlockSpec((size, 256), lambda j: (0, j))] * 4,
        out_specs=[whole(tokens), whole(tokens)],
        out_shape=[
            jax.ShapeDtypeStruct((count, width), F32),
            jax.ShapeDtypeStruct((count, width), BF),
        ],
        compiler_params=params(32),
        cost_estimate=cost(6),
        name="out_project",
    )(scalars, mixed, tokens, gain, *weights)


def norm_back_kernel(wide, f_ref, x_ref, gain_ref, base_ref, *rest):
    terms, outs = rest[:-wide], rest[-wide:]
    x = x_ref[...].astype(F32)
    inverse = row_scale(x)
    size = x_ref.shape[1] // 4
    f = f_ref[0]
    grads, normed = [], []
    dot_sum = 0.0
    for d in range(4):
        cols = slice(d * size, (d + 1) * size)
        grad = sum(t[:, cols].astype(F32) for t in terms)
        part = x_ref[:, quarter(f, d, size)].astype(F32) * inverse
        outs[1][:, cols] = jnp.sum(grad * part, axis=0, keepdims=True)
        grad = grad * gain_ref[:, cols]
        dot_sum += jnp.sum(grad * part, axis=-1, keepdims=True)
        grads.append(grad)
        normed.append(part)
    mean = dot_sum / x_ref.shape[1]
    for d in range(4):
        at = quarter(f, d, size)
        value = base_ref[:, at].astype(F32) + inverse * (grads[d] - normed[d] * mean)
        outs[0][:, at] = value
        if wide == 3:
            outs[2][:, at] = value.astype(BF)


def norm_back(scalars, rows, gain, base, terms, rounded):
    wide = 3 if rounded else 2
    shapes = [
        jax.ShapeDtypeStruct(rows.shape, F32),
        jax.ShapeDtypeStruct((1, rows.shape[1]), F32),
        jax.ShapeDtypeStruct(rows.shape, BF),
    ][:wide]
    return pl.pallas_call(
        functools.partial(norm_back_kernel, wide),
        in_specs=[smem()] + [vmem()] * (3 + len(terms)),
        out_specs=[vmem()] * wide,
        out_shape=shapes,
        compiler_params=params(40),
        cost_estimate=cost(2),
        name="norm_back",
    )(scalars, rows, gain, base, *terms)


def back_kernel(pairs, based, *refs):
    out_ref = refs[-1]
    step = pl.program_id(0)
    tile = refs[pairs].shape[0]
    size = tile * pl.num_programs(0)
    for d in range(4):
        at = pl.ds(pl.multiple_of(d * size + step * tile, tile), tile)
        total = sum(dot_nt(refs[i][...], refs[pairs + 4 * i + d][...]) for i in range(pairs))
        if based:
            total += refs[5 * pairs][:, at]
        out_ref[:, at] = total.astype(out_ref.dtype)


def back_project(rows, weights, kind, micros, base=None):
    count = rows[0].shape[0]
    size = weights[0][0].shape[0]
    whole = pl.BlockSpec((count, 4 * size), lambda j: (0, 0))
    extra = [] if base is None else [base]
    return pl.pallas_call(
        functools.partial(back_kernel, len(rows), base is not None),
        grid=(2,),
        in_specs=[pl.BlockSpec(r.shape, lambda j: (0, 0)) for r in rows]
        + [pl.BlockSpec((size // 2, w.shape[1]), lambda j: (j, 0)) for ws in weights for w in ws]
        + [whole] * len(extra),
        out_specs=whole,
        out_shape=jax.ShapeDtypeStruct((count, 4 * size), kind),
        compiler_params=params(40),
        cost_estimate=cost(micros),
        name="back_project",
    )(*rows, *[w for ws in weights for w in ws], *extra)


def cross(value):
    half = value.shape[1] // 2
    return jnp.concatenate([value[:, half:], value[:, :half]], axis=1)


def feed_kernel(m, kept, crossed, *refs):
    hidden, grads = refs[:m], refs[m : 2 * m]
    gates, ups = refs[2 * m : 2 * m + 4], refs[2 * m + 4 : 2 * m + 8]
    down_ref = refs[2 * m + 8]
    outs = refs[2 * m + 9 + kept :]
    rows_h, rows_dy, act_ref, dgu_ref, dh_ref, h_s, dy_s, dh_s = outs
    step = pl.program_id(0)
    count = hidden[0].shape[0]
    size = gates[0].shape[0]
    tile = gates[0].shape[1]

    @pl.when(step == 0)
    def _():
        for i in range(m):
            at = slice(i * count, (i + 1) * count)
            h_s[at], dy_s[at] = hidden[i][...], grads[i][...]
            rows_h[at], rows_dy[at] = hidden[i][...], grads[i][...]

    def ahead(weights):
        parts = [dot(h_s[:, d * size : (d + 1) * size], w[...]) for d, w in enumerate(weights)]
        if not crossed:
            return sum(parts)
        return parts[0] + parts[2] + cross(parts[1] + parts[3])

    gate, up = ahead(gates), ahead(ups)
    sig = jax.nn.sigmoid(gate)
    silu = gate * sig
    act_ref[...] = (silu * up).astype(BF)
    grad_act = dot_nt(dy_s[...], down_ref[...])
    grad_gate = (grad_act * up * sig * (1.0 + gate * (1.0 - sig))).astype(BF)
    grad_up = (grad_act * silu).astype(BF)
    dgu_ref[:, :tile] = grad_gate
    dgu_ref[:, tile:] = grad_up
    pairs = [(grad_gate, grad_up)] * 4
    if crossed:
        pairs[1] = pairs[3] = (cross(grad_gate), cross(grad_up))
    last = pl.num_programs(0) - 1
    for d in range(4):
        cols = slice(d * size, (d + 1) * size)
        dh = dot_nt(pairs[d][0], gates[d][...]) + dot_nt(pairs[d][1], ups[d][...])

        @pl.when(step == 0)
        def _():
            dh_s[:, cols] = dh

        @pl.when(step > 0)
        def _():
            dh_s[:, cols] += dh

    @pl.when(step == last)
    def _():
        dh_ref[...] = dh_s[...].astype(BF)


def feed_tile(units):
    crossed = units >= 128
    return (2 * units if crossed else 4 * units), crossed


def feed(hidden, grads, gate_up, down, slot, kept, n):
    m = len(hidden)
    count, depth = hidden[0].shape
    width = down.shape[0]
    tile, crossed = feed_tile(width // 4)
    steps = width // tile
    rows = m * count
    size = depth // 4

    def shard(d, part):
        flip = d >> 1 if crossed else 0
        return pl.BlockSpec((size, tile), lambda e: (0, part * steps + (e ^ flip)))

    chunk = pl.BlockSpec((count, depth), lambda e: (0, 0))
    block = pl.BlockSpec((rows, depth), lambda e: (slot, 0))
    shapes = [
        jax.ShapeDtypeStruct((n * count, depth), BF),
        jax.ShapeDtypeStruct((n * count, depth), BF),
        jax.ShapeDtypeStruct((n * count, width), BF),
        jax.ShapeDtypeStruct((n * count, 2 * width), BF),
        jax.ShapeDtypeStruct((rows, depth), BF),
    ]
    first = 2 * m + 9
    *kept, dh = pl.pallas_call(
        functools.partial(feed_kernel, m, len(kept), crossed),
        grid=(steps,),
        in_specs=[chunk] * (2 * m)
        + [shard(d, 0) for d in range(4)]
        + [shard(d, 1) for d in range(4)]
        + [pl.BlockSpec((tile, depth), lambda e: (e, 0))]
        + [pl.BlockSpec(memory_space=pl.ANY)] * len(kept),
        out_specs=[
            block,
            block,
            pl.BlockSpec((rows, tile), lambda e: (slot, e)),
            pl.BlockSpec((rows, 2 * tile), lambda e: (slot, e)),
            pl.BlockSpec((rows, depth), lambda e: (0, 0)),
        ],
        scratch_shapes=[pltpu.VMEM((rows, depth), BF)] * 2 + [pltpu.VMEM((rows, depth), F32)],
        out_shape=shapes,
        input_output_aliases={first + i: i for i in range(len(kept))},
        compiler_params=params(48),
        cost_estimate=cost(8 + 4 * m),
        name="feed",
    )(*hidden, *grads, *gate_up, *gate_up, down, *kept)
    return kept, [dh[i * count : (i + 1) * count] for i in range(m)]


def down_kernel(sc, act_ref, down_ref, y_ref):
    y_ref[...] = dot(act_ref[...], down_ref[...]).astype(BF)


def down_rows(scalars, act, down, n):
    count = act.shape[0] // n
    at = scalars.shape[0] - n
    return pl.pallas_call(
        down_kernel,
        grid_spec=pltpu.PrefetchScalarGridSpec(
            num_scalar_prefetch=1,
            grid=(n,),
            in_specs=[
                pl.BlockSpec((count, act.shape[1]), lambda i, sc: (i, 0)),
                pl.BlockSpec(down.shape, lambda i, sc: (0, 0)),
            ],
            out_specs=pl.BlockSpec((count, down.shape[1]), lambda i, sc: (sc[at + i], 0)),
        ),
        out_shape=jax.ShapeDtypeStruct((n * count, down.shape[1]), BF),
        compiler_params=params(32),
        cost_estimate=cost(12),
        name="down_rows",
    )(scalars, act, down)


def place_kernel(sc, *refs):
    out = refs[-1]
    count = refs[0].shape[0]
    for i, part in enumerate(refs[:-1]):
        out[pl.ds(pl.multiple_of(sc[i] * count, count), count), :] = part[...]


def place_rows(places, parts):
    count, width = parts[0].shape
    return pl.pallas_call(
        place_kernel,
        in_specs=[smem()] + [vmem()] * len(parts),
        out_specs=vmem(),
        out_shape=jax.ShapeDtypeStruct((count * len(parts), width), parts[0].dtype),
        compiler_params=params(24),
        cost_estimate=cost(2),
        name="place_rows",
    )(places, *parts)


def tn_kernel(adds, outs, left_ref, right_ref, *refs):
    turned = refs[-1]
    i, j = pl.program_id(0), pl.program_id(1)

    @pl.when(j == 0)
    def _():
        turned[...] = left_ref[...].T

    total = dot(turned[...], right_ref[...])
    for (low, high, crossed), extra in zip(adds, refs):
        extra = extra[...].astype(F32)
        if crossed:
            extra = cross(extra)
        if low is not None:
            extra = jnp.where((j >= low) & (j < high), extra, 0.0)
        total += extra
    for (row, low, high), out in zip(outs, refs[len(adds) :]):

        @pl.when((i == row) & (j >= low) & (j < high))
        def _():
            out[...] = total.astype(out.dtype)


def tn_blocks(left, right, blocks, kind, micros, adds=(), pieces=1):
    rows, depth = left.shape
    size, width = depth // 4, right.shape[1]
    tile = min(width, 512)
    steps = width // tile
    pieces = min(pieces, steps)
    if size % 128:
        result = []
        for block in blocks:
            total = lax.dot_general(
                left[:, block * size : (block + 1) * size],
                right,
                (((0,), (0,)), ((), ())),
                preferred_element_type=F32,
            )
            for array, part, parts, _ in adds:
                at = part * (width // parts)
                total = total.at[:, at : at + width // parts].add(array.astype(F32))
            result.append(jnp.split(total.astype(kind), pieces, axis=1))
        return result
    first = blocks[0]
    stride = blocks[1] - first if len(blocks) > 1 else 0

    def window(part, parts):
        count = max(1, steps // parts)
        return part * count, (part + 1) * count

    def added_spec(part, parts):
        low, high = window(part, parts)
        return pl.BlockSpec((size, tile), lambda i, j: (0, jnp.clip(j - low, 0, high - low - 1)))

    def out_spec(row, low, high):
        def index(i, j):
            at = jnp.clip(j - low, 0, high - low - 1)
            return (0, jnp.where(i < row, 0, jnp.where(i > row, high - low - 1, at)))

        return pl.BlockSpec((size, tile), index)

    windows = [
        (*(window(part, parts) if parts > 1 and steps > 1 else (None, None)), crossed)
        for _, part, parts, crossed in adds
    ]
    outs = [(row, *window(piece, pieces)) for row in range(len(blocks)) for piece in range(pieces)]
    result = pl.pallas_call(
        functools.partial(tn_kernel, windows, outs),
        grid=(len(blocks), steps),
        in_specs=[
            pl.BlockSpec((rows, size), lambda i, j: (0, first + stride * i)),
            pl.BlockSpec((rows, tile), lambda i, j: (0, j)),
        ]
        + [added_spec(part, parts) for _, part, parts, _ in adds],
        out_specs=[out_spec(*out) for out in outs],
        out_shape=[jax.ShapeDtypeStruct((size, width // pieces), kind)] * len(outs),
        scratch_shapes=[pltpu.VMEM((size, rows), BF)],
        compiler_params=params(32),
        cost_estimate=cost(micros),
        name="tn_blocks",
    )(left, right, *[a[0] for a in adds])
    return [list(result[row * pieces : (row + 1) * pieces]) for row in range(len(blocks))]


def spread_kernel(n, units, f_ref, *refs):
    arrays, outs = refs[:-2], refs[-2:]
    tile = arrays[0].shape[2] // 2
    span = outs[0].shape[1] // 4
    c = pl.program_id(0)
    e = 0
    for array in arrays:
        for at in range(0, tile, units):
            start = (f_ref[0] ^ e) * span + c * units
            e += 1
            for part in range(2):
                value = array[0, :, part * tile + at : part * tile + at + units].astype(F32)
                outs[part][:, pl.ds(pl.multiple_of(start, units), units)] = value


def spread(scalars, arrays, units):
    n, rows, _ = arrays[0].shape
    width = 4 * n * units
    return pl.pallas_call(
        functools.partial(spread_kernel, n, units),
        grid=(n,),
        in_specs=[smem()] + [pl.BlockSpec((1, *a.shape[1:]), lambda i: (i, 0, 0)) for a in arrays],
        out_specs=[pl.BlockSpec((rows, width), lambda i: (0, 0))] * 2,
        out_shape=[jax.ShapeDtypeStruct((rows, width), F32)] * 2,
        compiler_params=params(32),
        cost_estimate=cost(4),
        name="spread",
    )(scalars, *arrays)


def swap_fsdp(value, d):
    return lax.ppermute(value, "fsdp", [(i, i ^ d) for i in range(4)])


def after(value, *others):
    return lax.optimization_barrier((value, others))[0] if others else value


def gather_fsdp(shard):
    across = swap_fsdp(shard, 2)
    return [shard, swap_fsdp(shard, 1), across, swap_fsdp(across, 1)]


def xor_blocks(value, f, axis):
    size = value.shape[axis] // 4
    return jnp.concatenate(
        [lax.dynamic_slice_in_dim(value, (f ^ d) * size, size, axis) for d in range(4)], axis=axis
    )


def swap_cols(value, d, parts):
    width = value.shape[1] // (4 * parts)
    return jnp.concatenate(
        [
            value[:, (p * 4 + (e ^ d)) * width : (p * 4 + (e ^ d) + 1) * width]
            for p in range(parts)
            for e in range(4)
        ],
        axis=1,
    )


def ring_index(place, n):
    place = place % n
    return jnp.where(place < n // 2, 2 * place, 2 * (n - 1 - place) + 1)


def ring_shift(value, step, n):
    order = list(range(0, n, 2)) + list(range(n - 1, 0, -2))
    return lax.ppermute(value, "ctx", [(order[i], order[(i + step) % n]) for i in range(n)])


class Order:
    def __init__(self):
        self.last = ()

    def at(self, value):
        return after(value, *self.last)

    def done(self, value):
        self.last = (value,)
        return value

    def take(self, value):
        return self.done(self.at(value))

    def run(self, function, *args, **kwargs):
        return self.done(function(*self.at(args), **kwargs))


class Gather:
    def __init__(self, order, own, n):
        self.order, self.n, self.half, self.step = order, n, n // 2, 0
        self.chunks = {0: own}
        self.now = (own, own)
        self.width = own.shape[1] // 2

    def send(self):
        self.step += 1
        right, left = self.now
        if self.step == self.half:
            right, left = right[:, : self.width], left[:, self.width :]
        self.now = (ring_shift(right, 1, self.n), ring_shift(left, -1, self.n))

    def take(self):
        self.now = right, left = self.order.take(self.now)
        if self.step == self.half:
            self.chunks[self.half] = jnp.concatenate([right, left], axis=1)
        else:
            self.chunks[-self.step], self.chunks[self.step] = right, left

    def rest(self, hops=None):
        while self.step < self.half and hops != 0:
            self.take()
            self.send()
            hops = hops and hops - 1
        return self


class Scatter:
    def __init__(self, order, contrib, n):
        self.order, self.n, self.half, self.step = order, n, n // 2, 0
        self.contrib = contrib
        far = contrib(self.half)
        self.width = far.shape[1] // 2
        self.now = (far[:, : self.width].astype(BF), far[:, self.width :].astype(BF))

    def send(self):
        self.step += 1
        right, left = self.now
        self.now = (ring_shift(right, 1, self.n), ring_shift(left, -1, self.n))

    def take(self):
        self.now = got = self.order.take(self.now)
        r = self.half - self.step
        if r == 0:
            return (self.contrib(0), *got)
        got = [v.astype(F32) for v in got]
        width = self.width
        ahead, behind = self.contrib(r).astype(F32), self.contrib(-r).astype(F32)
        if self.step == 1:
            ahead = jnp.concatenate([ahead[:, :width] + got[0], ahead[:, width:]], axis=1)
            behind = jnp.concatenate([behind[:, :width], behind[:, width:] + got[1]], axis=1)
        else:
            ahead, behind = ahead + got[0], behind + got[1]
        self.now = (ahead.astype(BF), behind.astype(BF))

    def rest(self, hops=None):
        while self.step < self.half and hops != 0:
            self.take()
            self.send()
            hops = hops and hops - 1
        return self


def added(terms):
    return sum(t.astype(F32) for t in terms)


def deinterleave(both):
    runs = range(both.shape[1] // 256)
    return tuple(
        jnp.concatenate([both[:, p * 256 + o : p * 256 + o + 128] for p in runs], axis=1)
        for o in (0, 128)
    )


def turn_tables(block_ids, block, ends, starts):
    place = (block_ids[:, None] * block + jnp.arange(block, dtype=jnp.int32)[None, :]).reshape(-1)
    begin = jnp.max(jnp.where(place[:, None] >= starts[None, :], starts[None, :], 0), axis=1)
    freqs = ROPE_BASE ** (-(jnp.arange(HEAD // 2, dtype=F32) * 2.0 / HEAD))
    angle = (place - begin).astype(F32)[:, None] * freqs[None, :]
    cosine, sine = jnp.cos(angle), jnp.sin(angle)
    return (
        jnp.concatenate([cosine] * 4, axis=1),
        jnp.concatenate([-sine, sine, -sine, sine], axis=1),
    )


def turn_back(values, cosine, sine):
    parts = []
    for p in range(values.shape[1] // 128):
        part = values[:, p * 128 : (p + 1) * 128]
        if p % 2 == 0:
            low = lax.broadcasted_iota(jnp.int32, part.shape, 1) % HEAD < HEAD // 2
            turned = jnp.where(low, jnp.roll(part, -32, axis=1), jnp.roll(part, 32, axis=1))
            part = part * cosine - turned * sine
        parts.append(part)
    return jnp.concatenate(parts, axis=1)


def body(
    n,
    tokens,
    first_gain,
    query_weight,
    key_matrix,
    value_matrix,
    out_weight,
    second_gain,
    gate_weight,
    up_weight,
    down_weight,
    lengths,
    block_order,
    cotangent,
):
    token_rows, model = tokens.shape
    block = token_rows // 2
    c = lax.axis_index("ctx")
    f = lax.axis_index("fsdp")
    place = jnp.where(c % 2 == 0, c // 2, n - 1 - c // 2)
    half = n // 2
    rel = list(range(-(half - 1), half + 1))
    owners = ring_index(place + jnp.asarray(rel, jnp.int32), n)

    own_blocks = lax.dynamic_slice_in_dim(block_order, 2 * c, 2)
    key_blocks = jnp.take(block_order.reshape(n, 2), owners, axis=0).reshape(-1)
    seq_ends = jnp.cumsum(lengths[0])
    count = lengths.shape[1]
    slot_rel = [r for step in range(1, half) for r in (-step, step)] + [0, half]
    slot_owners = ring_index(place + jnp.asarray(slot_rel, jnp.int32), n)
    scalars = jnp.concatenate([f[None], own_blocks, key_blocks, seq_ends, slot_owners])
    scalars = scalars.astype(jnp.int32)
    cosine, sine = turn_tables(own_blocks, block, seq_ends, seq_ends - lengths[0])
    order = Order()

    units = gate_weight.shape[1] // (4 * n)
    span = gate_weight.shape[1] // 4
    width = 4 * units

    def own_units(weight):
        return [
            lax.dynamic_slice_in_dim(weight, (f ^ e) * span + c * units, units, 1)
            for e in range(4)
        ]

    gains = gather_fsdp(jnp.stack([first_gain, second_gain]))
    gains = jnp.concatenate(gains, axis=1).astype(F32)
    gain_one, gain_two = gains[:1], gains[1:]
    out_part = out_weight.shape[0] // n
    out_across = swap_fsdp(lax.dynamic_slice_in_dim(out_weight, c * out_part, out_part, 0), 2)
    key_across, value_across = swap_fsdp(key_matrix, 2), swap_fsdp(value_matrix, 2)
    grad_out = Gather(order, cotangent, n)
    grad_out.send()
    key_core, value_core = swap_fsdp(key_matrix, 1), swap_fsdp(value_matrix, 1)
    out_core, query_core = swap_fsdp(out_weight, 1), swap_fsdp(query_weight, 1)
    down_own = lax.dynamic_slice_in_dim(down_weight, c * units, units, 0)
    down_core = swap_fsdp(down_own, 1)

    hidden_one = order.run(norm_rows, scalars, tokens, gain_one)
    out_across = order.take(out_across)
    out_parts = Gather(order, out_across, n)
    out_parts.send()
    key_across = order.take(key_across)
    key_far = swap_fsdp(key_across, 1)
    out_parts.rest(1)
    value_across = order.take(value_across)
    value_far = swap_fsdp(value_across, 1)
    query_across = swap_fsdp(order.at(query_weight), 2)
    gate_up_own = order.done(
        jnp.concatenate(own_units(order.at(gate_weight)) + own_units(up_weight), axis=1)
    )
    gate_up_core = swap_fsdp(gate_up_own, 1)
    out_parts.rest(1)
    grad_out.take()
    key_far, value_far = order.take((key_far, value_far))
    weight_k = [key_matrix, key_core, key_across, key_far]
    weight_v = [value_matrix, value_core, value_across, value_far]
    kv_own = order.run(project, hidden_one, cosine, sine, [weight_k, weight_v], turned_tiles=1, scale=1.0, micros=4)
    kv = Gather(order, kv_own, n)
    kv.send()
    kv.rest(1)
    out_parts.take()
    kv.rest(1)
    query_across = order.take(query_across)
    query_far = swap_fsdp(query_across, 1)
    gate_up_across = swap_fsdp(order.at(gate_up_own), 2)
    down_across = swap_fsdp(order.at(after(down_own, query_across)), 2)
    kv.rest()
    kv.take()
    kv_chunks = [kv.chunks[r] for r in rel]
    out_parts.send()
    query_far = order.take(query_far)
    weight_q = [query_weight, query_core, query_across, query_far]

    queries = order.run(project, hidden_one, cosine, sine, [weight_q], turned_tiles=2, scale=0.125, micros=7)
    out_parts.rest()
    out_parts.take()
    out_across = order.run(place_rows, owners.astype(jnp.int32), [out_parts.chunks[r] for r in rel])
    out_far = swap_fsdp(out_across, 1)
    grad_out.send()
    mixed, lse = order.run(attention_forward, scalars, queries, kv_chunks, ends=count)
    grad_out.rest(1)
    weight_o = [out_weight, out_core, out_across, out_far]
    residual, hidden_two = order.run(out_project, scalars, mixed, tokens, gain_two, weight_o)
    grad_out.rest()
    hidden = Gather(order, hidden_two, n)
    hidden.send()
    gate_up_across = order.take(gate_up_across)
    gate_up_far = swap_fsdp(gate_up_across, 1)
    grad_out.take()
    down_across = order.take(down_across)
    down_far = swap_fsdp(down_across, 1)
    gate_up = [gate_up_own, gate_up_core, gate_up_across, gate_up_far]
    if units < 128:
        gate_up = [swap_cols(part, d, 2) for d, part in enumerate(gate_up)]
    down = jnp.concatenate([down_own, down_core, down_across, down_far], axis=0)

    kept, grads_two = [], {}
    for near in range(half + 1):
        group = (0,) if near == 0 else (half,) if near == half else (-near, near)
        slot = n - 2 if near == 0 else n - 1 if near == half else near - 1
        kept, parts = order.run(
            feed,
            [hidden.chunks[r] for r in group],
            [grad_out.chunks[r] for r in group],
            gate_up,
            down,
            slot=slot,
            kept=kept,
            n=n,
        )
        grads_two.update(zip(group, parts))
        if near < half:
            hidden.take()
        if near < half - 1:
            hidden.send()

    rows_h, rows_dy, act, grads = kept
    tile, crossed = feed_tile(units)
    waiting, under_way = [], []

    def tick():
        while under_way:
            mid, h = under_way.pop()
            mid[h] = order.take(mid[h])
        if waiting:
            mid, h = waiting.pop(0)
            mid[h] = swap_fsdp(order.at(mid[h]), 2)
            under_way.append((mid, h))

    class Product:
        def __init__(self, left, right, micros, by_units=False):
            self.left, self.right, self.micros, self.by_units = left, right, micros, by_units

        def kernel(self, blocks, kind, adds=(), pieces=1):
            def run(left, right, *arrays):
                own = [(a, *rest) for a, (_, *rest) in zip(arrays, adds)]
                micros = self.micros * len(blocks)
                return tn_blocks(left, right, blocks, kind, micros, own, pieces)

            return order.run(run, self.left, self.right, *[a for a, *_ in adds])

        def from_partner(self, value, d):
            return swap_cols(value, d, 2) if self.by_units and not crossed else value

        def first(self):
            self.near = [
                [swap_fsdp(piece, 1) for piece in row] for row in self.kernel((1, 3), BF, (), 4)
            ]

        def pieces(self, row):
            turned = self.by_units and crossed
            got = [self.from_partner(v, 1) for v in order.take(self.near[row])]
            return [(v, p, len(got), turned) for p, v in enumerate(got)]

        def second(self, halves=2):
            (self.mid,) = self.kernel((2,), BF, self.pieces(1), halves)
            waiting.extend((self.mid, h) for h in range(len(self.mid)))

        def last(self, kind):
            over = [self.from_partner(v, 2) for v in self.mid]
            if self.by_units and crossed:
                over = over[::-1]
            adds = [(v, h, len(over), False) for h, v in enumerate(over)]
            ((whole,),) = self.kernel((0,), kind, self.pieces(0) + adds)
            return whole

    sums = Scatter(order, lambda r: grads_two[r], n)
    sums.send()
    of_down = Product(act, rows_dy, 3)
    of_gate_up = Product(rows_h, grads, 5, True)
    of_down.first()
    sums.rest(1)
    of_gate_up.first()
    of_down.second(1)
    tick()
    sums.rest(1)
    of_gate_up.second()
    y_rows = order.run(down_rows, scalars, act, down, n=n)
    sums.rest(1)
    tick()
    down_grad = of_down.last(F32)
    sums.rest()
    grad_hidden_two = sums.take()
    grad_residual, gain_two_term, grad_branch = order.run(
        norm_back, scalars, residual, gain_two, cotangent, grad_hidden_two, rounded=True
    )
    grad_mixed = order.run(back_project, [grad_branch], [weight_o], kind=BF, micros=5)
    tick()
    y_own = lax.psum_scatter(order.at(y_rows), "ctx", scatter_dimension=0, tiled=True)
    of_out = Product(mixed, grad_branch, 2)
    of_out.first()

    parts = []

    def attention_part(first):
        parts.append(
            order.run(
                attention_backward,
                scalars,
                queries,
                grad_mixed,
                lse,
                cosine,
                sine,
                kv_chunks,
                ends=count,
                pairs=(first, 2),
            )
        )

    attention_part(0)
    of_out.second()
    tick()
    attention_part(2)
    grad_query = jnp.concatenate([p[0] for p in parts], axis=1)

    def kv_contrib(r):
        start = rel.index(r) * token_rows
        return jnp.concatenate([p[1][start : start + token_rows] for p in parts], axis=1)

    grad_kv = Scatter(order, kv_contrib, n)
    grad_kv.send()
    of_query = Product(hidden_one, grad_query, 2)
    of_query.first()
    grad_kv.rest(1)
    tick()
    gate_up_grad = of_gate_up.last(BF)
    rows = gate_up_grad.shape[0] // n
    gate_up_all = lax.all_to_all(
        gate_up_grad.reshape(n, rows, 2 * width), "ctx", 0, 0, tiled=False
    )
    grad_kv.rest(1)
    of_query.second()
    grad_hidden_one = order.run(back_project, [grad_query], [weight_q], kind=F32, micros=5)
    grad_kv.rest(1)
    tick()

    def scatter_rows(within):
        rows = within.shape[0] // n

        def contrib(r):
            start = ring_index(place + r, n) * rows
            return lax.dynamic_slice_in_dim(within, start, rows, 0)

        return Scatter(order, contrib, n)

    out_sums = scatter_rows(of_out.last(BF))
    grad_kv.rest()
    grad_kv = added(grad_kv.take())
    out_sums.send()
    grad_kv = turn_back(grad_kv, cosine, sine).astype(BF)
    grad_key, grad_value = deinterleave(grad_kv)
    grad_kv = jnp.concatenate([grad_key, grad_value], axis=1)
    of_kv = Product(hidden_one, grad_kv, 1.5)
    of_kv.first()
    grad_hidden_one = order.run(
        back_project, [grad_key, grad_value], [weight_k, weight_v], base=grad_hidden_one, kind=F32, micros=3
    )
    out_sums.rest(1)
    of_kv.second(1)
    tick()
    tokens_grad, gain_one_term = order.run(
        norm_back, scalars, tokens, gain_one, grad_residual, [grad_hidden_one], rounded=False
    )
    out_sums.rest(1)
    gain_terms = xor_blocks(jnp.concatenate([gain_one_term, gain_two_term], axis=0), f, 1)
    gain_terms = gain_terms.astype(BF).reshape(2, 4 * n, model // (4 * n)).transpose(1, 0, 2)
    gain_terms = lax.all_to_all(order.at(gain_terms), ("fsdp", "ctx"), 0, 0, tiled=False)
    out_sums.rest()
    out_grad = order.done(added(out_sums.take()))
    tick()
    gate_up_all = order.take(gate_up_all)
    if crossed:
        gate_up_all = gate_up_all.reshape(n, rows, width // tile, 2 * tile)
        gate_grad, up_grad = order.run(
            spread, scalars, [gate_up_all[:, :, s] for s in range(width // tile)], units=units
        )
    else:
        gate_up_all = gate_up_all.reshape(n, rows, 2, 4, units).transpose(2, 1, 3, 0, 4)
        gate_up_all = xor_blocks(gate_up_all, f, 2).reshape(2, rows, n * width).astype(F32)
        gate_grad, up_grad = order.done((gate_up_all[0], gate_up_all[1]))
    query_sums = scatter_rows(of_query.last(BF))
    query_sums.send()
    query_sums.rest(1)
    layer_out = order.done((residual + order.at(y_own).astype(F32)).astype(BF))
    query_sums.rest(1)
    tick()
    kv_sums = scatter_rows(of_kv.last(BF))
    kv_sums.send()
    query_sums.rest(1)
    kv_sums.rest(1)
    query_sums.rest()
    kv_sums.rest(1)
    query_grad = order.done(added(query_sums.take()))
    kv_sums.rest()
    gain_grads = jnp.sum(order.at(gain_terms).astype(F32), axis=0)
    kv_grad = added(kv_sums.take())
    kv_width = key_matrix.shape[1]
    key_grad, value_grad = kv_grad[:, :kv_width], kv_grad[:, kv_width:]
    return (
        layer_out,
        tokens_grad,
        gain_grads[0],
        query_grad,
        key_grad,
        value_grad,
        out_grad,
        gain_grads[1],
        gate_grad,
        up_grad,
        down_grad,
    )


def solution(mesh):
    rows, vector = P(("fsdp", "ctx"), None), P(("fsdp", "ctx"))
    weight = P("fsdp", None)

    def layer(*arrays):
        return body(mesh.shape["ctx"], *arrays)

    return jax.shard_map(
        layer,
        mesh=mesh,
        in_specs=(
            rows, P("fsdp"), weight, weight, weight, weight, P("fsdp"), weight, weight, weight,
            weight, P(), rows,
        ),
        out_specs=(rows, rows, vector, rows, rows, rows, rows, vector, rows, rows, rows),
        check_vma=False,
    )
```

time: 1140 us -> 714 us (0.63)
  matrix products: 306 us -> 0 us
  Pallas kernels: 0 us -> 230 us
  waiting for transfers between devices: 401 us -> 208 us
  other arithmetic: 131 us -> 37.4 us
  local copies, waits for them, and re-layouts: 161 us -> 73.4 us
  starting transfers between devices: 90.8 us -> 139 us
  blocking collectives: 28 us -> 0 us
    dot_general x99 -> x0, matrix products: 306 us -> none  [the longest x19 55.2 us: mm_nt(): lax.dot_general(left_in, right_in, (((1,), (1,)), ((), ())), preferred_el...]
    pallas_call x0 -> x35, Pallas kernels: none -> 230 us  [the longest x15 70 us: tn_blocks(): pl.pallas_call(functools.partial(tn_kernel, windows, outs), grid=(len(blo...]
    ppermute x28 -> x65, waiting for transfers between devices: 247 us -> 69.2 us  [swap_fsdp(): return lax.ppermute(value, 'fsdp', [(i, i ^ d) for i in range(4)])]
    concatenate x16 -> x17, other arithmetic: 53.3 us -> 5.02 us  [the longest x1 2.33 us: body(): down = jnp.concatenate([down_own, down_core, down_across, down_far], axis=0)]
    unnamed x359 -> x261, local copies, waits for them, and re-layouts: 83.1 us -> 50.7 us
    ppermute x72, starting transfers between devices: 72.9 us -> 104 us  [ring_shift(): lax.ppermute(value, 'ctx', [(order[i], order[(i + step) % n]) for i in ra...]
    unnamed x2 -> x0, blocking collectives: 28 us -> none
    ppermute x72, waiting for transfers between devices: 154 us -> 138 us  [ring_shift(): lax.ppermute(value, 'ctx', [(order[i], order[(i + step) % n]) for i in ra...]
  transfers between devices with their start and end apart: 101 -> 140, of which waited for: 37 -> 58; matrix products, arithmetic and copies ran while one was open for 52% -> 9% of each run, Pallas kernels for 0% -> 31%
where the time goes in v2:
time: 714 us; the launch traced here: 704 us
  Pallas kernels  230 us (32%)
  waiting for transfers between devices  208 us (29%)
  starting transfers between devices  139 us (19%)
  local copies, waits for them, and re-layouts  73.4 us (10%)
  other arithmetic  37.4 us (5%)
  between operations  16.2 us (2%)
    ppermute x72, waiting for transfers between devices, ring_shift(): lax.ppermute(value, 'ctx', [(order[i], order[(i + step) % n]) for i in ra...  138 us
    ppermute x72, starting transfers between devices, ring_shift(): lax.ppermute(value, 'ctx', [(order[i], order[(i + step) % n]) for i in ra...  104 us
    pallas_call x15, Pallas kernels, tn_blocks(): pl.pallas_call(functools.partial(tn_kernel, windows, outs), grid=(len(blo...  70 us
    ppermute x65, waiting for transfers between devices, swap_fsdp(): return lax.ppermute(value, 'fsdp', [(i, i ^ d) for i in range(4)])  69.2 us
    pallas_call x5, Pallas kernels, feed(): pl.pallas_call(functools.partial(feed_kernel, m, len(kept), crossed), gri...  65.3 us
    unnamed x261, local copies, waits for them, and re-layouts  50.7 us
    pallas_call x2, Pallas kernels, attention_backward(): pl.pallas_call(functools.partial(backward_kernel, n, group, ends, first),...  29.6 us
    ppermute x65, starting transfers between devices, swap_fsdp(): return lax.ppermute(value, 'fsdp', [(i, i ^ d) for i in range(4)])  25.5 us
  transfers between devices with their start and end apart: 140, of which 58 were waited for; matrix products, arithmetic and copies ran while one was open for 9% of the time, Pallas kernels for 31%

profile of v2, /device:TPU:0, one launch (start us, length us, event | category | flops | bytes accessed | tf_op | source)
XLA Modules:
  0.0 703.8 jit_solution(5885866097294409328)
XLA Ops:
  34.6 8.2 %collective-permute-done.6.refs_2_ = bf16[64,2048]{1,0:T(8,128)(2,1)} collective-permute-done((bf16[64,2048]{1,0:T(8,128)(2,1)S(1)}, bf16[64,2048]{1,0:T(8,128)(2,1)}, u32[]{:S(2)}, u32[]{:S(2)}) %collective-permute-start.6) | collective-permute-done | bytes 262176 | tf_op jit(solution)/shard_map/ppermute | solution.py:783
  65.1 8.1 %collective-permute-done.18.rest_2_ = bf16[160,1024]{1,0:T(8,128)(2,1)S(1)} collective-permute-done((bf16[160,1024]{1,0:T(8,128)(2,1)S(1)}, bf16[160,1024]{1,0:T(8,128)(2,1)S(1)}, u32[]{:S(2)}, u32[]{:S(2)}) %collective-permute-start.18) | collective-permute-done | bytes 327712 | tf_op jit(solution)/shard_map/ppermute | solution.py:783
  78.5 10.7 %collective-permute-done.22.refs_0_ = bf16[64,2048]{1,0:T(8,128)(2,1)S(1)} collective-permute-done((bf16[64,2048]{1,0:T(8,128)(2,1)S(1)}, bf16[64,2048]{1,0:T(8,128)(2,1)S(1)}, u32[]{:S(2)}, u32[]{:S(2)}) %collective-permute-start.22) | collective-permute-done | bytes 262176 | tf_op jit(solution)/shard_map/ppermute | solution.py:783
  122.9 18.7 %attention_forward.1 = (bf16[160,2048]{1,0:T(8,128)(2,1)S(1)}, f32[160,128]{1,0:T(8,128)S(1)}) custom-call(s32[31]{0:T(128)S(1)} %concatenate.144.f_ref.sc, bf16[160,2048]{1,0:T(8,128)(2,1)S(1)} %project.3.q_ref, bf16[160,1024]{1,0:T(8,128)(2,1)S(1)} %collective-permute-done.25.rest_0_, bf16[160,1024]{1,0:T(8,128)(2,1)S(1)} %collective-permute-done.20.rest_1_, ...), custom_call_target="tpu_custom_call" | custom-call | flops 180000000 | tf_op jit(solution)/shard_map/attention_forward/pallas_call | solution.py:131
  159.0 9.7 %collective-permute-done.38.refs_4_.refs_8_.refs_6_.refs_10_ = bf16[512,2048]{1,0:T(8,128)(2,1)} collective-permute-done((bf16[512,2048]{1,0:T(8,128)(2,1)S(1)}, bf16[512,2048]{1,0:T(8,128)(2,1)}, u32[]{:S(2)}, u32[]{:S(2)}) %collective-permute-start.38) | collective-permute-done | bytes 2097184 | tf_op jit(solution)/shard_map/ppermute | solution.py:745
  182.4 8.3 %collective-permute-done.43 = bf16[256,2048]{1,0:T(8,128)(2,1)S(1)} collective-permute-done((bf16[256,2048]{1,0:T(8,128)(2,1)S(1)}, bf16[256,2048]{1,0:T(8,128)(2,1)S(1)}, u32[]{:S(2)}, u32[]{:S(2)}) %collective-permute-start.43) | collective-permute-done | bytes 1048608 | tf_op jit(solution)/shard_map/ppermute | solution.py:745
  197.1 11.0 %feed.5 = (bf16[1280,2048]{1,0:T(8,128)(2,1)}, bf16[1280,2048]{1,0:T(8,128)(2,1)}, bf16[1280,1024]{1,0:T(8,128)(2,1)}, bf16[1280,2048]{1,0:T(8,128)(2,1)}, bf16[160,2048]{1,0:T(8,128)(2,1)S(1)}) custom-call(bf16[160,2048]{1,0:T(8,128)(2,1)S(1)} %get-tuple-element.548.refs_0_, bf16[160,2048]{1,0:T(8,128)(2,1)S(1)} %copy-done.47, ...), custom_call_target="tpu_custom_call" | custom-call | flops 120000000 | tf_op jit(solution)/shard_map/feed/pallas_call | solution.py:560
  211.2 14.4 %feed.6 = (bf16[1280,2048]{1,0:T(8,128)(2,1)}, bf16[1280,2048]{1,0:T(8,128)(2,1)}, bf16[1280,1024]{1,0:T(8,128)(2,1)}, bf16[1280,2048]{1,0:T(8,128)(2,1)}, bf16[320,2048]{1,0:T(8,128)(2,1)S(1)}) custom-call(bf16[160,2048]{1,0:T(8,128)(2,1)S(1)} %collective-permute-done.35.refs_0_, ...), custom_call_target="tpu_custom_call", output_to_operand_aliasing={{0}: (13, {}), {1}: (14, {}), {2}: (15, {}), {3}: (16, {})} | custom-call | flops 160000000 | tf_op jit(solution)/shard_map/feed/pallas_call | solution.py:560
  229.0 14.4 %feed.7 = (bf16[1280,2048]{1,0:T(8,128)(2,1)}, bf16[1280,2048]{1,0:T(8,128)(2,1)}, bf16[1280,1024]{1,0:T(8,128)(2,1)}, bf16[1280,2048]{1,0:T(8,128)(2,1)}, bf16[320,2048]{1,0:T(8,128)(2,1)S(1)}) custom-call(bf16[160,2048]{1,0:T(8,128)(2,1)S(1)} %collective-permute-done.47.refs_0_, ...), custom_call_target="tpu_custom_call", output_to_operand_aliasing={{0}: (13, {}), {1}: (14, {}), {2}: (15, {}), {3}: (16, {})} | custom-call | flops 160000000 | tf_op jit(solution)/shard_map/feed/pallas_call | solution.py:560
  246.5 14.5 %feed.8 = (bf16[1280,2048]{1,0:T(8,128)(2,1)}, bf16[1280,2048]{1,0:T(8,128)(2,1)}, bf16[1280,1024]{1,0:T(8,128)(2,1)}, bf16[1280,2048]{1,0:T(8,128)(2,1)}, bf16[320,2048]{1,0:T(8,128)(2,1)S(1)}) custom-call(bf16[160,2048]{1,0:T(8,128)(2,1)S(1)} %collective-permute-done.49.refs_0_, ...), custom_call_target="tpu_custom_call", output_to_operand_aliasing={{0}: (13, {}), {1}: (14, {}), {2}: (15, {}), {3}: (16, {})} | custom-call | flops 160000000 | tf_op jit(solution)/shard_map/feed/pallas_call | solution.py:560
  261.1 11.0 %feed.9 = (bf16[1280,2048]{1,0:T(8,128)(2,1)}, bf16[1280,2048]{1,0:T(8,128)(2,1)}, bf16[1280,1024]{1,0:T(8,128)(2,1)}, bf16[1280,2048]{1,0:T(8,128)(2,1)}, bf16[160,2048]{1,0:T(8,128)(2,1)S(1)}) custom-call(bf16[160,2048]{1,0:T(8,128)(2,1)S(1)} %pad_maximum_fusion.1.refs_0_, ...), custom_call_target="tpu_custom_call", output_to_operand_aliasing={{0}: (11, {}), {1}: (12, {}), {2}: (13, {}), {3}: (14, {})} | custom-call | flops 120000000 | tf_op jit(solution)/shard_map/feed/pallas_call | solution.py:560
  288.6 10.4 %tn_blocks.16 = (bf16[512,512]{1,0:T(8,128)(2,1)}, bf16[512,512]{1,0:T(8,128)(2,1)}, bf16[512,512]{1,0:T(8,128)(2,1)S(1)}, bf16[512,512]{1,0:T(8,128)(2,1)S(1)},...) custom-call(bf16[1280,2048]{1,0:T(8,128)(2,1)S(1)} %bitcast.23, ...), custom_call_target="tpu_custom_call" | custom-call | flops 100000000 | tf_op jit(solution)/shard_map/tn_blocks/pallas_call | solution.py:696
  305.5 14.2 %collective-permute-done.60 = bf16[160,2048]{1,0:T(8,128)(2,1)S(1)} collective-permute-done((bf16[160,2048]{1,0:T(8,128)(2,1)S(1)}, bf16[160,2048]{1,0:T(8,128)(2,1)S(1)}, u32[]{:S(2)}, u32[]{:S(2)}) %collective-permute-start.60) | collective-permute-done | bytes 655392 | tf_op jit(solution)/shard_map/ppermute | solution.py:783
  320.0 7.8 %collective-permute-done.65.refs_4_ = bf16[256,2048]{1,0:T(8,128)(2,1)S(1)} collective-permute-done((bf16[256,2048]{1,0:T(8,128)(2,1)S(1)}, bf16[256,2048]{1,0:T(8,128)(2,1)S(1)}, u32[]{:S(2)}, u32[]{:S(2)}) %collective-permute-start.65) | collective-permute-done | bytes 1048608 | tf_op jit(solution)/shard_map/ppermute | solution.py:745
  342.6 7.4 %down_rows.1 = bf16[1280,2048]{1,0:T(8,128)(2,1)S(1)} custom-call(s32[31]{0:T(128)S(1)} %concatenate.144.f_ref.sc, bf16[1280,1024]{1,0:T(8,128)(2,1)S(1)} %copy-done.9, bf16[1024,2048]{1,0:T(8,128)(2,1)S(1)} %copy-done.7), custom_call_target="tpu_custom_call" | custom-call | flops 120000000 | tf_op jit(solution)/shard_map/down_rows/pallas_call | solution.py:592
  391.3 14.8 %attention_backward.2 = (bf16[160,1024]{1,0:T(8,128)(2,1)}, bf16[1280,512]{1,0:T(8,128)(2,1)}) custom-call(s32[31]{0:T(128)} %copy-done.86, bf16[160,2048]{1,0:T(8,128)(2,1)} %copy-done.11, bf16[160,2048]{1,0:T(8,128)(2,1)} %copy-done.25, f32[160,128]{1,0:T(8,128)} %copy-done.83, f32[160,128]{1,0:T(8,128)} %copy-done.67, f32[160,128]{1,0:T(8,128)} %copy-done.23, ...), custom_call_target="tpu_custom_call" | custom-call | flops 260000000 | tf_op jit(solution)/shard_map/attention_backward/pallas_call | solution.py:236
  413.6 14.8 %attention_backward.3 = (bf16[160,1024]{1,0:T(8,128)(2,1)}, bf16[1280,512]{1,0:T(8,128)(2,1)}) custom-call(s32[31]{0:T(128)} %copy-done.86, bf16[160,2048]{1,0:T(8,128)(2,1)} %copy-done.11, bf16[160,2048]{1,0:T(8,128)(2,1)} %copy-done.25, f32[160,128]{1,0:T(8,128)} %copy-done.83, f32[160,128]{1,0:T(8,128)} %copy-done.67, f32[160,128]{1,0:T(8,128)} %copy-done.23, ...), custom_call_target="tpu_custom_call" | custom-call | flops 260000000 | tf_op jit(solution)/shard_map/attention_backward/pallas_call | solution.py:236
  442.1 14.5 %collective-permute-done.88.refs_4_ = bf16[512,1024]{1,0:T(8,128)(2,1)S(1)} collective-permute-done((bf16[512,1024]{1,0:T(8,128)(2,1)}, bf16[512,1024]{1,0:T(8,128)(2,1)S(1)}, u32[]{:S(2)}, u32[]{:S(2)}) %collective-permute-start.88) | collective-permute-done | bytes 1048608 | tf_op jit(solution)/shard_map/ppermute | solution.py:745
  463.3 7.5 %tn_blocks.23 = bf16[512,2048]{1,0:T(8,128)(2,1)S(1)} custom-call(bf16[1280,2048]{1,0:T(8,128)(2,1)S(1)} %copy-done, bf16[1280,2048]{1,0:T(8,128)(2,1)S(1)} %copy-done.2, bf16[512,512]{1,0:T(8,128)(2,1)S(1)} %collective-permute-done.84.refs_0_, bf16[512,512]{1,0:T(8,128)(2,1)} %collective-permute-done.85.refs_1_, ...), custom_call_target="tpu_custom_call" | custom-call | flops 50000000 | tf_op jit(solution)/shard_map/tn_blocks/pallas_call | solution.py:696
  484.9 8.9 %collective-permute-done.99 = bf16[160,1024]{1,0:T(8,128)(2,1)S(1)} collective-permute-done((bf16[160,1024]{1,0:T(8,128)(2,1)S(1)}, bf16[160,1024]{1,0:T(8,128)(2,1)S(1)}, u32[]{:S(2)}, u32[]{:S(2)}) %collective-permute-start.99) | collective-permute-done | bytes 327712 | tf_op jit(solution)/shard_map/ppermute | solution.py:783
  511.1 7.9 %collective-permute-done.102 = bf16[160,1024]{1,0:T(8,128)(2,1)} collective-permute-done((bf16[160,1024]{1,0:T(8,128)(2,1)}, bf16[160,1024]{1,0:T(8,128)(2,1)}, u32[]{:S(2)}, u32[]{:S(2)}) %collective-permute-start.102) | collective-permute-done | bytes 327712 | tf_op jit(solution)/shard_map/ppermute | solution.py:783
  534.0 13.0 %collective-permute-done.109 = bf16[64,1024]{1,0:T(8,128)(2,1)S(1)} collective-permute-done((bf16[64,1024]{1,0:T(8,128)(2,1)S(1)}, bf16[64,1024]{1,0:T(8,128)(2,1)S(1)}, u32[]{:S(2)}, u32[]{:S(2)}) %collective-permute-start.109) | collective-permute-done | bytes 131104 | tf_op jit(solution)/shard_map/ppermute | solution.py:783
  548.5 29.3 %collective-permute-start.112 = (bf16[64,2048]{1,0:T(8,128)(2,1)}, bf16[64,2048]{1,0:T(8,128)(2,1)}, u32[]{:S(2)}, u32[]{:S(2)}) collective-permute-start(bf16[64,2048]{1,0:T(8,128)(2,1)} %pad_maximum_fusion.8), channel_id=1, source_target_pairs={{0,2},{2,4},{4,6},{6,7},{7,5},{5,3},{3,1},{1,0},{8,10},{10,12},{12... | collective-permute-start | bytes 786440 | tf_op jit(solution)/shard_map/ppermute | solution.py:783
  648.9 9.2 %collective-permute-done.122.refs_2_ = bf16[512,1024]{1,0:T(8,128)(2,1)} collective-permute-done((bf16[512,1024]{1,0:T(8,128)(2,1)}, bf16[512,1024]{1,0:T(8,128)(2,1)}, u32[]{:S(2)}, u32[]{:S(2)}) %collective-permute-start.122) | collective-permute-done | bytes 1048608 | tf_op jit(solution)/shard_map/ppermute | solution.py:745
  (662 shorter events, 398.9 us)
Async XLA Ops:
  7.2 631.8 %reduce-scatter.2.cloned.1.call-start = ((), (), s32[]{:S(2)}) async-start(), calls=%async_computation.3 | async-start | bytes 5898240 | tf_op jit(solution)/shard_map/reduce_scatter | solution.py:1115
  14.7 29.2 %collective-permute-start.4 = (bf16[512,512]{1,0:T(8,128)(2,1)}, bf16[512,512]{1,0:T(8,128)(2,1)S(1)}, u32[]{:S(2)}, u32[]{:S(2)}) collective-permute-start(bf16[512,512]{1,0:T(8,128)(2,1)} %refs_6_), channel_id=1, source_target_pairs={{0,16},{8,24},{16,0},{24,8},{1,17},{9,25},{17,1},{25,9},{2,18},{10... | collective-permute-start | bytes 1572872 | tf_op jit(solution)/shard_map/ppermute | solution.py:745
  19.5 30.9 %collective-permute-start.13 = (bf16[160,2048]{1,0:T(8,128)(2,1)}, bf16[160,2048]{1,0:T(8,128)(2,1)}, u32[]{:S(2)}, u32[]{:S(2)}) collective-permute-start(bf16[160,2048]{1,0:T(8,128)(2,1)} %base_ref), channel_id=1, source_target_pairs={{0,2},{2,4},{4,6},{6,7},{7,5},{5,3},{3,1},{1,0},{8,10},{10,12},{12... | collective-permute-start | bytes 1966088 | tf_op jit(solution)/shard_map/ppermute | solution.py:783
  43.9 47.7 %collective-permute-start.9 = (bf16[512,2048]{1,0:T(8,128)(2,1)}, bf16[512,2048]{1,0:T(8,128)(2,1)}, u32[]{:S(2)}, u32[]{:S(2)}) collective-permute-start(bf16[512,2048]{1,0:T(8,128)(2,1)} %refs_1_.2), channel_id=1, source_target_pairs={{0,16},{8,24},{16,0},{24,8},{1,17},{9,25},{17,1},{25,9},{2,18},{10... | collective-permute-start | bytes 6291464 | tf_op jit(solution)/shard_map/ppermute | solution.py:745
  105.2 40.6 %collective-permute-start.31 = (bf16[512,2048]{1,0:T(8,128)(2,1)}, bf16[512,2048]{1,0:T(8,128)(2,1)}, u32[]{:S(2)}, u32[]{:S(2)}) collective-permute-start(bf16[512,2048]{1,0:T(8,128)(2,1)} %refs_1_.1), channel_id=1, source_target_pairs={{0,8},{8,0},{16,24},{24,16},{1,9},{9,1},{17,25},{25,17},{2,10},{10... | collective-permute-start | bytes 6291464 | tf_op jit(solution)/shard_map/ppermute | solution.py:745
  120.2 27.1 %collective-permute-start.32 = (bf16[512,2048]{1,0:T(8,128)(2,1)}, bf16[512,2048]{1,0:T(8,128)(2,1)}, u32[]{:S(2)}, u32[]{:S(2)}) collective-permute-start(bf16[512,2048]{1,0:T(8,128)(2,1)} %place_rows.1.w2.refs_3_), channel_id=1, source_target_pairs={{0,8},{8,0},{16,24},{24,16},{1,9},{9,1},{17,25},{25,17},{2,10},{10... | collective-permute-start | bytes 6291464 | tf_op jit(solution)/shard_map/ppermute | solution.py:745
  120.2 48.5 %collective-permute-start.38 = (bf16[512,2048]{1,0:T(8,128)(2,1)S(1)}, bf16[512,2048]{1,0:T(8,128)(2,1)}, u32[]{:S(2)}, u32[]{:S(2)}) collective-permute-start(bf16[512,2048]{1,0:T(8,128)(2,1)S(1)} %dynamic-slice_dynamic-update-slice_fusion.refs_2_.refs_6_.refs_4_.refs_8_), channel_id=1, source_target_pairs={{0,16},{8,24},{16,0},{24,8},{1,17},{9,25},{17,1},{25,9},{2,18},{10... | collective-permute-start | bytes 6291464 | tf_op jit(solution)/shard_map/ppermute | solution.py:745
  145.7 45.0 %collective-permute-start.43 = (bf16[256,2048]{1,0:T(8,128)(2,1)S(1)}, bf16[256,2048]{1,0:T(8,128)(2,1)S(1)}, u32[]{:S(2)}, u32[]{:S(2)}) collective-permute-start(bf16[256,2048]{1,0:T(8,128)(2,1)S(1)} %constant_dynamic-slice_fusion.6), channel_id=1, source_target_pairs={{0,16},{8,24},{16,0},{24,8},{1,17},{9,25},{17,1},{25,9},{2,18},{10... | collective-permute-start | bytes 3145736 | tf_op jit(solution)/shard_map/ppermute | solution.py:745
  147.3 48.4 %collective-permute-start.37 = (bf16[512,2048]{1,0:T(8,128)(2,1)S(1)}, bf16[512,2048]{1,0:T(8,128)(2,1)S(1)}, u32[]{:S(2)}, u32[]{:S(2)}) collective-permute-start(bf16[512,2048]{1,0:T(8,128)(2,1)S(1)} %dynamic-slice_dynamic-update-slice_fusion.refs_2_.refs_6_.refs_4_.refs_8_), channel_id=1, source_target_pairs={{0,8},{8,0},{16,24},{24,16},{1,9},{9,1},{17,25},{25,17},{2,10},{10... | collective-permute-start | bytes 6291464 | tf_op jit(solution)/shard_map/ppermute | solution.py:745
  352.4 29.7 %collective-permute-start.68 = (bf16[512,1024]{1,0:T(8,128)(2,1)}, bf16[512,1024]{1,0:T(8,128)(2,1)S(1)}, u32[]{:S(2)}, u32[]{:S(2)}) collective-permute-start(bf16[512,1024]{1,0:T(8,128)(2,1)} %copy-done.94), channel_id=1, source_target_pairs={{0,16},{8,24},{16,0},{24,8},{1,17},{9,25},{17,1},{25,9},{2,18},{10... | collective-permute-start | bytes 3145736 | tf_op jit(solution)/shard_map/ppermute | solution.py:745
  383.1 30.5 %collective-permute-start.75 = (bf16[512,1024]{1,0:T(8,128)(2,1)S(1)}, bf16[512,1024]{1,0:T(8,128)(2,1)S(1)}, u32[]{:S(2)}, u32[]{:S(2)}) collective-permute-start(bf16[512,1024]{1,0:T(8,128)(2,1)S(1)} %copy-done.92), channel_id=1, source_target_pairs={{0,16},{8,24},{16,0},{24,8},{1,17},{9,25},{17,1},{25,9},{2,18},{10... | collective-permute-start | bytes 3145736 | tf_op jit(solution)/shard_map/ppermute | solution.py:745
  408.4 31.6 %collective-permute-start.84 = (bf16[512,512]{1,0:T(8,128)(2,1)}, bf16[512,512]{1,0:T(8,128)(2,1)S(1)}, u32[]{:S(2)}, u32[]{:S(2)}) collective-permute-start(bf16[512,512]{1,0:T(8,128)(2,1)} %get-tuple-element.640), channel_id=1, source_target_pairs={{0,8},{8,0},{16,24},{24,16},{1,9},{9,1},{17,25},{25,17},{2,10},{10... | collective-permute-start | bytes 1572872 | tf_op jit(solution)/shard_map/ppermute | solution.py:745
  408.4 32.0 %collective-permute-start.85 = (bf16[512,512]{1,0:T(8,128)(2,1)}, bf16[512,512]{1,0:T(8,128)(2,1)}, u32[]{:S(2)}, u32[]{:S(2)}) collective-permute-start(bf16[512,512]{1,0:T(8,128)(2,1)} %get-tuple-element.641), channel_id=1, source_target_pairs={{0,8},{8,0},{16,24},{24,16},{1,9},{9,1},{17,25},{25,17},{2,10},{10... | collective-permute-start | bytes 1572872 | tf_op jit(solution)/shard_map/ppermute | solution.py:745
  408.9 28.1 %collective-permute-start.89 = (bf16[160,512]{1,0:T(8,128)(2,1)}, bf16[160,512]{1,0:T(8,128)(2,1)}, u32[]{:S(2)}, u32[]{:S(2)}) collective-permute-start(bf16[160,512]{1,0:T(8,128)(2,1)} %get-tuple-element.953), channel_id=1, source_target_pairs={{0,2},{2,4},{4,6},{6,7},{7,5},{5,3},{3,1},{1,0},{8,10},{10,12},{12... | collective-permute-start | bytes 491528 | tf_op jit(solution)/shard_map/ppermute | solution.py:783
  440.0 30.8 %collective-permute-start.96 = (bf16[160,1024]{1,0:T(8,128)(2,1)S(1)}, bf16[160,1024]{1,0:T(8,128)(2,1)S(1)}, u32[]{:S(2)}, u32[]{:S(2)}) collective-permute-start(bf16[160,1024]{1,0:T(8,128)(2,1)S(1)} %pad_maximum_fusion.6), channel_id=1, source_target_pairs={{0,1},{2,0},{4,2},{6,4},{7,6},{5,7},{3,5},{1,3},{8,9},{10,8},{12,1... | collective-permute-start | bytes 983048 | tf_op jit(solution)/shard_map/ppermute | solution.py:783
  440.5 30.4 %collective-permute-start.95 = (bf16[160,1024]{1,0:T(8,128)(2,1)S(1)}, bf16[160,1024]{1,0:T(8,128)(2,1)S(1)}, u32[]{:S(2)}, u32[]{:S(2)}) collective-permute-start(bf16[160,1024]{1,0:T(8,128)(2,1)S(1)} %pad_maximum_fusion.5), channel_id=1, source_target_pairs={{0,2},{2,4},{4,6},{6,7},{7,5},{5,3},{3,1},{1,0},{8,10},{10,12},{12... | collective-permute-start | bytes 983048 | tf_op jit(solution)/shard_map/ppermute | solution.py:783
  442.1 29.7 %collective-permute-start.91 = (bf16[512,512]{1,0:T(8,128)(2,1)S(1)}, bf16[512,512]{1,0:T(8,128)(2,1)S(1)}, u32[]{:S(2)}, u32[]{:S(2)}) collective-permute-start(bf16[512,512]{1,0:T(8,128)(2,1)S(1)} %get-tuple-element.768), channel_id=1, source_target_pairs={{0,8},{8,0},{16,24},{24,16},{1,9},{9,1},{17,25},{25,17},{2,10},{10... | collective-permute-start | bytes 1572872 | tf_op jit(solution)/shard_map/ppermute | solution.py:745
  474.2 29.4 %collective-permute-start.104 = (bf16[512,512]{1,0:T(8,128)(2,1)}, bf16[512,512]{1,0:T(8,128)(2,1)}, u32[]{:S(2)}, u32[]{:S(2)}) collective-permute-start(bf16[512,512]{1,0:T(8,128)(2,1)} %get-tuple-element.708), channel_id=1, source_target_pairs={{0,8},{8,0},{16,24},{24,16},{1,9},{9,1},{17,25},{25,17},{2,10},{10... | collective-permute-start | bytes 1572872 | tf_op jit(solution)/shard_map/ppermute | solution.py:745
  499.1 115.2 %all-to-all-start = ((bf16[8,64,2048]{2,1,0:T(8,128)(2,1)}), bf16[8,64,2048]{2,1,0:T(8,128)(2,1)}, u32[]{:S(2)}, u32[]{:S(2)}) async-start(bf16[8,64,2048]{2,1,0:T(8,128)(2,1)} %bitcast.24), calls=%async_computation.1 | async-start | bytes 4194304 | tf_op jit(solution)/shard_map/all_to_all | solution.py:1155
  528.6 49.2 %collective-permute-start.107 = (bf16[512,512]{1,0:T(8,128)(2,1)}, bf16[512,512]{1,0:T(8,128)(2,1)S(1)}, u32[]{:S(2)}, u32[]{:S(2)}) collective-permute-start(bf16[512,512]{1,0:T(8,128)(2,1)} %get-tuple-element.827), channel_id=1, source_target_pairs={{0,8},{8,0},{16,24},{24,16},{1,9},{9,1},{17,25},{25,17},{2,10},{10... | collective-permute-start | bytes 1572872 | tf_op jit(solution)/shard_map/ppermute | solution.py:745
  528.6 49.2 %collective-permute-start.108 = (bf16[512,512]{1,0:T(8,128)(2,1)S(1)}, bf16[512,512]{1,0:T(8,128)(2,1)S(1)}, u32[]{:S(2)}, u32[]{:S(2)}) collective-permute-start(bf16[512,512]{1,0:T(8,128)(2,1)S(1)} %get-tuple-element.828), channel_id=1, source_target_pairs={{0,8},{8,0},{16,24},{24,16},{1,9},{9,1},{17,25},{25,17},{2,10},{10... | collective-permute-start | bytes 1572872 | tf_op jit(solution)/shard_map/ppermute | solution.py:745
  529.1 50.5 %collective-permute-start.100 = (bf16[512,1024]{1,0:T(8,128)(2,1)}, bf16[512,1024]{1,0:T(8,128)(2,1)}, u32[]{:S(2)}, u32[]{:S(2)}) collective-permute-start(bf16[512,1024]{1,0:T(8,128)(2,1)} %get-tuple-element.810), channel_id=1, source_target_pairs={{0,16},{8,24},{16,0},{24,8},{1,17},{9,25},{17,1},{25,9},{2,18},{10... | collective-permute-start | bytes 3145736 | tf_op jit(solution)/shard_map/ppermute | solution.py:745
  547.8 38.1 %collective-permute-start.113 = (bf16[64,2048]{1,0:T(8,128)(2,1)}, bf16[64,2048]{1,0:T(8,128)(2,1)}, u32[]{:S(2)}, u32[]{:S(2)}) collective-permute-start(bf16[64,2048]{1,0:T(8,128)(2,1)} %pad_maximum_fusion.9), channel_id=1, source_target_pairs={{0,1},{2,0},{4,2},{6,4},{7,6},{5,7},{3,5},{1,3},{8,9},{10,8},{12,1... | collective-permute-start | bytes 786440 | tf_op jit(solution)/shard_map/ppermute | solution.py:783
  548.5 37.4 %collective-permute-start.112 = (bf16[64,2048]{1,0:T(8,128)(2,1)}, bf16[64,2048]{1,0:T(8,128)(2,1)}, u32[]{:S(2)}, u32[]{:S(2)}) collective-permute-start(bf16[64,2048]{1,0:T(8,128)(2,1)} %pad_maximum_fusion.8), channel_id=1, source_target_pairs={{0,2},{2,4},{4,6},{6,7},{7,5},{5,3},{3,1},{1,0},{8,10},{10,12},{12... | collective-permute-start | bytes 786440 | tf_op jit(solution)/shard_map/ppermute | solution.py:783
  (240 other events, 3466.8 us)
Sparse Core Ops, SparseCore 0:
  431.8 143.9 reduce-scatter.1

commit v3 on v2

--- a/solution.py
+++ b/solution.py
@@ -464,7 +464,7 @@
         + [whole] * len(extra),
         out_specs=whole,
         out_shape=jax.ShapeDtypeStruct((count, 4 * size), kind),
-        compiler_params=params(40),
+        compiler_params=params(40 if len(rows) == 1 else 60),
         cost_estimate=cost(micros),
         name="back_project",
     )(*rows, *[w for ws in weights for w in ws], *extra)
@@ -534,7 +534,7 @@
     return (2 * units if crossed else 4 * units), crossed
 
 
-def feed(hidden, grads, gate_up, down, slot, kept, n):
+def feed(hidden, grads, gate, up, down, slot, kept, n):
     m = len(hidden)
     count, depth = hidden[0].shape
     width = down.shape[0]
@@ -543,9 +543,9 @@
     rows = m * count
     size = depth // 4
 
-    def shard(d, part):
+    def shard(d):
         flip = d >> 1 if crossed else 0
-        return pl.BlockSpec((size, tile), lambda e: (0, part * steps + (e ^ flip)))
+        return pl.BlockSpec((size, tile), lambda e: (0, e ^ flip))
 
     chunk = pl.BlockSpec((count, depth), lambda e: (0, 0))
     block = pl.BlockSpec((rows, depth), lambda e: (slot, 0))
@@ -561,8 +561,7 @@
         functools.partial(feed_kernel, m, len(kept), crossed),
         grid=(steps,),
         in_specs=[chunk] * (2 * m)
-        + [shard(d, 0) for d in range(4)]
-        + [shard(d, 1) for d in range(4)]
+        + [shard(d) for d in range(4)] * 2
         + [pl.BlockSpec((tile, depth), lambda e: (e, 0))]
         + [pl.BlockSpec(memory_space=pl.ANY)] * len(kept),
         out_specs=[
@@ -578,7 +577,7 @@
         compiler_params=params(48),
         cost_estimate=cost(8 + 4 * m),
         name="feed",
-    )(*hidden, *grads, *gate_up, *gate_up, down, *kept)
+    )(*hidden, *grads, *gate, *up, down, *kept)
     return kept, [dh[i * count : (i + 1) * count] for i in range(m)]
 
 
@@ -665,7 +664,7 @@
                 (((0,), (0,)), ((), ())),
                 preferred_element_type=F32,
             )
-            for array, part, parts, _ in adds:
+            for array, part, parts, _, _ in adds:
                 at = part * (width // parts)
                 total = total.at[:, at : at + width // parts].add(array.astype(F32))
             result.append(jnp.split(total.astype(kind), pieces, axis=1))
@@ -677,8 +676,10 @@
         count = max(1, steps // parts)
         return part * count, (part + 1) * count
 
-    def added_spec(part, parts):
+    def added_spec(part, parts, flip):
         low, high = window(part, parts)
+        if parts == 1:
+            return pl.BlockSpec((size, tile), lambda i, j: (0, j ^ flip))
         return pl.BlockSpec((size, tile), lambda i, j: (0, jnp.clip(j - low, 0, high - low - 1)))
 
     def out_spec(row, low, high):
@@ -690,7 +691,7 @@
 
     windows = [
         (*(window(part, parts) if parts > 1 and steps > 1 else (None, None)), crossed)
-        for _, part, parts, crossed in adds
+        for _, part, parts, _, crossed in adds
     ]
     outs = [(row, *window(piece, pieces)) for row in range(len(blocks)) for piece in range(pieces)]
     result = pl.pallas_call(
@@ -700,7 +701,7 @@
             pl.BlockSpec((rows, size), lambda i, j: (0, first + stride * i)),
             pl.BlockSpec((rows, tile), lambda i, j: (0, j)),
         ]
-        + [added_spec(part, parts) for _, part, parts, _ in adds],
+        + [added_spec(part, parts, flip) for _, part, parts, flip, _ in adds],
         out_specs=[out_spec(*out) for out in outs],
         out_shape=[jax.ShapeDtypeStruct((size, width // pieces), kind)] * len(outs),
         scratch_shapes=[pltpu.VMEM((size, rows), BF)],
@@ -711,34 +712,31 @@
     return [list(result[row * pieces : (row + 1) * pieces]) for row in range(len(blocks))]
 
 
-def spread_kernel(n, units, f_ref, *refs):
-    arrays, outs = refs[:-2], refs[-2:]
-    tile = arrays[0].shape[2] // 2
+def spread_kernel(units, tile, f_ref, all_ref, *outs):
     span = outs[0].shape[1] // 4
     c = pl.program_id(0)
-    e = 0
-    for array in arrays:
-        for at in range(0, tile, units):
-            start = (f_ref[0] ^ e) * span + c * units
-            e += 1
-            for part in range(2):
-                value = array[0, :, part * tile + at : part * tile + at + units].astype(F32)
-                outs[part][:, pl.ds(pl.multiple_of(start, units), units)] = value
-
-
-def spread(scalars, arrays, units):
-    n, rows, _ = arrays[0].shape
+    for e in range(4):
+        step, at = divmod(e * units, tile)
+        start = (f_ref[0] ^ e) * span + c * units
+        for part in range(2):
+            low = (2 * step + part) * tile + at
+            value = all_ref[0, :, low : low + units].astype(F32)
+            outs[part][:, pl.ds(pl.multiple_of(start, units), units)] = value
+
+
+def spread(scalars, gathered, units, tile):
+    n, rows, _ = gathered.shape
     width = 4 * n * units
     return pl.pallas_call(
-        functools.partial(spread_kernel, n, units),
+        functools.partial(spread_kernel, units, tile),
         grid=(n,),
-        in_specs=[smem()] + [pl.BlockSpec((1, *a.shape[1:]), lambda i: (i, 0, 0)) for a in arrays],
+        in_specs=[smem(), pl.BlockSpec((1, *gathered.shape[1:]), lambda i: (i, 0, 0))],
         out_specs=[pl.BlockSpec((rows, width), lambda i: (0, 0))] * 2,
         out_shape=[jax.ShapeDtypeStruct((rows, width), F32)] * 2,
         compiler_params=params(32),
         cost_estimate=cost(4),
         name="spread",
-    )(scalars, *arrays)
+    )(scalars, gathered)
 
 
 def swap_fsdp(value, d):
@@ -809,6 +807,8 @@
         self.width = own.shape[1] // 2
 
     def send(self):
+        if self.step == self.half:
+            return
         self.step += 1
         right, left = self.now
         if self.step == self.half:
@@ -816,6 +816,8 @@
         self.now = (ring_shift(right, 1, self.n), ring_shift(left, -1, self.n))
 
     def take(self):
+        if self.half in self.chunks:
+            return
         self.now = right, left = self.order.take(self.now)
         if self.step == self.half:
             self.chunks[self.half] = jnp.concatenate([right, left], axis=1)
@@ -856,7 +858,7 @@
             behind = jnp.concatenate([behind[:, :width], behind[:, width:] + got[1]], axis=1)
         else:
             ahead, behind = ahead + got[0], behind + got[1]
-        self.now = (ahead.astype(BF), behind.astype(BF))
+        self.now = self.order.done((ahead.astype(BF), behind.astype(BF)))
 
     def rest(self, hops=None):
         while self.step < self.half and hops != 0:
@@ -931,7 +933,8 @@
     key_blocks = jnp.take(block_order.reshape(n, 2), owners, axis=0).reshape(-1)
     seq_ends = jnp.cumsum(lengths[0])
     count = lengths.shape[1]
-    slot_rel = [r for step in range(1, half) for r in (-step, step)] + [0, half]
+    groups = [(-1, 0, 1)] + [(-step, step) for step in range(2, half)] + [(half,)]
+    slot_rel = [r for group in (groups[0], groups[-1], *groups[1:-1]) for r in group]
     slot_owners = ring_index(place + jnp.asarray(slot_rel, jnp.int32), n)
     scalars = jnp.concatenate([f[None], own_blocks, key_blocks, seq_ends, slot_owners])
     scalars = scalars.astype(jnp.int32)
@@ -943,10 +946,13 @@
     width = 4 * units
 
     def own_units(weight):
-        return [
-            lax.dynamic_slice_in_dim(weight, (f ^ e) * span + c * units, units, 1)
-            for e in range(4)
-        ]
+        return jnp.concatenate(
+            [
+                lax.dynamic_slice_in_dim(weight, (f ^ e) * span + c * units, units, 1)
+                for e in range(4)
+            ],
+            axis=1,
+        )
 
     gains = gather_fsdp(jnp.stack([first_gain, second_gain]))
     gains = jnp.concatenate(gains, axis=1).astype(F32)
@@ -958,101 +964,86 @@
     grad_out.send()
     key_core, value_core = swap_fsdp(key_matrix, 1), swap_fsdp(value_matrix, 1)
     out_core, query_core = swap_fsdp(out_weight, 1), swap_fsdp(query_weight, 1)
-    down_own = lax.dynamic_slice_in_dim(down_weight, c * units, units, 0)
-    down_core = swap_fsdp(down_own, 1)
+    def across(value):
+        return swap_fsdp(order.at(value), 2)
+
+    def shards(own, core, over):
+        return [own, core, over, swap_fsdp(over, 1)]
 
     hidden_one = order.run(norm_rows, scalars, tokens, gain_one)
     out_across = order.take(out_across)
     out_parts = Gather(order, out_across, n)
     out_parts.send()
-    key_across = order.take(key_across)
-    key_far = swap_fsdp(key_across, 1)
+    weight_k = shards(key_matrix, key_core, order.take(key_across))
     out_parts.rest(1)
-    value_across = order.take(value_across)
-    value_far = swap_fsdp(value_across, 1)
-    query_across = swap_fsdp(order.at(query_weight), 2)
-    gate_up_own = order.done(
-        jnp.concatenate(own_units(order.at(gate_weight)) + own_units(up_weight), axis=1)
-    )
-    gate_up_core = swap_fsdp(gate_up_own, 1)
+    weight_v = shards(value_matrix, value_core, order.take(value_across))
+    query_across = across(query_weight)
+    gate_own = order.run(own_units, gate_weight)
+    up_own = order.run(own_units, up_weight)
+    gate_core, up_core = swap_fsdp(gate_own, 1), swap_fsdp(up_own, 1)
+    down_own = order.done(lax.dynamic_slice_in_dim(order.at(down_weight), c * units, units, 0))
+    down_core = swap_fsdp(down_own, 1)
     out_parts.rest(1)
     grad_out.take()
-    key_far, value_far = order.take((key_far, value_far))
-    weight_k = [key_matrix, key_core, key_across, key_far]
-    weight_v = [value_matrix, value_core, value_across, value_far]
     kv_own = order.run(project, hidden_one, cosine, sine, [weight_k, weight_v], turned_tiles=1, scale=1.0, micros=4)
     kv = Gather(order, kv_own, n)
     kv.send()
     kv.rest(1)
+    kv.rest(1)
     out_parts.take()
-    kv.rest(1)
-    query_across = order.take(query_across)
-    query_far = swap_fsdp(query_across, 1)
-    gate_up_across = swap_fsdp(order.at(gate_up_own), 2)
-    down_across = swap_fsdp(order.at(after(down_own, query_across)), 2)
+    weight_q = shards(query_weight, query_core, order.take(query_across))
+    gate_across = across(gate_own)
     kv.rest()
     kv.take()
+    out_parts.send()
     kv_chunks = [kv.chunks[r] for r in rel]
-    out_parts.send()
-    query_far = order.take(query_far)
-    weight_q = [query_weight, query_core, query_across, query_far]
 
     queries = order.run(project, hidden_one, cosine, sine, [weight_q], turned_tiles=2, scale=0.125, micros=7)
     out_parts.rest()
     out_parts.take()
+    gate = shards(gate_own, gate_core, order.take(gate_across))
+    up_across = across(up_own)
+    grad_out.send()
     out_across = order.run(place_rows, owners.astype(jnp.int32), [out_parts.chunks[r] for r in rel])
-    out_far = swap_fsdp(out_across, 1)
-    grad_out.send()
+    weight_o = shards(out_weight, out_core, out_across)
     mixed, lse = order.run(attention_forward, scalars, queries, kv_chunks, ends=count)
-    grad_out.rest(1)
-    weight_o = [out_weight, out_core, out_across, out_far]
+    up = shards(up_own, up_core, order.take(up_across))
+    down_across = across(down_own)
+    grad_out.take()
     residual, hidden_two = order.run(out_project, scalars, mixed, tokens, gain_two, weight_o)
-    grad_out.rest()
     hidden = Gather(order, hidden_two, n)
     hidden.send()
-    gate_up_across = order.take(gate_up_across)
-    gate_up_far = swap_fsdp(gate_up_across, 1)
-    grad_out.take()
-    down_across = order.take(down_across)
-    down_far = swap_fsdp(down_across, 1)
-    gate_up = [gate_up_own, gate_up_core, gate_up_across, gate_up_far]
+    hidden.rest(1)
+    grad_out.send()
+    down = shards(down_own, down_core, order.take(down_across))
     if units < 128:
-        gate_up = [swap_cols(part, d, 2) for d, part in enumerate(gate_up)]
-    down = jnp.concatenate([down_own, down_core, down_across, down_far], axis=0)
+        gate = [swap_cols(part, d, 1) for d, part in enumerate(gate)]
+        up = [swap_cols(part, d, 1) for d, part in enumerate(up)]
+    down = order.done(jnp.concatenate(down, axis=0))
 
     kept, grads_two = [], {}
-    for near in range(half + 1):
-        group = (0,) if near == 0 else (half,) if near == half else (-near, near)
-        slot = n - 2 if near == 0 else n - 1 if near == half else near - 1
+    for at, group in enumerate(groups):
+        slot = slot_rel.index(group[0]) // len(group)
         kept, parts = order.run(
             feed,
             [hidden.chunks[r] for r in group],
             [grad_out.chunks[r] for r in group],
-            gate_up,
+            gate,
+            up,
             down,
             slot=slot,
             kept=kept,
             n=n,
         )
         grads_two.update(zip(group, parts))
-        if near < half:
+        if at < half - 1:
             hidden.take()
-        if near < half - 1:
             hidden.send()
+            grad_out.take()
+            grad_out.send()
 
     rows_h, rows_dy, act, grads = kept
     tile, crossed = feed_tile(units)
-    waiting, under_way = [], []
-
-    def tick():
-        while under_way:
-            mid, h = under_way.pop()
-            mid[h] = order.take(mid[h])
-        if waiting:
-            mid, h = waiting.pop(0)
-            mid[h] = swap_fsdp(order.at(mid[h]), 2)
-            under_way.append((mid, h))
-
     class Product:
         def __init__(self, left, right, micros, by_units=False):
             self.left, self.right, self.micros, self.by_units = left, right, micros, by_units
@@ -1070,23 +1061,25 @@
 
         def first(self):
             self.near = [
-                [swap_fsdp(piece, 1) for piece in row] for row in self.kernel((1, 3), BF, (), 4)
+                [swap_fsdp(piece, 1) for piece in row] for row in self.kernel((1, 3), BF, (), 2)
             ]
 
         def pieces(self, row):
             turned = self.by_units and crossed
             got = [self.from_partner(v, 1) for v in order.take(self.near[row])]
-            return [(v, p, len(got), turned) for p, v in enumerate(got)]
-
-        def second(self, halves=2):
-            (self.mid,) = self.kernel((2,), BF, self.pieces(1), halves)
-            waiting.extend((self.mid, h) for h in range(len(self.mid)))
+            return [(v, p, len(got), 0, turned) for p, v in enumerate(got)]
+
+        def second(self, halves=1):
+            (mid,) = self.kernel((2,), BF, self.pieces(1), halves)
+            self.mid = [swap_fsdp(v, 2) for v in mid]
+
+        def settle(self):
+            self.mid = order.take(self.mid)
 
         def last(self, kind):
-            over = [self.from_partner(v, 2) for v in self.mid]
-            if self.by_units and crossed:
-                over = over[::-1]
-            adds = [(v, h, len(over), False) for h, v in enumerate(over)]
+            over = [self.from_partner(v, 2) for v in order.at(self.mid)]
+            flip = 2 if self.by_units and crossed else 0
+            adds = [(v, h, len(over), flip, False) for h, v in enumerate(over)]
             ((whole,),) = self.kernel((0,), kind, self.pieces(0) + adds)
             return whole
 
@@ -1094,25 +1087,26 @@
     sums.send()
     of_down = Product(act, rows_dy, 3)
     of_gate_up = Product(rows_h, grads, 5, True)
+    of_gate_up.first()
+    sums.rest(1)
     of_down.first()
+    of_gate_up.second()
     sums.rest(1)
-    of_gate_up.first()
-    of_down.second(1)
-    tick()
+    y_rows = order.run(down_rows, scalars, act, down, n=n)
+    of_down.second()
     sums.rest(1)
-    of_gate_up.second()
-    y_rows = order.run(down_rows, scalars, act, down, n=n)
-    sums.rest(1)
-    tick()
-    down_grad = of_down.last(F32)
     sums.rest()
     grad_hidden_two = sums.take()
     grad_residual, gain_two_term, grad_branch = order.run(
         norm_back, scalars, residual, gain_two, cotangent, grad_hidden_two, rounded=True
     )
     grad_mixed = order.run(back_project, [grad_branch], [weight_o], kind=BF, micros=5)
-    tick()
-    y_own = lax.psum_scatter(order.at(y_rows), "ctx", scatter_dimension=0, tiled=True)
+    of_gate_up.settle()
+    gate_up_grad = of_gate_up.last(BF)
+    rows = gate_up_grad.shape[0] // n
+    gate_up_all = lax.all_to_all(
+        gate_up_grad.reshape(n, rows, 2 * width), "ctx", 0, 0, tiled=False
+    )
     of_out = Product(mixed, grad_branch, 2)
     of_out.first()
 
@@ -1135,92 +1129,85 @@
         )
 
     attention_part(0)
+    of_down.settle()
     of_out.second()
-    tick()
     attention_part(2)
+    gate_up_all = order.take(gate_up_all)
     grad_query = jnp.concatenate([p[0] for p in parts], axis=1)
 
     def kv_contrib(r):
         start = rel.index(r) * token_rows
         return jnp.concatenate([p[1][start : start + token_rows] for p in parts], axis=1)
+
+    def scatter_rows(within):
+        rows = within.shape[0] // n
+
+        def contrib(r):
+            start = ring_index(place + r, n) * rows
+            return lax.dynamic_slice_in_dim(within, start, rows, 0)
+
+        return Scatter(order, contrib, n)
 
     grad_kv = Scatter(order, kv_contrib, n)
     grad_kv.send()
     of_query = Product(hidden_one, grad_query, 2)
     of_query.first()
     grad_kv.rest(1)
-    tick()
-    gate_up_grad = of_gate_up.last(BF)
-    rows = gate_up_grad.shape[0] // n
-    gate_up_all = lax.all_to_all(
-        gate_up_grad.reshape(n, rows, 2 * width), "ctx", 0, 0, tiled=False
-    )
+    grad_hidden_one = order.run(back_project, [grad_query], [weight_q], kind=F32, micros=5)
+    of_out.settle()
     grad_kv.rest(1)
     of_query.second()
-    grad_hidden_one = order.run(back_project, [grad_query], [weight_q], kind=F32, micros=5)
     grad_kv.rest(1)
-    tick()
-
-    def scatter_rows(within):
-        rows = within.shape[0] // n
-
-        def contrib(r):
-            start = ring_index(place + r, n) * rows
-            return lax.dynamic_slice_in_dim(within, start, rows, 0)
-
-        return Scatter(order, contrib, n)
-
-    out_sums = scatter_rows(of_out.last(BF))
+    out_within = of_out.last(BF)
     grad_kv.rest()
     grad_kv = added(grad_kv.take())
+    y_own = lax.psum_scatter(order.at(y_rows), "ctx", scatter_dimension=0, tiled=True)
+    out_sums = scatter_rows(out_within)
     out_sums.send()
     grad_kv = turn_back(grad_kv, cosine, sine).astype(BF)
     grad_key, grad_value = deinterleave(grad_kv)
     grad_kv = jnp.concatenate([grad_key, grad_value], axis=1)
     of_kv = Product(hidden_one, grad_kv, 1.5)
     of_kv.first()
+    out_sums.rest(1)
     grad_hidden_one = order.run(
         back_project, [grad_key, grad_value], [weight_k, weight_v], base=grad_hidden_one, kind=F32, micros=3
     )
     out_sums.rest(1)
-    of_kv.second(1)
-    tick()
     tokens_grad, gain_one_term = order.run(
         norm_back, scalars, tokens, gain_one, grad_residual, [grad_hidden_one], rounded=False
     )
     out_sums.rest(1)
     gain_terms = xor_blocks(jnp.concatenate([gain_one_term, gain_two_term], axis=0), f, 1)
     gain_terms = gain_terms.astype(BF).reshape(2, 4 * n, model // (4 * n)).transpose(1, 0, 2)
-    gain_terms = lax.all_to_all(order.at(gain_terms), ("fsdp", "ctx"), 0, 0, tiled=False)
+    gain_terms = lax.all_to_all(gain_terms, ("fsdp", "ctx"), 0, 0, tiled=False)
+    of_query.settle()
+    of_kv.second()
+    query_sums = scatter_rows(of_query.last(BF))
+    query_sums.send()
     out_sums.rest()
     out_grad = order.done(added(out_sums.take()))
-    tick()
-    gate_up_all = order.take(gate_up_all)
+    query_sums.rest(1)
     if crossed:
-        gate_up_all = gate_up_all.reshape(n, rows, width // tile, 2 * tile)
-        gate_grad, up_grad = order.run(
-            spread, scalars, [gate_up_all[:, :, s] for s in range(width // tile)], units=units
-        )
+        gate_grad, up_grad = order.run(spread, scalars, gate_up_all, units=units, tile=tile)
     else:
         gate_up_all = gate_up_all.reshape(n, rows, 2, 4, units).transpose(2, 1, 3, 0, 4)
         gate_up_all = xor_blocks(gate_up_all, f, 2).reshape(2, rows, n * width).astype(F32)
         gate_grad, up_grad = order.done((gate_up_all[0], gate_up_all[1]))
-    query_sums = scatter_rows(of_query.last(BF))
-    query_sums.send()
-    query_sums.rest(1)
-    layer_out = order.done((residual + order.at(y_own).astype(F32)).astype(BF))
-    query_sums.rest(1)
-    tick()
+    gain_terms = order.take(gain_terms)
+    of_kv.settle()
     kv_sums = scatter_rows(of_kv.last(BF))
     kv_sums.send()
     query_sums.rest(1)
+    down_grad = of_down.last(F32)
     kv_sums.rest(1)
     query_sums.rest()
     kv_sums.rest(1)
     query_grad = order.done(added(query_sums.take()))
     kv_sums.rest()
-    gain_grads = jnp.sum(order.at(gain_terms).astype(F32), axis=0)
-    kv_grad = added(kv_sums.take())
+    layer_out = order.done((residual + order.at(y_own).astype(F32)).astype(BF))
+    kv_grad = order.done(added(kv_sums.take()))
+    gain_grads = jnp.sum(gain_terms.astype(F32), axis=0)
     kv_width = key_matrix.shape[1]
     key_grad, value_grad = kv_grad[:, :kv_width], kv_grad[:, kv_width:]
     return (

time: 714 us -> 621 us (0.87)
  waiting for transfers between devices: 208 us -> 142 us
  starting transfers between devices: 139 us -> 116 us
  Pallas kernels: 230 us -> 222 us
    ppermute x65 -> x49, waiting for transfers between devices: 69.2 us -> 17.5 us  [swap_fsdp(): return lax.ppermute(value, 'fsdp', [(i, i ^ d) for i in range(4)])]
    ppermute x72, waiting for transfers between devices: 138 us -> 119 us  [ring_shift(): lax.ppermute(value, 'ctx', [(order[i], order[(i + step) % n]) for i in ra...]
    ppermute x72, starting transfers between devices: 104 us -> 87 us  [ring_shift(): lax.ppermute(value, 'ctx', [(order[i], order[(i + step) % n]) for i in ra...]
    pallas_call x5 -> x4, Pallas kernels: 65.3 us -> 59.2 us  [feed(): pl.pallas_call(functools.partial(feed_kernel, m, len(kept), crossed), gri...]
    unnamed x261 -> x284, local copies, waits for them, and re-layouts: 50.7 us -> 56.4 us
    ppermute x65 -> x49, starting transfers between devices: 25.5 us -> 21.3 us  [swap_fsdp(): return lax.ppermute(value, 'fsdp', [(i, i ^ d) for i in range(4)])]
  transfers between devices with their start and end apart: 140 -> 124, of which waited for: 58 -> 40; matrix products, arithmetic and copies ran while one was open for 9% -> 9% of each run, Pallas kernels for 31% -> 34%
where the time goes in v3:
time: 621 us; the launch traced here: 610 us
  Pallas kernels  222 us (36%)
  waiting for transfers between devices  142 us (23%)
  starting transfers between devices  116 us (19%)
  local copies, waits for them, and re-layouts  74.7 us (12%)
  other arithmetic  37.4 us (6%)
  between operations  16.7 us (3%)
    ppermute x72, waiting for transfers between devices, ring_shift(): lax.ppermute(value, 'ctx', [(order[i], order[(i + step) % n]) for i in ra...  119 us
    ppermute x72, starting transfers between devices, ring_shift(): lax.ppermute(value, 'ctx', [(order[i], order[(i + step) % n]) for i in ra...  87 us
    pallas_call x15, Pallas kernels, tn_blocks(): pl.pallas_call(functools.partial(tn_kernel, windows, outs), grid=(len(blo...  69.4 us
    pallas_call x4, Pallas kernels, feed(): pl.pallas_call(functools.partial(feed_kernel, m, len(kept), crossed), gri...  59.2 us
    unnamed x284, local copies, waits for them, and re-layouts  56.4 us
    pallas_call x2, Pallas kernels, attention_backward(): pl.pallas_call(functools.partial(backward_kernel, n, group, ends, first),...  28.5 us
    ppermute x49, starting transfers between devices, swap_fsdp(): return lax.ppermute(value, 'fsdp', [(i, i ^ d) for i in range(4)])  21.3 us
    ppermute x49, waiting for transfers between devices, swap_fsdp(): return lax.ppermute(value, 'fsdp', [(i, i ^ d) for i in range(4)])  17.5 us
  transfers between devices with their start and end apart: 124, of which 40 were waited for; matrix products, arithmetic and copies ran while one was open for 9% of the time, Pallas kernels for 34%

profile of v3, /device:TPU:0, one launch (start us, length us, event | category | flops | bytes accessed | tf_op | source)
XLA Modules:
  0.0 609.6 jit_solution(8780778654592813879)
XLA Ops:
  27.0 6.0 collective-permute-done.8.refs_2_.refs_4_
  34.5 8.1 %collective-permute-done.6.refs_2_ = bf16[64,2048]{1,0:T(8,128)(2,1)S(1)} collective-permute-done((bf16[64,2048]{1,0:T(8,128)(2,1)S(1)}, bf16[64,2048]{1,0:T(8,128)(2,1)S(1)}, u32[]{:S(2)}, u32[]{:S(2)}) %collective-permute-start.6) | collective-permute-done | bytes 262176 | tf_op jit(solution)/shard_map/ppermute | solution.py:781
  67.3 8.1 %collective-permute-done.20.rest_2_ = bf16[160,1024]{1,0:T(8,128)(2,1)S(1)} collective-permute-done((bf16[160,1024]{1,0:T(8,128)(2,1)S(1)}, bf16[160,1024]{1,0:T(8,128)(2,1)S(1)}, u32[]{:S(2)}, u32[]{:S(2)}) %collective-permute-start.20) | collective-permute-done | bytes 327712 | tf_op jit(solution)/shard_map/ppermute | solution.py:781
  81.4 5.9 collective-permute-done.22.rest_1_
  98.1 6.4 %collective-permute-done.25.rest_0_ = bf16[160,1024]{1,0:T(8,128)(2,1)S(1)} collective-permute-done((bf16[160,1024]{1,0:T(8,128)(2,1)S(1)}, bf16[160,1024]{1,0:T(8,128)(2,1)S(1)}, u32[]{:S(2)}, u32[]{:S(2)}) %collective-permute-start.25) | collective-permute-done | bytes 327712 | tf_op jit(solution)/shard_map/ppermute | solution.py:781
  125.8 17.5 %attention_forward.1 = (bf16[160,2048]{1,0:T(8,128)(2,1)S(1)}, f32[160,128]{1,0:T(8,128)S(1)}) custom-call(s32[31]{0:T(128)S(1)} %concatenate.147.f_ref.sc, bf16[160,2048]{1,0:T(8,128)(2,1)S(1)} %project.3.q_ref, bf16[160,1024]{1,0:T(8,128)(2,1)S(1)} %copy-done.60, bf16[160,1024]{1,0:T(8,128)(2,1)S(1)} %copy-done.71, ...), custom_call_target="tpu_custom_call" | custom-call | flops 180000000 | tf_op jit(solution)/shard_map/attention_forward/pallas_call | solution.py:131
  149.5 6.6 %out_project.1 = (f32[160,2048]{1,0:T(8,128)S(1)}, bf16[160,2048]{1,0:T(8,128)(2,1)S(1)}) custom-call(s32[31]{0:T(128)S(1)} %concatenate.147.f_ref.sc, bf16[160,2048]{1,0:T(8,128)(2,1)S(1)} %get-tuple-element.702.o_ref.left_ref, bf16[160,2048]{1,0:T(8,128)(2,1)S(1)} %copy-done.50, f32[1,2048]{1,0:T(1,128)S(1)} %get-tuple-element.607.gain_ref, ...), custom_call_target="tpu_custom_call" | custom-call | flops 60000000 | tf_op jit(solution)/shard_map/out_project/pallas_call | solution.py:381
  158.6 13.6 %collective-permute-done.37.refs_0_ = bf16[160,2048]{1,0:T(8,128)(2,1)S(1)} collective-permute-done((bf16[160,2048]{1,0:T(8,128)(2,1)S(1)}, bf16[160,2048]{1,0:T(8,128)(2,1)S(1)}, u32[]{:S(2)}, u32[]{:S(2)}) %collective-permute-start.37) | collective-permute-done | bytes 655392 | tf_op jit(solution)/shard_map/ppermute | solution.py:781
  184.5 19.5 %feed.4 = (bf16[1280,2048]{1,0:T(8,128)(2,1)}, bf16[1280,2048]{1,0:T(8,128)(2,1)}, bf16[1280,1024]{1,0:T(8,128)(2,1)}, bf16[1280,2048]{1,0:T(8,128)(2,1)}, bf16[480,2048]{1,0:T(8,128)(2,1)}) custom-call(bf16[160,2048]{1,0:T(8,128)(2,1)S(1)} %collective-permute-done.37.refs_0_, bf16[160,2048]{1,0:T(8,128)(2,1)S(1)} %get-tuple-element.489.refs_1_, ...), custom_call_target="tpu_custom_call" | custom-call | flops 200000000 | tf_op jit(solution)/shard_map/feed/pallas_call | solution.py:560
  210.4 14.3 %feed.5 = (bf16[1280,2048]{1,0:T(8,128)(2,1)}, bf16[1280,2048]{1,0:T(8,128)(2,1)}, bf16[1280,1024]{1,0:T(8,128)(2,1)}, bf16[1280,2048]{1,0:T(8,128)(2,1)}, bf16[320,2048]{1,0:T(8,128)(2,1)}) custom-call(bf16[160,2048]{1,0:T(8,128)(2,1)S(1)} %collective-permute-done.39.refs_0_, ...), custom_call_target="tpu_custom_call", output_to_operand_aliasing={{0}: (13, {}), {1}: (14, {}), {2}: (15, {}), {3}: (16, {})} | custom-call | flops 160000000 | tf_op jit(solution)/shard_map/feed/pallas_call | solution.py:560
  231.6 14.3 %feed.6 = (bf16[1280,2048]{1,0:T(8,128)(2,1)}, bf16[1280,2048]{1,0:T(8,128)(2,1)}, bf16[1280,1024]{1,0:T(8,128)(2,1)}, bf16[1280,2048]{1,0:T(8,128)(2,1)}, bf16[320,2048]{1,0:T(8,128)(2,1)}) custom-call(bf16[160,2048]{1,0:T(8,128)(2,1)S(1)} %collective-permute-done.48.refs_0_, ...), custom_call_target="tpu_custom_call", output_to_operand_aliasing={{0}: (13, {}), {1}: (14, {}), {2}: (15, {}), {3}: (16, {})} | custom-call | flops 160000000 | tf_op jit(solution)/shard_map/feed/pallas_call | solution.py:560
  247.2 11.1 %feed.7 = (bf16[1280,2048]{1,0:T(8,128)(2,1)}, bf16[1280,2048]{1,0:T(8,128)(2,1)}, bf16[1280,1024]{1,0:T(8,128)(2,1)}, bf16[1280,2048]{1,0:T(8,128)(2,1)}, bf16[160,2048]{1,0:T(8,128)(2,1)S(1)}) custom-call(bf16[160,2048]{1,0:T(8,128)(2,1)S(1)} %pad_maximum_fusion.3.refs_0_, ...), custom_call_target="tpu_custom_call", output_to_operand_aliasing={{0}: (11, {}), {1}: (12, {}), {2}: (13, {}), {3}: (14, {})} | custom-call | flops 120000000 | tf_op jit(solution)/shard_map/feed/pallas_call | solution.py:560
  265.4 10.0 %tn_blocks.15 = (bf16[512,1024]{1,0:T(8,128)(2,1)S(1)}, bf16[512,1024]{1,0:T(8,128)(2,1)S(1)}, bf16[512,1024]{1,0:T(8,128)(2,1)S(1)}, bf16[512,1024]{1,0:T(8,128)(2,1)S(1)}) custom-call(bf16[1280,2048]{1,0:T(8,128)(2,1)S(1)} %copy-done, bf16[1280,2048]{1,0:T(8,128)(2,1)S(1)} %copy-done.1), custom_call_target="tpu_custom_call" | custom-call | flops 100000000 | tf_op jit(solution)/shard_map/tn_blocks/pallas_call | solution.py:697
  278.5 7.3 %tn_blocks.16 = (bf16[256,1024]{1,0:T(8,128)(2,1)S(1)}, bf16[256,1024]{1,0:T(8,128)(2,1)S(1)}, bf16[256,1024]{1,0:T(8,128)(2,1)}, bf16[256,1024]{1,0:T(8,128)(2,1)}) custom-call(bf16[1280,1024]{1,0:T(8,128)(2,1)S(1)} %copy-done.7, bf16[1280,2048]{1,0:T(8,128)(2,1)S(1)} %copy-done.3), custom_call_target="tpu_custom_call" | custom-call | flops 60000000 | tf_op jit(solution)/shard_map/tn_blocks/pallas_call | solution.py:697
  287.5 5.7 tn_blocks.17
  299.0 7.4 %down_rows.1 = bf16[1280,2048]{1,0:T(8,128)(2,1)S(1)} custom-call(s32[31]{0:T(128)S(1)} %concatenate.147.f_ref.sc, bf16[1280,1024]{1,0:T(8,128)(2,1)S(1)} %copy-done.7, bf16[1024,2048]{1,0:T(8,128)(2,1)S(1)} %copy-done.6), custom_call_target="tpu_custom_call" | custom-call | flops 120000000 | tf_op jit(solution)/shard_map/down_rows/pallas_call | solution.py:591
  320.6 14.7 %collective-permute-done.66.rest_1_ = bf16[160,2048]{1,0:T(8,128)(2,1)S(1)} collective-permute-done((bf16[160,2048]{1,0:T(8,128)(2,1)S(1)}, bf16[160,2048]{1,0:T(8,128)(2,1)S(1)}, u32[]{:S(2)}, u32[]{:S(2)}) %collective-permute-start.66) | collective-permute-done | bytes 655392 | tf_op jit(solution)/shard_map/ppermute | solution.py:781
  345.7 6.4 %tn_blocks.19 = bf16[512,2048]{1,0:T(8,128)(2,1)S(1)} custom-call(bf16[1280,2048]{1,0:T(8,128)(2,1)S(1)} %bitcast.19, bf16[1280,2048]{1,0:T(8,128)(2,1)S(1)} %bitcast.21, bf16[512,1024]{1,0:T(8,128)(2,1)S(1)} %collective-permute-done.68.refs_0_, bf16[512,1024]{1,0:T(8,128)(2,1)} %collective-permute-done.69.refs_1_, ...), custom_call_target="tpu_custom_call" | custom-call | flops 50000000 | tf_op jit(solution)/shard_map/tn_blocks/pallas_call | solution.py:697
  367.4 14.2 %attention_backward.2 = (bf16[160,1024]{1,0:T(8,128)(2,1)}, bf16[1280,512]{1,0:T(8,128)(2,1)}) custom-call(s32[31]{0:T(128)} %copy-done.101, bf16[160,2048]{1,0:T(8,128)(2,1)} %copy-done.21, bf16[160,2048]{1,0:T(8,128)(2,1)} %copy-done.48, f32[160,128]{1,0:T(8,128)} %copy-done.94, f32[160,128]{1,0:T(8,128)} %copy-done.84, f32[160,128]{1,0:T(8,128)} %copy-done.46, ...), custom_call_target="tpu_custom_call" | custom-call | flops 260000000 | tf_op jit(solution)/shard_map/attention_backward/pallas_call | solution.py:236
  395.3 14.2 %attention_backward.3 = (bf16[160,1024]{1,0:T(8,128)(2,1)}, bf16[1280,512]{1,0:T(8,128)(2,1)}) custom-call(s32[31]{0:T(128)} %copy-done.101, bf16[160,2048]{1,0:T(8,128)(2,1)} %copy-done.21, bf16[160,2048]{1,0:T(8,128)(2,1)} %copy-done.48, f32[160,128]{1,0:T(8,128)} %copy-done.94, f32[160,128]{1,0:T(8,128)} %copy-done.84, f32[160,128]{1,0:T(8,128)} %copy-done.46, ...), custom_call_target="tpu_custom_call" | custom-call | flops 260000000 | tf_op jit(solution)/shard_map/attention_backward/pallas_call | solution.py:236
  432.1 5.9 collective-permute-done.78.refs_2_
  483.7 9.4 %collective-permute-done.95 = bf16[64,2048]{1,0:T(8,128)(2,1)} collective-permute-done((bf16[64,2048]{1,0:T(8,128)(2,1)}, bf16[64,2048]{1,0:T(8,128)(2,1)}, u32[]{:S(2)}, u32[]{:S(2)}) %collective-permute-start.95) | collective-permute-done | bytes 262176 | tf_op jit(solution)/shard_map/ppermute | solution.py:781
  498.1 7.9 %collective-permute-done.96 = bf16[64,2048]{1,0:T(8,128)(2,1)} collective-permute-done((bf16[64,2048]{1,0:T(8,128)(2,1)S(1)}, bf16[64,2048]{1,0:T(8,128)(2,1)}, u32[]{:S(2)}, u32[]{:S(2)}) %collective-permute-start.96) | collective-permute-done | bytes 262176 | tf_op jit(solution)/shard_map/ppermute | solution.py:781
  550.6 6.2 %spread.1 = (f32[64,8192]{1,0:T(8,128)}, f32[64,8192]{1,0:T(8,128)}) custom-call(s32[31]{0:T(128)S(1)} %copy-done.102, bf16[8,64,2048]{2,1,0:T(8,128)(2,1)} %all-to-all-done.all_ref), custom_call_target="tpu_custom_call" | custom-call | flops 40000000 | tf_op jit(solution)/shard_map/spread/pallas_call | solution.py:730
  (656 shorter events, 352.3 us)
Async XLA Ops:
  14.6 29.4 %collective-permute-start.4 = (bf16[512,512]{1,0:T(8,128)(2,1)}, bf16[512,512]{1,0:T(8,128)(2,1)}, u32[]{:S(2)}, u32[]{:S(2)}) collective-permute-start(bf16[512,512]{1,0:T(8,128)(2,1)} %refs_6_), channel_id=1, source_target_pairs={{0,16},{8,24},{16,0},{24,8},{1,17},{9,25},{17,1},{25,9},{2,18},{10... | collective-permute-start | bytes 1572872 | tf_op jit(solution)/shard_map/ppermute | solution.py:743
  19.3 30.5 %collective-permute-start.18 = (bf16[160,2048]{1,0:T(8,128)(2,1)}, bf16[160,2048]{1,0:T(8,128)(2,1)}, u32[]{:S(2)}, u32[]{:S(2)}) collective-permute-start(bf16[160,2048]{1,0:T(8,128)(2,1)} %base_ref), channel_id=1, source_target_pairs={{0,2},{2,4},{4,6},{6,7},{7,5},{5,3},{3,1},{1,0},{8,10},{10,12},{12... | collective-permute-start | bytes 1966088 | tf_op jit(solution)/shard_map/ppermute | solution.py:781
  44.0 48.6 %collective-permute-start.9 = (bf16[512,2048]{1,0:T(8,128)(2,1)}, bf16[512,2048]{1,0:T(8,128)(2,1)S(1)}, u32[]{:S(2)}, u32[]{:S(2)}) collective-permute-start(bf16[512,2048]{1,0:T(8,128)(2,1)} %refs_1_.1), channel_id=1, source_target_pairs={{0,16},{8,24},{16,0},{24,8},{1,17},{9,25},{17,1},{25,9},{2,18},{10... | collective-permute-start | bytes 6291464 | tf_op jit(solution)/shard_map/ppermute | solution.py:743
  87.3 26.6 %collective-permute-start.3 = (bf16[512,2048]{1,0:T(8,128)(2,1)S(1)}, bf16[512,2048]{1,0:T(8,128)(2,1)S(1)}, u32[]{:S(2)}, u32[]{:S(2)}) collective-permute-start(bf16[512,2048]{1,0:T(8,128)(2,1)S(1)} %copy-done.29), channel_id=1, source_target_pairs={{0,8},{8,0},{16,24},{24,16},{1,9},{9,1},{17,25},{25,17},{2,10},{10... | collective-permute-start | bytes 6291464 | tf_op jit(solution)/shard_map/ppermute | solution.py:743
  93.9 27.5 %collective-permute-start.31 = (bf16[512,1024]{1,0:T(8,128)(2,1)S(1)}, bf16[512,1024]{1,0:T(8,128)(2,1)S(1)}, u32[]{:S(2)}, u32[]{:S(2)}) collective-permute-start(bf16[512,1024]{1,0:T(8,128)(2,1)S(1)} %pad_maximum_fusion.1.refs_6_.refs_4_.refs_2_), channel_id=1, source_target_pairs={{0,16},{8,24},{16,0},{24,8},{1,17},{9,25},{17,1},{25,9},{2,18},{10... | collective-permute-start | bytes 3145736 | tf_op jit(solution)/shard_map/ppermute | solution.py:743
  114.0 35.5 %collective-permute-start.32 = (bf16[512,2048]{1,0:T(8,128)(2,1)}, bf16[512,2048]{1,0:T(8,128)(2,1)S(1)}, u32[]{:S(2)}, u32[]{:S(2)}) collective-permute-start(bf16[512,2048]{1,0:T(8,128)(2,1)} %refs_1_), channel_id=1, source_target_pairs={{0,8},{8,0},{16,24},{24,16},{1,9},{9,1},{17,25},{25,17},{2,10},{10... | collective-permute-start | bytes 6291464 | tf_op jit(solution)/shard_map/ppermute | solution.py:743
  122.2 27.2 %collective-permute-start.33 = (bf16[512,2048]{1,0:T(8,128)(2,1)S(1)}, bf16[512,2048]{1,0:T(8,128)(2,1)S(1)}, u32[]{:S(2)}, u32[]{:S(2)}) collective-permute-start(bf16[512,2048]{1,0:T(8,128)(2,1)S(1)} %place_rows.1.w2.refs_3_), channel_id=1, source_target_pairs={{0,8},{8,0},{16,24},{24,16},{1,9},{9,1},{17,25},{25,17},{2,10},{10... | collective-permute-start | bytes 6291464 | tf_op jit(solution)/shard_map/ppermute | solution.py:743
  148.1 26.2 %collective-permute-start.46 = (bf16[256,2048]{1,0:T(8,128)(2,1)}, bf16[256,2048]{1,0:T(8,128)(2,1)S(1)}, u32[]{:S(2)}, u32[]{:S(2)}) collective-permute-start(bf16[256,2048]{1,0:T(8,128)(2,1)} %constant_dynamic-slice_fusion.6), channel_id=1, source_target_pairs={{0,16},{8,24},{16,0},{24,8},{1,17},{9,25},{17,1},{25,9},{2,18},{10... | collective-permute-start | bytes 3145736 | tf_op jit(solution)/shard_map/ppermute | solution.py:743
  174.9 31.2 %collective-permute-start.39 = (bf16[160,2048]{1,0:T(8,128)(2,1)S(1)}, bf16[160,2048]{1,0:T(8,128)(2,1)S(1)}, u32[]{:S(2)}, u32[]{:S(2)}) collective-permute-start(bf16[160,2048]{1,0:T(8,128)(2,1)S(1)} %collective-permute-done.37.refs_0_), channel_id=1, source_target_pairs={{0,2},{2,4},{4,6},{6,7},{7,5},{5,3},{3,1},{1,0},{8,10},{10,12},{12... | collective-permute-start | bytes 1966088 | tf_op jit(solution)/shard_map/ppermute | solution.py:781
  176.5 29.6 %collective-permute-start.40 = (bf16[160,2048]{1,0:T(8,128)(2,1)S(1)}, bf16[160,2048]{1,0:T(8,128)(2,1)S(1)}, u32[]{:S(2)}, u32[]{:S(2)}) collective-permute-start(bf16[160,2048]{1,0:T(8,128)(2,1)S(1)} %collective-permute-done.38.refs_2_), channel_id=1, source_target_pairs={{0,1},{2,0},{4,2},{6,4},{7,6},{5,7},{3,5},{1,3},{8,9},{10,8},{12,1... | collective-permute-start | bytes 1966088 | tf_op jit(solution)/shard_map/ppermute | solution.py:781
  177.0 31.2 %collective-permute-start.50 = (bf16[160,2048]{1,0:T(8,128)(2,1)S(1)}, bf16[160,2048]{1,0:T(8,128)(2,1)S(1)}, u32[]{:S(2)}, u32[]{:S(2)}) collective-permute-start(bf16[160,2048]{1,0:T(8,128)(2,1)S(1)} %collective-permute-done.34.refs_2_), channel_id=1, source_target_pairs={{0,2},{2,4},{4,6},{6,7},{7,5},{5,3},{3,1},{1,0},{8,10},{10,12},{12... | collective-permute-start | bytes 1966088 | tf_op jit(solution)/shard_map/ppermute | solution.py:781
  180.0 28.2 %collective-permute-start.51 = (bf16[160,2048]{1,0:T(8,128)(2,1)S(1)}, bf16[160,2048]{1,0:T(8,128)(2,1)S(1)}, u32[]{:S(2)}, u32[]{:S(2)}) collective-permute-start(bf16[160,2048]{1,0:T(8,128)(2,1)S(1)} %collective-permute-done.35.refs_3_), channel_id=1, source_target_pairs={{0,1},{2,0},{4,2},{6,4},{7,6},{5,7},{3,5},{1,3},{8,9},{10,8},{12,1... | collective-permute-start | bytes 1966088 | tf_op jit(solution)/shard_map/ppermute | solution.py:781
  293.2 52.4 %collective-permute-start.70 = (bf16[512,2048]{1,0:T(8,128)(2,1)}, bf16[512,2048]{1,0:T(8,128)(2,1)}, u32[]{:S(2)}, u32[]{:S(2)}) collective-permute-start(bf16[512,2048]{1,0:T(8,128)(2,1)} %tn_blocks.17), channel_id=1, source_target_pairs={{0,16},{8,24},{16,0},{24,8},{1,17},{9,25},{17,1},{25,9},{2,18},{10... | collective-permute-start | bytes 6291464 | tf_op jit(solution)/shard_map/ppermute | solution.py:743
  308.8 36.9 %collective-permute-start.68 = (bf16[512,1024]{1,0:T(8,128)(2,1)}, bf16[512,1024]{1,0:T(8,128)(2,1)S(1)}, u32[]{:S(2)}, u32[]{:S(2)}) collective-permute-start(bf16[512,1024]{1,0:T(8,128)(2,1)} %copy-done.110), channel_id=1, source_target_pairs={{0,8},{8,0},{16,24},{24,16},{1,9},{9,1},{17,25},{25,17},{2,10},{10... | collective-permute-start | bytes 3145736 | tf_op jit(solution)/shard_map/ppermute | solution.py:743
  308.8 36.9 %collective-permute-start.69 = (bf16[512,1024]{1,0:T(8,128)(2,1)}, bf16[512,1024]{1,0:T(8,128)(2,1)}, u32[]{:S(2)}, u32[]{:S(2)}) collective-permute-start(bf16[512,1024]{1,0:T(8,128)(2,1)} %copy-done.109), channel_id=1, source_target_pairs={{0,8},{8,0},{16,24},{24,16},{1,9},{9,1},{17,25},{25,17},{2,10},{10... | collective-permute-start | bytes 3145736 | tf_op jit(solution)/shard_map/ppermute | solution.py:743
  353.4 58.6 %all-to-all-start = ((bf16[8,64,2048]{2,1,0:T(8,128)(2,1)}), bf16[8,64,2048]{2,1,0:T(8,128)(2,1)}, u32[]{:S(2)}, u32[]{:S(2)}) async-start(bf16[8,64,2048]{2,1,0:T(8,128)(2,1)} %bitcast.22), calls=%async_computation | async-start | bytes 4194304 | tf_op jit(solution)/shard_map/all_to_all | solution.py:1107
  358.0 238.7 %reduce-scatter.2.cloned.1.call-start = ((), (), s32[]{:S(2)}) async-start(), calls=%async_computation.3 | async-start | bytes 5898240 | tf_op jit(solution)/shard_map/reduce_scatter | solution.py:1164
  390.9 47.1 %collective-permute-start.78 = (bf16[512,2048]{1,0:T(8,128)(2,1)}, bf16[512,2048]{1,0:T(8,128)(2,1)}, u32[]{:S(2)}, u32[]{:S(2)}) collective-permute-start(bf16[512,2048]{1,0:T(8,128)(2,1)} %tn_blocks.21), channel_id=1, source_target_pairs={{0,16},{8,24},{16,0},{24,8},{1,17},{9,25},{17,1},{25,9},{2,18},{10... | collective-permute-start | bytes 6291464 | tf_op jit(solution)/shard_map/ppermute | solution.py:743
  458.6 65.4 %collective-permute-start.91 = (bf16[512,2048]{1,0:T(8,128)(2,1)}, bf16[512,2048]{1,0:T(8,128)(2,1)}, u32[]{:S(2)}, u32[]{:S(2)}) collective-permute-start(bf16[512,2048]{1,0:T(8,128)(2,1)} %copy-done.76), channel_id=1, source_target_pairs={{0,16},{8,24},{16,0},{24,8},{1,17},{9,25},{17,1},{25,9},{2,18},{10... | collective-permute-start | bytes 6291464 | tf_op jit(solution)/shard_map/ppermute | solution.py:743
  476.0 55.5 %collective-permute-start.100 = (bf16[512,1024]{1,0:T(8,128)(2,1)}, bf16[512,1024]{1,0:T(8,128)(2,1)}, u32[]{:S(2)}, u32[]{:S(2)}) collective-permute-start(bf16[512,1024]{1,0:T(8,128)(2,1)} %copy-done.104), channel_id=1, source_target_pairs={{0,8},{8,0},{16,24},{24,16},{1,9},{9,1},{17,25},{25,17},{2,10},{10... | collective-permute-start | bytes 3145736 | tf_op jit(solution)/shard_map/ppermute | solution.py:743
  476.0 56.0 %collective-permute-start.99 = (bf16[512,1024]{1,0:T(8,128)(2,1)}, bf16[512,1024]{1,0:T(8,128)(2,1)}, u32[]{:S(2)}, u32[]{:S(2)}) collective-permute-start(bf16[512,1024]{1,0:T(8,128)(2,1)} %copy-done.103), channel_id=1, source_target_pairs={{0,8},{8,0},{16,24},{24,16},{1,9},{9,1},{17,25},{25,17},{2,10},{10... | collective-permute-start | bytes 3145736 | tf_op jit(solution)/shard_map/ppermute | solution.py:743
  526.3 35.6 %collective-permute-start.87 = (bf16[512,512]{1,0:T(8,128)(2,1)}, bf16[512,512]{1,0:T(8,128)(2,1)}, u32[]{:S(2)}, u32[]{:S(2)}) collective-permute-start(bf16[512,512]{1,0:T(8,128)(2,1)} %copy-done.113), channel_id=1, source_target_pairs={{0,8},{8,0},{16,24},{24,16},{1,9},{9,1},{17,25},{25,17},{2,10},{10... | collective-permute-start | bytes 1572872 | tf_op jit(solution)/shard_map/ppermute | solution.py:743
  531.4 31.0 %collective-permute-start.88 = (bf16[512,512]{1,0:T(8,128)(2,1)}, bf16[512,512]{1,0:T(8,128)(2,1)}, u32[]{:S(2)}, u32[]{:S(2)}) collective-permute-start(bf16[512,512]{1,0:T(8,128)(2,1)} %get-tuple-element.713), channel_id=1, source_target_pairs={{0,8},{8,0},{16,24},{24,16},{1,9},{9,1},{17,25},{25,17},{2,10},{10... | collective-permute-start | bytes 1572872 | tf_op jit(solution)/shard_map/ppermute | solution.py:743
  531.9 29.9 %collective-permute-start.98 = (bf16[512,1024]{1,0:T(8,128)(2,1)}, bf16[512,1024]{1,0:T(8,128)(2,1)}, u32[]{:S(2)}, u32[]{:S(2)}) collective-permute-start(bf16[512,1024]{1,0:T(8,128)(2,1)} %tn_blocks.26), channel_id=1, source_target_pairs={{0,16},{8,24},{16,0},{24,8},{1,17},{9,25},{17,1},{25,9},{2,18},{10... | collective-permute-start | bytes 3145736 | tf_op jit(solution)/shard_map/ppermute | solution.py:743
  (240 other events, 2980.5 us)
Sparse Core Ops, SparseCore 0:
  458.6 116.5 reduce-scatter.1

commit v4 on v3

--- a/solution.py
+++ b/solution.py
@@ -11,7 +11,7 @@
 NORM_EPS = 1e-05
 ROPE_BASE = 500000.0
 MASKED = -1e30
-VARIANTS = 5
+VARIANTS = 10
 BF = jnp.bfloat16
 F32 = jnp.float32
 MIB = 2**20
@@ -578,32 +578,28 @@
         cost_estimate=cost(8 + 4 * m),
         name="feed",
     )(*hidden, *grads, *gate, *up, down, *kept)
-    return kept, [dh[i * count : (i + 1) * count] for i in range(m)]
-
-
-def down_kernel(sc, act_ref, down_ref, y_ref):
+    return kept, dh
+
+
+def down_kernel(act_ref, down_ref, y_ref):
     y_ref[...] = dot(act_ref[...], down_ref[...]).astype(BF)
 
 
-def down_rows(scalars, act, down, n):
+def down_rows(act, down, n):
     count = act.shape[0] // n
-    at = scalars.shape[0] - n
     return pl.pallas_call(
         down_kernel,
-        grid_spec=pltpu.PrefetchScalarGridSpec(
-            num_scalar_prefetch=1,
-            grid=(n,),
-            in_specs=[
-                pl.BlockSpec((count, act.shape[1]), lambda i, sc: (i, 0)),
-                pl.BlockSpec(down.shape, lambda i, sc: (0, 0)),
-            ],
-            out_specs=pl.BlockSpec((count, down.shape[1]), lambda i, sc: (sc[at + i], 0)),
-        ),
+        grid=(n // 2,),
+        in_specs=[
+            pl.BlockSpec((2 * count, act.shape[1]), lambda i: (i, 0)),
+            pl.BlockSpec(down.shape, lambda i: (0, 0)),
+        ],
+        out_specs=pl.BlockSpec((2 * count, down.shape[1]), lambda i: (i, 0)),
         out_shape=jax.ShapeDtypeStruct((n * count, down.shape[1]), BF),
         compiler_params=params(32),
-        cost_estimate=cost(12),
+        cost_estimate=cost(8),
         name="down_rows",
-    )(scalars, act, down)
+    )(act, down)
 
 
 def place_kernel(sc, *refs):
@@ -935,9 +931,7 @@
     count = lengths.shape[1]
     groups = [(-1, 0, 1)] + [(-step, step) for step in range(2, half)] + [(half,)]
     slot_rel = [r for group in (groups[0], groups[-1], *groups[1:-1]) for r in group]
-    slot_owners = ring_index(place + jnp.asarray(slot_rel, jnp.int32), n)
-    scalars = jnp.concatenate([f[None], own_blocks, key_blocks, seq_ends, slot_owners])
-    scalars = scalars.astype(jnp.int32)
+    scalars = jnp.concatenate([f[None], own_blocks, key_blocks, seq_ends]).astype(jnp.int32)
     cosine, sine = turn_tables(own_blocks, block, seq_ends, seq_ends - lengths[0])
     order = Order()
 
@@ -1024,7 +1018,7 @@
     kept, grads_two = [], {}
     for at, group in enumerate(groups):
         slot = slot_rel.index(group[0]) // len(group)
-        kept, parts = order.run(
+        kept, sums = order.run(
             feed,
             [hidden.chunks[r] for r in group],
             [grad_out.chunks[r] for r in group],
@@ -1035,7 +1029,7 @@
             kept=kept,
             n=n,
         )
-        grads_two.update(zip(group, parts))
+        grads_two.update((r, (sums, i)) for i, r in enumerate(group))
         if at < half - 1:
             hidden.take()
             hidden.send()
@@ -1083,7 +1077,11 @@
             ((whole,),) = self.kernel((0,), kind, self.pieces(0) + adds)
             return whole
 
-    sums = Scatter(order, lambda r: grads_two[r], n)
+    def feed_contrib(r):
+        value, i = grads_two[r]
+        return value[i * token_rows : (i + 1) * token_rows]
+
+    sums = Scatter(order, feed_contrib, n)
     sums.send()
     of_down = Product(act, rows_dy, 3)
     of_gate_up = Product(rows_h, grads, 5, True)
@@ -1092,7 +1090,7 @@
     of_down.first()
     of_gate_up.second()
     sums.rest(1)
-    y_rows = order.run(down_rows, scalars, act, down, n=n)
+    y_rows = order.run(down_rows, act, down, n=n)
     of_down.second()
     sums.rest(1)
     sums.rest()
@@ -1130,9 +1128,7 @@
 
     attention_part(0)
     of_down.settle()
-    of_out.second()
     attention_part(2)
-    gate_up_all = order.take(gate_up_all)
     grad_query = jnp.concatenate([p[0] for p in parts], axis=1)
 
     def kv_contrib(r):
@@ -1150,20 +1146,28 @@
 
     grad_kv = Scatter(order, kv_contrib, n)
     grad_kv.send()
+    of_out.second()
     of_query = Product(hidden_one, grad_query, 2)
     of_query.first()
+    gate_up_all = order.take(gate_up_all)
     grad_kv.rest(1)
     grad_hidden_one = order.run(back_project, [grad_query], [weight_q], kind=F32, micros=5)
-    of_out.settle()
     grad_kv.rest(1)
     of_query.second()
     grad_kv.rest(1)
+    of_out.settle()
     out_within = of_out.last(BF)
     grad_kv.rest()
     grad_kv = added(grad_kv.take())
-    y_own = lax.psum_scatter(order.at(y_rows), "ctx", scatter_dimension=0, tiled=True)
     out_sums = scatter_rows(out_within)
     out_sums.send()
+
+    def y_contrib(r):
+        start = slot_rel.index(r) * token_rows
+        return y_rows[start : start + token_rows]
+
+    y_sums = Scatter(order, y_contrib, n)
+    y_sums.send()
     grad_kv = turn_back(grad_kv, cosine, sine).astype(BF)
     grad_key, grad_value = deinterleave(grad_kv)
     grad_kv = jnp.concatenate([grad_key, grad_value], axis=1)
@@ -1173,20 +1177,25 @@
     grad_hidden_one = order.run(
         back_project, [grad_key, grad_value], [weight_k, weight_v], base=grad_hidden_one, kind=F32, micros=3
     )
+    of_kv.second()
+    y_sums.rest(1)
     out_sums.rest(1)
     tokens_grad, gain_one_term = order.run(
         norm_back, scalars, tokens, gain_one, grad_residual, [grad_hidden_one], rounded=False
     )
+    y_sums.rest(1)
     out_sums.rest(1)
     gain_terms = xor_blocks(jnp.concatenate([gain_one_term, gain_two_term], axis=0), f, 1)
     gain_terms = gain_terms.astype(BF).reshape(2, 4 * n, model // (4 * n)).transpose(1, 0, 2)
     gain_terms = lax.all_to_all(gain_terms, ("fsdp", "ctx"), 0, 0, tiled=False)
+    out_sums.rest()
+    out_grad = order.done(added(out_sums.take()))
+    y_sums.rest(1)
     of_query.settle()
-    of_kv.second()
     query_sums = scatter_rows(of_query.last(BF))
     query_sums.send()
-    out_sums.rest()
-    out_grad = order.done(added(out_sums.take()))
+    y_sums.rest()
+    layer_out = order.done((residual + added(y_sums.take())).astype(BF))
     query_sums.rest(1)
     if crossed:
         gate_grad, up_grad = order.run(spread, scalars, gate_up_all, units=units, tile=tile)
@@ -1194,7 +1203,6 @@
         gate_up_all = gate_up_all.reshape(n, rows, 2, 4, units).transpose(2, 1, 3, 0, 4)
         gate_up_all = xor_blocks(gate_up_all, f, 2).reshape(2, rows, n * width).astype(F32)
         gate_grad, up_grad = order.done((gate_up_all[0], gate_up_all[1]))
-    gain_terms = order.take(gain_terms)
     of_kv.settle()
     kv_sums = scatter_rows(of_kv.last(BF))
     kv_sums.send()
@@ -1202,10 +1210,10 @@
     down_grad = of_down.last(F32)
     kv_sums.rest(1)
     query_sums.rest()
+    gain_terms = order.take(gain_terms)
     kv_sums.rest(1)
     query_grad = order.done(added(query_sums.take()))
     kv_sums.rest()
-    layer_out = order.done((residual + order.at(y_own).astype(F32)).astype(BF))
     kv_grad = order.done(added(kv_sums.take()))
     gain_grads = jnp.sum(gain_terms.astype(F32), axis=0)
     kv_width = key_matrix.shape[1]

time: 621 us -> 597 us (0.961)
  local copies, waits for them, and re-layouts: 74.7 us -> 58.2 us
  between operations: 16.7 us -> 2.66 us
  other arithmetic: 37.4 us -> 44 us
    unnamed x284 -> x236, local copies, waits for them, and re-layouts: 56.4 us -> 40 us
    ppermute x72 -> x80, waiting for transfers between devices: 119 us -> 132 us  [ring_shift(): lax.ppermute(value, 'ctx', [(order[i], order[(i + step) % n]) for i in ra...]
    convert_element_type x12 -> x14, other arithmetic: 9.64 us -> 18.7 us  [take(): self.now = self.order.done((ahead.astype(BF), behind.astype(BF)))]
    ppermute x72 -> x80, starting transfers between devices: 87 us -> 85.7 us  [ring_shift(): lax.ppermute(value, 'ctx', [(order[i], order[(i + step) % n]) for i in ra...]
  transfers between devices with their start and end apart: 124 -> 131, of which waited for: 40 -> 49; matrix products, arithmetic and copies ran while one was open for 9% -> 10% of each run, Pallas kernels for 34% -> 35%
where the time goes in v4:
time: 597 us; the launch traced here: 591 us
  Pallas kernels  222 us (37%)
  waiting for transfers between devices  148 us (25%)
  starting transfers between devices  116 us (19%)
  local copies, waits for them, and re-layouts  58.2 us (10%)
  other arithmetic  44 us (7%)
    ppermute x80, waiting for transfers between devices, ring_shift(): lax.ppermute(value, 'ctx', [(order[i], order[(i + step) % n]) for i in ra...  132 us
    ppermute x80, starting transfers between devices, ring_shift(): lax.ppermute(value, 'ctx', [(order[i], order[(i + step) % n]) for i in ra...  85.7 us
    pallas_call x15, Pallas kernels, tn_blocks(): pl.pallas_call(functools.partial(tn_kernel, windows, outs), grid=(len(blo...  70.1 us
    pallas_call x4, Pallas kernels, feed(): pl.pallas_call(functools.partial(feed_kernel, m, len(kept), crossed), gri...  59.3 us
    unnamed x236, local copies, waits for them, and re-layouts  40 us
    pallas_call x2, Pallas kernels, attention_backward(): pl.pallas_call(functools.partial(backward_kernel, n, group, ends, first),...  28 us
    ppermute x49, starting transfers between devices, swap_fsdp(): return lax.ppermute(value, 'fsdp', [(i, i ^ d) for i in range(4)])  20.8 us
    convert_element_type x14, other arithmetic, take(): self.now = self.order.done((ahead.astype(BF), behind.astype(BF)))  18.7 us
  transfers between devices with their start and end apart: 131, of which 49 were waited for; matrix products, arithmetic and copies ran while one was open for 10% of the time, Pallas kernels for 35%

profile of v4, /device:TPU:0, one launch (start us, length us, event | category | flops | bytes accessed | tf_op | source)
XLA Modules:
  0.0 590.7 jit_solution(16454202302897661252)
XLA Ops:
  19.7 6.7 %collective-permute-done.8.refs_2_.refs_4_ = bf16[512,512]{1,0:T(8,128)(2,1)S(1)} collective-permute-done((bf16[512,512]{1,0:T(8,128)(2,1)}, bf16[512,512]{1,0:T(8,128)(2,1)S(1)}, u32[]{:S(2)}, u32[]{:S(2)}) %collective-permute-start.8) | collective-permute-done | bytes 524320 | tf_op jit(solution)/shard_map/ppermute | solution.py:739
  27.9 7.4 %collective-permute-done.6.refs_2_ = bf16[64,2048]{1,0:T(8,128)(2,1)S(1)} collective-permute-done((bf16[64,2048]{1,0:T(8,128)(2,1)S(1)}, bf16[64,2048]{1,0:T(8,128)(2,1)S(1)}, u32[]{:S(2)}, u32[]{:S(2)}) %collective-permute-start.6) | collective-permute-done | bytes 262176 | tf_op jit(solution)/shard_map/ppermute | solution.py:777
  59.5 8.1 %collective-permute-done.20.rest_2_ = bf16[160,1024]{1,0:T(8,128)(2,1)S(1)} collective-permute-done((bf16[160,1024]{1,0:T(8,128)(2,1)S(1)}, bf16[160,1024]{1,0:T(8,128)(2,1)S(1)}, u32[]{:S(2)}, u32[]{:S(2)}) %collective-permute-start.20) | collective-permute-done | bytes 327712 | tf_op jit(solution)/shard_map/ppermute | solution.py:777
  73.0 6.6 %collective-permute-done.22.rest_1_ = bf16[160,1024]{1,0:T(8,128)(2,1)S(1)} collective-permute-done((bf16[160,1024]{1,0:T(8,128)(2,1)S(1)}, bf16[160,1024]{1,0:T(8,128)(2,1)S(1)}, u32[]{:S(2)}, u32[]{:S(2)}) %collective-permute-start.22) | collective-permute-done | bytes 327712 | tf_op jit(solution)/shard_map/ppermute | solution.py:777
  89.4 7.8 %collective-permute-done.25.rest_0_ = bf16[160,1024]{1,0:T(8,128)(2,1)S(1)} collective-permute-done((bf16[160,1024]{1,0:T(8,128)(2,1)S(1)}, bf16[160,1024]{1,0:T(8,128)(2,1)S(1)}, u32[]{:S(2)}, u32[]{:S(2)}) %collective-permute-start.25) | collective-permute-done | bytes 327712 | tf_op jit(solution)/shard_map/ppermute | solution.py:777
  117.8 16.9 %attention_forward.1 = (bf16[160,2048]{1,0:T(8,128)(2,1)S(1)}, f32[160,128]{1,0:T(8,128)S(1)}) custom-call(s32[23]{0:T(128)S(1)} %pad_add_fusion.f_ref.sc, bf16[160,2048]{1,0:T(8,128)(2,1)S(1)} %project.3.q_ref, bf16[160,1024]{1,0:T(8,128)(2,1)S(1)} %collective-permute-done.25.rest_0_, bf16[160,1024]{1,0:T(8,128)(2,1)S(1)} %collective-permute-done.22.rest_1_, ...), custom_call_target="tpu_custom_call" | custom-call | flops 180000000 | tf_op jit(solution)/shard_map/attention_forward/pallas_call | solution.py:131
  141.7 6.7 %out_project.1 = (f32[160,2048]{1,0:T(8,128)S(1)}, bf16[160,2048]{1,0:T(8,128)(2,1)S(1)}) custom-call(s32[23]{0:T(128)S(1)} %pad_add_fusion.f_ref.sc, bf16[160,2048]{1,0:T(8,128)(2,1)S(1)} %get-tuple-element.706.o_ref.left_ref, bf16[160,2048]{1,0:T(8,128)(2,1)S(1)} %copy-done.34, f32[1,2048]{1,0:T(1,128)S(1)} %get-tuple-element.611.gain_ref, ...), custom_call_target="tpu_custom_call" | custom-call | flops 60000000 | tf_op jit(solution)/shard_map/out_project/pallas_call | solution.py:381
  152.6 12.9 %collective-permute-done.37.refs_0_ = bf16[160,2048]{1,0:T(8,128)(2,1)S(1)} collective-permute-done((bf16[160,2048]{1,0:T(8,128)(2,1)S(1)}, bf16[160,2048]{1,0:T(8,128)(2,1)S(1)}, u32[]{:S(2)}, u32[]{:S(2)}) %collective-permute-start.37) | collective-permute-done | bytes 655392 | tf_op jit(solution)/shard_map/ppermute | solution.py:777
  176.8 19.5 %feed.4 = (bf16[1280,2048]{1,0:T(8,128)(2,1)}, bf16[1280,2048]{1,0:T(8,128)(2,1)}, bf16[1280,1024]{1,0:T(8,128)(2,1)}, bf16[1280,2048]{1,0:T(8,128)(2,1)}, bf16[480,2048]{1,0:T(8,128)(2,1)}) custom-call(bf16[160,2048]{1,0:T(8,128)(2,1)S(1)} %collective-permute-done.37.refs_0_, bf16[160,2048]{1,0:T(8,128)(2,1)S(1)} %copy-done.70, ...), custom_call_target="tpu_custom_call" | custom-call | flops 200000000 | tf_op jit(solution)/shard_map/feed/pallas_call | solution.py:560
  204.3 14.5 %feed.5 = (bf16[1280,2048]{1,0:T(8,128)(2,1)}, bf16[1280,2048]{1,0:T(8,128)(2,1)}, bf16[1280,1024]{1,0:T(8,128)(2,1)}, bf16[1280,2048]{1,0:T(8,128)(2,1)}, bf16[320,2048]{1,0:T(8,128)(2,1)}) custom-call(bf16[160,2048]{1,0:T(8,128)(2,1)S(1)} %collective-permute-done.39.refs_0_, ...), custom_call_target="tpu_custom_call", output_to_operand_aliasing={{0}: (13, {}), {1}: (14, {}), {2}: (15, {}), {3}: (16, {})} | custom-call | flops 160000000 | tf_op jit(solution)/shard_map/feed/pallas_call | solution.py:560
  223.2 14.4 %feed.6 = (bf16[1280,2048]{1,0:T(8,128)(2,1)}, bf16[1280,2048]{1,0:T(8,128)(2,1)}, bf16[1280,1024]{1,0:T(8,128)(2,1)}, bf16[1280,2048]{1,0:T(8,128)(2,1)}, bf16[320,2048]{1,0:T(8,128)(2,1)}) custom-call(bf16[160,2048]{1,0:T(8,128)(2,1)S(1)} %collective-permute-done.48.refs_0_, ...), custom_call_target="tpu_custom_call", output_to_operand_aliasing={{0}: (13, {}), {1}: (14, {}), {2}: (15, {}), {3}: (16, {})} | custom-call | flops 160000000 | tf_op jit(solution)/shard_map/feed/pallas_call | solution.py:560
  238.8 11.0 %feed.7 = (bf16[1280,2048]{1,0:T(8,128)(2,1)}, bf16[1280,2048]{1,0:T(8,128)(2,1)}, bf16[1280,1024]{1,0:T(8,128)(2,1)}, bf16[1280,2048]{1,0:T(8,128)(2,1)}, bf16[160,2048]{1,0:T(8,128)(2,1)S(1)}) custom-call(bf16[160,2048]{1,0:T(8,128)(2,1)S(1)} %pad_maximum_fusion.3.refs_0_, ...), custom_call_target="tpu_custom_call", output_to_operand_aliasing={{0}: (11, {}), {1}: (12, {}), {2}: (13, {}), {3}: (14, {})} | custom-call | flops 120000000 | tf_op jit(solution)/shard_map/feed/pallas_call | solution.py:560
  256.9 10.0 %tn_blocks.15 = (bf16[512,1024]{1,0:T(8,128)(2,1)S(1)}, bf16[512,1024]{1,0:T(8,128)(2,1)S(1)}, bf16[512,1024]{1,0:T(8,128)(2,1)S(1)}, bf16[512,1024]{1,0:T(8,128)(2,1)S(1)}) custom-call(bf16[1280,2048]{1,0:T(8,128)(2,1)S(1)} %copy-done, bf16[1280,2048]{1,0:T(8,128)(2,1)S(1)} %copy-done.1), custom_call_target="tpu_custom_call" | custom-call | flops 100000000 | tf_op jit(solution)/shard_map/tn_blocks/pallas_call | solution.py:693
  273.3 7.3 %tn_blocks.16 = (bf16[256,1024]{1,0:T(8,128)(2,1)S(1)}, bf16[256,1024]{1,0:T(8,128)(2,1)S(1)}, bf16[256,1024]{1,0:T(8,128)(2,1)}, bf16[256,1024]{1,0:T(8,128)(2,1)}) custom-call(bf16[1280,1024]{1,0:T(8,128)(2,1)S(1)} %copy-done.5, bf16[1280,2048]{1,0:T(8,128)(2,1)S(1)} %copy-done.3), custom_call_target="tpu_custom_call" | custom-call | flops 60000000 | tf_op jit(solution)/shard_map/tn_blocks/pallas_call | solution.py:693
  281.4 5.7 tn_blocks.17
  292.7 6.1 %down_rows.1 = bf16[1280,2048]{1,0:T(8,128)(2,1)S(1)} custom-call(bf16[1280,1024]{1,0:T(8,128)(2,1)S(1)} %copy-done.5, bf16[1024,2048]{1,0:T(8,128)(2,1)S(1)} %copy-done.4), custom_call_target="tpu_custom_call" | custom-call | flops 80000000 | tf_op jit(solution)/shard_map/down_rows/pallas_call | solution.py:590
  313.0 11.5 %collective-permute-done.68.rest_1_ = bf16[160,2048]{1,0:T(8,128)(2,1)S(1)} collective-permute-done((bf16[160,2048]{1,0:T(8,128)(2,1)S(1)}, bf16[160,2048]{1,0:T(8,128)(2,1)S(1)}, u32[]{:S(2)}, u32[]{:S(2)}) %collective-permute-start.68) | collective-permute-done | bytes 655392 | tf_op jit(solution)/shard_map/ppermute | solution.py:777
  334.6 6.4 %tn_blocks.19 = bf16[512,2048]{1,0:T(8,128)(2,1)S(1)} custom-call(bf16[1280,2048]{1,0:T(8,128)(2,1)S(1)} %bitcast.17, bf16[1280,2048]{1,0:T(8,128)(2,1)S(1)} %copy-done.2, bf16[512,1024]{1,0:T(8,128)(2,1)S(1)} %collective-permute-done.70.refs_0_, bf16[512,1024]{1,0:T(8,128)(2,1)} %collective-permute-done.71.refs_1_, ...), custom_call_target="tpu_custom_call" | custom-call | flops 50000000 | tf_op jit(solution)/shard_map/tn_blocks/pallas_call | solution.py:693
  347.9 5.9 tn_blocks.20
  354.3 13.8 %attention_backward.2 = (bf16[160,1024]{1,0:T(8,128)(2,1)}, bf16[1280,512]{1,0:T(8,128)(2,1)}) custom-call(s32[23]{0:T(128)} %copy-done.81, bf16[160,2048]{1,0:T(8,128)(2,1)} %copy-done.12, bf16[160,2048]{1,0:T(8,128)(2,1)} %copy-done.32, f32[160,128]{1,0:T(8,128)} %copy-done.74, f32[160,128]{1,0:T(8,128)} %copy-done.61, f32[160,128]{1,0:T(8,128)} %copy-done.30, ...), custom_call_target="tpu_custom_call" | custom-call | flops 260000000 | tf_op jit(solution)/shard_map/attention_backward/pallas_call | solution.py:236
  370.6 14.1 %attention_backward.3 = (bf16[160,1024]{1,0:T(8,128)(2,1)}, bf16[1280,512]{1,0:T(8,128)(2,1)}) custom-call(s32[23]{0:T(128)} %copy-done.81, bf16[160,2048]{1,0:T(8,128)(2,1)} %copy-done.12, bf16[160,2048]{1,0:T(8,128)(2,1)} %copy-done.32, f32[160,128]{1,0:T(8,128)} %copy-done.74, f32[160,128]{1,0:T(8,128)} %copy-done.61, f32[160,128]{1,0:T(8,128)} %copy-done.30, ...), custom_call_target="tpu_custom_call" | custom-call | flops 260000000 | tf_op jit(solution)/shard_map/attention_backward/pallas_call | solution.py:236
  503.9 9.3 %collective-permute-done.97 = bf16[160,2048]{1,0:T(8,128)(2,1)} collective-permute-done((bf16[160,2048]{1,0:T(8,128)(2,1)}, bf16[160,2048]{1,0:T(8,128)(2,1)}, u32[]{:S(2)}, u32[]{:S(2)}) %collective-permute-start.97) | collective-permute-done | bytes 655392 | tf_op jit(solution)/shard_map/ppermute | solution.py:777
  524.3 7.2 %collective-permute-done.103 = bf16[160,2048]{1,0:T(8,128)(2,1)S(1)} collective-permute-done((bf16[160,2048]{1,0:T(8,128)(2,1)}, bf16[160,2048]{1,0:T(8,128)(2,1)S(1)}, u32[]{:S(2)}, u32[]{:S(2)}) %collective-permute-start.103) | collective-permute-done | bytes 655392 | tf_op jit(solution)/shard_map/ppermute | solution.py:777
  548.4 6.6 %spread.1 = (f32[64,8192]{1,0:T(8,128)}, f32[64,8192]{1,0:T(8,128)}) custom-call(s32[23]{0:T(128)S(1)} %copy-done.82, bf16[8,64,2048]{2,1,0:T(8,128)(2,1)} %all-to-all-done.all_ref), custom_call_target="tpu_custom_call" | custom-call | flops 40000000 | tf_op jit(solution)/shard_map/spread/pallas_call | solution.py:726
  (626 shorter events, 351.7 us)
Async XLA Ops:
  8.1 29.3 %collective-permute-start.4 = (bf16[512,512]{1,0:T(8,128)(2,1)}, bf16[512,512]{1,0:T(8,128)(2,1)}, u32[]{:S(2)}, u32[]{:S(2)}) collective-permute-start(bf16[512,512]{1,0:T(8,128)(2,1)} %refs_6_), channel_id=1, source_target_pairs={{0,16},{8,24},{16,0},{24,8},{1,17},{9,25},{17,1},{25,9},{2,18},{10... | collective-permute-start | bytes 1572872 | tf_op jit(solution)/shard_map/ppermute | solution.py:739
  12.1 30.5 %collective-permute-start.18 = (bf16[160,2048]{1,0:T(8,128)(2,1)}, bf16[160,2048]{1,0:T(8,128)(2,1)}, u32[]{:S(2)}, u32[]{:S(2)}) collective-permute-start(bf16[160,2048]{1,0:T(8,128)(2,1)} %base_ref), channel_id=1, source_target_pairs={{0,2},{2,4},{4,6},{6,7},{7,5},{5,3},{3,1},{1,0},{8,10},{10,12},{12... | collective-permute-start | bytes 1966088 | tf_op jit(solution)/shard_map/ppermute | solution.py:777
  37.4 47.5 %collective-permute-start.9 = (bf16[512,2048]{1,0:T(8,128)(2,1)}, bf16[512,2048]{1,0:T(8,128)(2,1)S(1)}, u32[]{:S(2)}, u32[]{:S(2)}) collective-permute-start(bf16[512,2048]{1,0:T(8,128)(2,1)} %refs_1_.1), channel_id=1, source_target_pairs={{0,16},{8,24},{16,0},{24,8},{1,17},{9,25},{17,1},{25,9},{2,18},{10... | collective-permute-start | bytes 6291464 | tf_op jit(solution)/shard_map/ppermute | solution.py:739
  79.6 26.4 %collective-permute-start.3 = (bf16[512,2048]{1,0:T(8,128)(2,1)S(1)}, bf16[512,2048]{1,0:T(8,128)(2,1)S(1)}, u32[]{:S(2)}, u32[]{:S(2)}) collective-permute-start(bf16[512,2048]{1,0:T(8,128)(2,1)S(1)} %copy-done.15), channel_id=1, source_target_pairs={{0,8},{8,0},{16,24},{24,16},{1,9},{9,1},{17,25},{25,17},{2,10},{10... | collective-permute-start | bytes 6291464 | tf_op jit(solution)/shard_map/ppermute | solution.py:739
  86.2 27.2 %collective-permute-start.31 = (bf16[512,1024]{1,0:T(8,128)(2,1)S(1)}, bf16[512,1024]{1,0:T(8,128)(2,1)S(1)}, u32[]{:S(2)}, u32[]{:S(2)}) collective-permute-start(bf16[512,1024]{1,0:T(8,128)(2,1)S(1)} %pad_maximum_fusion.1.refs_6_.refs_4_.refs_2_), channel_id=1, source_target_pairs={{0,16},{8,24},{16,0},{24,8},{1,17},{9,25},{17,1},{25,9},{2,18},{10... | collective-permute-start | bytes 3145736 | tf_op jit(solution)/shard_map/ppermute | solution.py:739
  106.0 34.8 %collective-permute-start.32 = (bf16[512,2048]{1,0:T(8,128)(2,1)S(1)}, bf16[512,2048]{1,0:T(8,128)(2,1)}, u32[]{:S(2)}, u32[]{:S(2)}) collective-permute-start(bf16[512,2048]{1,0:T(8,128)(2,1)S(1)} %copy-done.13), channel_id=1, source_target_pairs={{0,8},{8,0},{16,24},{24,16},{1,9},{9,1},{17,25},{25,17},{2,10},{10... | collective-permute-start | bytes 6291464 | tf_op jit(solution)/shard_map/ppermute | solution.py:739
  114.2 26.6 %collective-permute-start.33 = (bf16[512,2048]{1,0:T(8,128)(2,1)S(1)}, bf16[512,2048]{1,0:T(8,128)(2,1)S(1)}, u32[]{:S(2)}, u32[]{:S(2)}) collective-permute-start(bf16[512,2048]{1,0:T(8,128)(2,1)S(1)} %place_rows.1.w2.refs_3_), channel_id=1, source_target_pairs={{0,8},{8,0},{16,24},{24,16},{1,9},{9,1},{17,25},{25,17},{2,10},{10... | collective-permute-start | bytes 6291464 | tf_op jit(solution)/shard_map/ppermute | solution.py:739
  140.0 28.3 %collective-permute-start.46 = (bf16[256,2048]{1,0:T(8,128)(2,1)}, bf16[256,2048]{1,0:T(8,128)(2,1)S(1)}, u32[]{:S(2)}, u32[]{:S(2)}) collective-permute-start(bf16[256,2048]{1,0:T(8,128)(2,1)} %constant_dynamic-slice_fusion.6), channel_id=1, source_target_pairs={{0,16},{8,24},{16,0},{24,8},{1,17},{9,25},{17,1},{25,9},{2,18},{10... | collective-permute-start | bytes 3145736 | tf_op jit(solution)/shard_map/ppermute | solution.py:739
  168.9 27.4 %collective-permute-start.39 = (bf16[160,2048]{1,0:T(8,128)(2,1)S(1)}, bf16[160,2048]{1,0:T(8,128)(2,1)S(1)}, u32[]{:S(2)}, u32[]{:S(2)}) collective-permute-start(bf16[160,2048]{1,0:T(8,128)(2,1)S(1)} %collective-permute-done.37.refs_0_), channel_id=1, source_target_pairs={{0,2},{2,4},{4,6},{6,7},{7,5},{5,3},{3,1},{1,0},{8,10},{10,12},{12... | collective-permute-start | bytes 1966088 | tf_op jit(solution)/shard_map/ppermute | solution.py:777
  170.5 25.8 %collective-permute-start.40 = (bf16[160,2048]{1,0:T(8,128)(2,1)S(1)}, bf16[160,2048]{1,0:T(8,128)(2,1)S(1)}, u32[]{:S(2)}, u32[]{:S(2)}) collective-permute-start(bf16[160,2048]{1,0:T(8,128)(2,1)S(1)} %collective-permute-done.38.refs_2_), channel_id=1, source_target_pairs={{0,1},{2,0},{4,2},{6,4},{7,6},{5,7},{3,5},{1,3},{8,9},{10,8},{12,1... | collective-permute-start | bytes 1966088 | tf_op jit(solution)/shard_map/ppermute | solution.py:777
  170.9 29.5 %collective-permute-start.50 = (bf16[160,2048]{1,0:T(8,128)(2,1)S(1)}, bf16[160,2048]{1,0:T(8,128)(2,1)S(1)}, u32[]{:S(2)}, u32[]{:S(2)}) collective-permute-start(bf16[160,2048]{1,0:T(8,128)(2,1)S(1)} %copy-done.72), channel_id=1, source_target_pairs={{0,2},{2,4},{4,6},{6,7},{7,5},{5,3},{3,1},{1,0},{8,10},{10,12},{12... | collective-permute-start | bytes 1966088 | tf_op jit(solution)/shard_map/ppermute | solution.py:777
  173.9 28.2 %collective-permute-start.51 = (bf16[160,2048]{1,0:T(8,128)(2,1)}, bf16[160,2048]{1,0:T(8,128)(2,1)S(1)}, u32[]{:S(2)}, u32[]{:S(2)}) collective-permute-start(bf16[160,2048]{1,0:T(8,128)(2,1)} %collective-permute-done.35.refs_3_), channel_id=1, source_target_pairs={{0,1},{2,0},{4,2},{6,4},{7,6},{5,7},{3,5},{1,3},{8,9},{10,8},{12,1... | collective-permute-start | bytes 1966088 | tf_op jit(solution)/shard_map/ppermute | solution.py:777
  287.2 47.4 %collective-permute-start.72 = (bf16[512,2048]{1,0:T(8,128)(2,1)}, bf16[512,2048]{1,0:T(8,128)(2,1)}, u32[]{:S(2)}, u32[]{:S(2)}) collective-permute-start(bf16[512,2048]{1,0:T(8,128)(2,1)} %tn_blocks.17), channel_id=1, source_target_pairs={{0,16},{8,24},{16,0},{24,8},{1,17},{9,25},{17,1},{25,9},{2,18},{10... | collective-permute-start | bytes 6291464 | tf_op jit(solution)/shard_map/ppermute | solution.py:739
  298.8 35.8 %collective-permute-start.70 = (bf16[512,1024]{1,0:T(8,128)(2,1)}, bf16[512,1024]{1,0:T(8,128)(2,1)S(1)}, u32[]{:S(2)}, u32[]{:S(2)}) collective-permute-start(bf16[512,1024]{1,0:T(8,128)(2,1)} %copy-done.86), channel_id=1, source_target_pairs={{0,8},{8,0},{16,24},{24,16},{1,9},{9,1},{17,25},{25,17},{2,10},{10... | collective-permute-start | bytes 3145736 | tf_op jit(solution)/shard_map/ppermute | solution.py:739
  298.9 35.7 %collective-permute-start.71 = (bf16[512,1024]{1,0:T(8,128)(2,1)}, bf16[512,1024]{1,0:T(8,128)(2,1)}, u32[]{:S(2)}, u32[]{:S(2)}) collective-permute-start(bf16[512,1024]{1,0:T(8,128)(2,1)} %copy-done.85), channel_id=1, source_target_pairs={{0,8},{8,0},{16,24},{24,16},{1,9},{9,1},{17,25},{25,17},{2,10},{10... | collective-permute-start | bytes 3145736 | tf_op jit(solution)/shard_map/ppermute | solution.py:739
  342.3 60.0 %all-to-all-start = ((bf16[8,64,2048]{2,1,0:T(8,128)(2,1)}), bf16[8,64,2048]{2,1,0:T(8,128)(2,1)}, u32[]{:S(2)}, u32[]{:S(2)}) async-start(bf16[8,64,2048]{2,1,0:T(8,128)(2,1)} %bitcast.22), calls=%async_computation | async-start | bytes 4194304 | tf_op jit(solution)/shard_map/all_to_all | solution.py:1105
  353.8 36.4 %collective-permute-start.76 = (bf16[512,1024]{1,0:T(8,128)(2,1)}, bf16[512,1024]{1,0:T(8,128)(2,1)S(1)}, u32[]{:S(2)}, u32[]{:S(2)}) collective-permute-start(bf16[512,1024]{1,0:T(8,128)(2,1)} %get-tuple-element.637), channel_id=1, source_target_pairs={{0,8},{8,0},{16,24},{24,16},{1,9},{9,1},{17,25},{25,17},{2,10},{10... | collective-permute-start | bytes 3145736 | tf_op jit(solution)/shard_map/ppermute | solution.py:739
  353.8 36.4 %collective-permute-start.77 = (bf16[512,1024]{1,0:T(8,128)(2,1)S(1)}, bf16[512,1024]{1,0:T(8,128)(2,1)S(1)}, u32[]{:S(2)}, u32[]{:S(2)}) collective-permute-start(bf16[512,1024]{1,0:T(8,128)(2,1)S(1)} %get-tuple-element.638), channel_id=1, source_target_pairs={{0,8},{8,0},{16,24},{24,16},{1,9},{9,1},{17,25},{25,17},{2,10},{10... | collective-permute-start | bytes 3145736 | tf_op jit(solution)/shard_map/ppermute | solution.py:739
  393.3 45.3 %collective-permute-start.88 = (bf16[512,2048]{1,0:T(8,128)(2,1)}, bf16[512,2048]{1,0:T(8,128)(2,1)}, u32[]{:S(2)}, u32[]{:S(2)}) collective-permute-start(bf16[512,2048]{1,0:T(8,128)(2,1)} %tn_blocks.21), channel_id=1, source_target_pairs={{0,16},{8,24},{16,0},{24,8},{1,17},{9,25},{17,1},{25,9},{2,18},{10... | collective-permute-start | bytes 6291464 | tf_op jit(solution)/shard_map/ppermute | solution.py:739
  469.2 49.3 %collective-permute-start.107 = (bf16[512,2048]{1,0:T(8,128)(2,1)}, bf16[512,2048]{1,0:T(8,128)(2,1)}, u32[]{:S(2)}, u32[]{:S(2)}) collective-permute-start(bf16[512,2048]{1,0:T(8,128)(2,1)} %copy-done.52), channel_id=1, source_target_pairs={{0,16},{8,24},{16,0},{24,8},{1,17},{9,25},{17,1},{25,9},{2,18},{10... | collective-permute-start | bytes 6291464 | tf_op jit(solution)/shard_map/ppermute | solution.py:739
  518.5 36.7 %collective-permute-start.112 = (bf16[512,512]{1,0:T(8,128)(2,1)}, bf16[512,512]{1,0:T(8,128)(2,1)}, u32[]{:S(2)}, u32[]{:S(2)}) collective-permute-start(bf16[512,512]{1,0:T(8,128)(2,1)} %get-tuple-element.717), channel_id=1, source_target_pairs={{0,8},{8,0},{16,24},{24,16},{1,9},{9,1},{17,25},{25,17},{2,10},{10... | collective-permute-start | bytes 1572872 | tf_op jit(solution)/shard_map/ppermute | solution.py:739
  518.5 36.9 %collective-permute-start.113 = (bf16[512,512]{1,0:T(8,128)(2,1)}, bf16[512,512]{1,0:T(8,128)(2,1)}, u32[]{:S(2)}, u32[]{:S(2)}) collective-permute-start(bf16[512,512]{1,0:T(8,128)(2,1)} %get-tuple-element.718), channel_id=1, source_target_pairs={{0,8},{8,0},{16,24},{24,16},{1,9},{9,1},{17,25},{25,17},{2,10},{10... | collective-permute-start | bytes 1572872 | tf_op jit(solution)/shard_map/ppermute | solution.py:739
  519.1 35.9 %collective-permute-start.114 = (bf16[512,1024]{1,0:T(8,128)(2,1)S(1)}, bf16[512,1024]{1,0:T(8,128)(2,1)}, u32[]{:S(2)}, u32[]{:S(2)}) collective-permute-start(bf16[512,1024]{1,0:T(8,128)(2,1)S(1)} %copy-done.67), channel_id=1, source_target_pairs={{0,16},{8,24},{16,0},{24,8},{1,17},{9,25},{17,1},{25,9},{2,18},{10... | collective-permute-start | bytes 3145736 | tf_op jit(solution)/shard_map/ppermute | solution.py:739
  543.0 32.3 %all-to-all-start.1 = ((bf16[32,2,64]{2,1,0:T(2,128)(2,1)}), bf16[32,2,64]{2,1,0:T(2,128)(2,1)S(1)}, u32[]{:S(2)}, u32[]{:S(2)}) async-start(bf16[32,2,64]{2,1,0:T(2,128)(2,1)} %maximum_bitcast_fusion), calls=%async_computation.1 | async-start | bytes 32768 | tf_op jit(solution)/shard_map/all_to_all | solution.py:1190
  (223 other events, 2887.0 us)

commit v5 on v4

--- a/solution.py
+++ b/solution.py
@@ -1155,30 +1155,39 @@
     grad_kv.rest(1)
     of_query.second()
     grad_kv.rest(1)
-    of_out.settle()
-    out_within = of_out.last(BF)
-    grad_kv.rest()
-    grad_kv = added(grad_kv.take())
-    out_sums = scatter_rows(out_within)
-    out_sums.send()
 
     def y_contrib(r):
         start = slot_rel.index(r) * token_rows
         return y_rows[start : start + token_rows]
 
+    def spread_out():
+        if crossed:
+            return order.run(spread, scalars, gate_up_all, units=units, tile=tile)
+        both = gate_up_all.reshape(n, rows, 2, 4, units).transpose(2, 1, 3, 0, 4)
+        both = xor_blocks(both, f, 2).reshape(2, rows, n * width).astype(F32)
+        return order.done((both[0], both[1]))
+
     y_sums = Scatter(order, y_contrib, n)
     y_sums.send()
+    down_grad = of_down.last(F32)
+    of_out.settle()
+    out_sums = scatter_rows(of_out.last(BF))
+    grad_kv.rest()
+    grad_kv = added(grad_kv.take())
+    out_sums.send()
+    y_sums.rest(1)
     grad_kv = turn_back(grad_kv, cosine, sine).astype(BF)
     grad_key, grad_value = deinterleave(grad_kv)
     grad_kv = jnp.concatenate([grad_key, grad_value], axis=1)
     of_kv = Product(hidden_one, grad_kv, 1.5)
     of_kv.first()
+    gate_grad, up_grad = spread_out()
     out_sums.rest(1)
+    y_sums.rest(1)
     grad_hidden_one = order.run(
         back_project, [grad_key, grad_value], [weight_k, weight_v], base=grad_hidden_one, kind=F32, micros=3
     )
     of_kv.second()
-    y_sums.rest(1)
     out_sums.rest(1)
     tokens_grad, gain_one_term = order.run(
         norm_back, scalars, tokens, gain_one, grad_residual, [grad_hidden_one], rounded=False
@@ -1188,31 +1197,26 @@
     gain_terms = xor_blocks(jnp.concatenate([gain_one_term, gain_two_term], axis=0), f, 1)
     gain_terms = gain_terms.astype(BF).reshape(2, 4 * n, model // (4 * n)).transpose(1, 0, 2)
     gain_terms = lax.all_to_all(gain_terms, ("fsdp", "ctx"), 0, 0, tiled=False)
+    of_query.settle()
+    query_sums = scatter_rows(of_query.last(BF))
+    y_sums.rest()
+    layer_out = order.done((residual + added(y_sums.take())).astype(BF))
+    query_sums.send()
     out_sums.rest()
     out_grad = order.done(added(out_sums.take()))
-    y_sums.rest(1)
-    of_query.settle()
-    query_sums = scatter_rows(of_query.last(BF))
-    query_sums.send()
-    y_sums.rest()
-    layer_out = order.done((residual + added(y_sums.take())).astype(BF))
-    query_sums.rest(1)
-    if crossed:
-        gate_grad, up_grad = order.run(spread, scalars, gate_up_all, units=units, tile=tile)
-    else:
-        gate_up_all = gate_up_all.reshape(n, rows, 2, 4, units).transpose(2, 1, 3, 0, 4)
-        gate_up_all = xor_blocks(gate_up_all, f, 2).reshape(2, rows, n * width).astype(F32)
-        gate_grad, up_grad = order.done((gate_up_all[0], gate_up_all[1]))
+    gain_terms = order.take(gain_terms)
     of_kv.settle()
     kv_sums = scatter_rows(of_kv.last(BF))
+    query_sums.rest(1)
     kv_sums.send()
     query_sums.rest(1)
-    down_grad = of_down.last(F32)
+    kv_sums.rest(1)
+    query_sums.rest(1)
     kv_sums.rest(1)
     query_sums.rest()
-    gain_terms = order.take(gain_terms)
+    query_sums = query_sums.take()
     kv_sums.rest(1)
-    query_grad = order.done(added(query_sums.take()))
+    query_grad = order.done(added(query_sums))
     kv_sums.rest()
     kv_grad = order.done(added(kv_sums.take()))
     gain_grads = jnp.sum(gain_terms.astype(F32), axis=0)

time: 597 us -> 584 us (0.978)
  waiting for transfers between devices: 148 us -> 140 us
    ppermute x80, waiting for transfers between devices: 132 us -> 117 us  [ring_shift(): lax.ppermute(value, 'ctx', [(order[i], order[(i + step) % n]) for i in ra...]
    ppermute x49, waiting for transfers between devices: 16.3 us -> 23.1 us  [swap_fsdp(): return lax.ppermute(value, 'fsdp', [(i, i ^ d) for i in range(4)])]
    unnamed x236 -> x246, local copies, waits for them, and re-layouts: 40 us -> 42.2 us
  transfers between devices with their start and end apart: 131 -> 131, of which waited for: 49 -> 49; matrix products, arithmetic and copies ran while one was open for 10% -> 9% of each run, Pallas kernels for 35% -> 35%
where the time goes in v5:
time: 584 us; the launch traced here: 577 us
  Pallas kernels  222 us (38%)
  waiting for transfers between devices  140 us (24%)
  starting transfers between devices  112 us (19%)
  local copies, waits for them, and re-layouts  61.3 us (10%)
  other arithmetic  38.5 us (7%)
    ppermute x80, waiting for transfers between devices, ring_shift(): lax.ppermute(value, 'ctx', [(order[i], order[(i + step) % n]) for i in ra...  117 us
    ppermute x80, starting transfers between devices, ring_shift(): lax.ppermute(value, 'ctx', [(order[i], order[(i + step) % n]) for i in ra...  85.4 us
    pallas_call x15, Pallas kernels, tn_blocks(): pl.pallas_call(functools.partial(tn_kernel, windows, outs), grid=(len(blo...  71.7 us
    pallas_call x4, Pallas kernels, feed(): pl.pallas_call(functools.partial(feed_kernel, m, len(kept), crossed), gri...  59.4 us
    unnamed x246, local copies, waits for them, and re-layouts  42.2 us
    pallas_call x2, Pallas kernels, attention_backward(): pl.pallas_call(functools.partial(backward_kernel, n, group, ends, first),...  27.5 us
    ppermute x49, waiting for transfers between devices, swap_fsdp(): return lax.ppermute(value, 'fsdp', [(i, i ^ d) for i in range(4)])  23.1 us
    ppermute x49, starting transfers between devices, swap_fsdp(): return lax.ppermute(value, 'fsdp', [(i, i ^ d) for i in range(4)])  19.6 us
  transfers between devices with their start and end apart: 131, of which 49 were waited for; matrix products, arithmetic and copies ran while one was open for 9% of the time, Pallas kernels for 35%

profile of v5, /device:TPU:0, one launch (start us, length us, event | category | flops | bytes accessed | tf_op | source)
XLA Modules:
  0.0 576.7 jit_solution(8885853398794494408)
XLA Ops:
  19.7 6.7 %collective-permute-done.8.refs_2_.refs_4_ = bf16[512,512]{1,0:T(8,128)(2,1)S(1)} collective-permute-done((bf16[512,512]{1,0:T(8,128)(2,1)}, bf16[512,512]{1,0:T(8,128)(2,1)S(1)}, u32[]{:S(2)}, u32[]{:S(2)}) %collective-permute-start.8) | collective-permute-done | bytes 524320 | tf_op jit(solution)/shard_map/ppermute | solution.py:739
  27.9 7.4 %collective-permute-done.6.refs_2_ = bf16[64,2048]{1,0:T(8,128)(2,1)S(1)} collective-permute-done((bf16[64,2048]{1,0:T(8,128)(2,1)S(1)}, bf16[64,2048]{1,0:T(8,128)(2,1)S(1)}, u32[]{:S(2)}, u32[]{:S(2)}) %collective-permute-start.6) | collective-permute-done | bytes 262176 | tf_op jit(solution)/shard_map/ppermute | solution.py:777
  59.4 8.1 %collective-permute-done.20.rest_2_ = bf16[160,1024]{1,0:T(8,128)(2,1)S(1)} collective-permute-done((bf16[160,1024]{1,0:T(8,128)(2,1)S(1)}, bf16[160,1024]{1,0:T(8,128)(2,1)S(1)}, u32[]{:S(2)}, u32[]{:S(2)}) %collective-permute-start.20) | collective-permute-done | bytes 327712 | tf_op jit(solution)/shard_map/ppermute | solution.py:777
  72.8 6.6 %collective-permute-done.22.rest_1_ = bf16[160,1024]{1,0:T(8,128)(2,1)S(1)} collective-permute-done((bf16[160,1024]{1,0:T(8,128)(2,1)S(1)}, bf16[160,1024]{1,0:T(8,128)(2,1)S(1)}, u32[]{:S(2)}, u32[]{:S(2)}) %collective-permute-start.22) | collective-permute-done | bytes 327712 | tf_op jit(solution)/shard_map/ppermute | solution.py:777
  89.2 7.8 %collective-permute-done.25.rest_0_ = bf16[160,1024]{1,0:T(8,128)(2,1)S(1)} collective-permute-done((bf16[160,1024]{1,0:T(8,128)(2,1)S(1)}, bf16[160,1024]{1,0:T(8,128)(2,1)S(1)}, u32[]{:S(2)}, u32[]{:S(2)}) %collective-permute-start.25) | collective-permute-done | bytes 327712 | tf_op jit(solution)/shard_map/ppermute | solution.py:777
  117.8 16.5 %attention_forward.1 = (bf16[160,2048]{1,0:T(8,128)(2,1)S(1)}, f32[160,128]{1,0:T(8,128)S(1)}) custom-call(s32[23]{0:T(128)S(1)} %pad_add_fusion.f_ref.sc, bf16[160,2048]{1,0:T(8,128)(2,1)S(1)} %project.3.q_ref, bf16[160,1024]{1,0:T(8,128)(2,1)S(1)} %collective-permute-done.25.rest_0_, bf16[160,1024]{1,0:T(8,128)(2,1)S(1)} %collective-permute-done.22.rest_1_, ...), custom_call_target="tpu_custom_call" | custom-call | flops 180000000 | tf_op jit(solution)/shard_map/attention_forward/pallas_call | solution.py:131
  141.7 6.7 %out_project.1 = (f32[160,2048]{1,0:T(8,128)S(1)}, bf16[160,2048]{1,0:T(8,128)(2,1)S(1)}) custom-call(s32[23]{0:T(128)S(1)} %pad_add_fusion.f_ref.sc, bf16[160,2048]{1,0:T(8,128)(2,1)S(1)} %get-tuple-element.714.o_ref.left_ref, bf16[160,2048]{1,0:T(8,128)(2,1)S(1)} %copy-done.37, f32[1,2048]{1,0:T(1,128)S(1)} %get-tuple-element.611.gain_ref, ...), custom_call_target="tpu_custom_call" | custom-call | flops 60000000 | tf_op jit(solution)/shard_map/out_project/pallas_call | solution.py:381
  152.6 12.9 %collective-permute-done.37.refs_0_ = bf16[160,2048]{1,0:T(8,128)(2,1)S(1)} collective-permute-done((bf16[160,2048]{1,0:T(8,128)(2,1)S(1)}, bf16[160,2048]{1,0:T(8,128)(2,1)S(1)}, u32[]{:S(2)}, u32[]{:S(2)}) %collective-permute-start.37) | collective-permute-done | bytes 655392 | tf_op jit(solution)/shard_map/ppermute | solution.py:777
  176.8 19.5 %feed.4 = (bf16[1280,2048]{1,0:T(8,128)(2,1)}, bf16[1280,2048]{1,0:T(8,128)(2,1)}, bf16[1280,1024]{1,0:T(8,128)(2,1)}, bf16[1280,2048]{1,0:T(8,128)(2,1)}, bf16[480,2048]{1,0:T(8,128)(2,1)}) custom-call(bf16[160,2048]{1,0:T(8,128)(2,1)S(1)} %collective-permute-done.37.refs_0_, bf16[160,2048]{1,0:T(8,128)(2,1)S(1)} %copy-done.73, ...), custom_call_target="tpu_custom_call" | custom-call | flops 200000000 | tf_op jit(solution)/shard_map/feed/pallas_call | solution.py:560
  204.2 14.5 %feed.5 = (bf16[1280,2048]{1,0:T(8,128)(2,1)}, bf16[1280,2048]{1,0:T(8,128)(2,1)}, bf16[1280,1024]{1,0:T(8,128)(2,1)}, bf16[1280,2048]{1,0:T(8,128)(2,1)}, bf16[320,2048]{1,0:T(8,128)(2,1)}) custom-call(bf16[160,2048]{1,0:T(8,128)(2,1)S(1)} %collective-permute-done.39.refs_0_, ...), custom_call_target="tpu_custom_call", output_to_operand_aliasing={{0}: (13, {}), {1}: (14, {}), {2}: (15, {}), {3}: (16, {})} | custom-call | flops 160000000 | tf_op jit(solution)/shard_map/feed/pallas_call | solution.py:560
  223.1 14.5 %feed.6 = (bf16[1280,2048]{1,0:T(8,128)(2,1)}, bf16[1280,2048]{1,0:T(8,128)(2,1)}, bf16[1280,1024]{1,0:T(8,128)(2,1)}, bf16[1280,2048]{1,0:T(8,128)(2,1)}, bf16[320,2048]{1,0:T(8,128)(2,1)}) custom-call(bf16[160,2048]{1,0:T(8,128)(2,1)S(1)} %collective-permute-done.48.refs_0_, ...), custom_call_target="tpu_custom_call", output_to_operand_aliasing={{0}: (13, {}), {1}: (14, {}), {2}: (15, {}), {3}: (16, {})} | custom-call | flops 160000000 | tf_op jit(solution)/shard_map/feed/pallas_call | solution.py:560
  238.8 11.0 %feed.7 = (bf16[1280,2048]{1,0:T(8,128)(2,1)}, bf16[1280,2048]{1,0:T(8,128)(2,1)}, bf16[1280,1024]{1,0:T(8,128)(2,1)}, bf16[1280,2048]{1,0:T(8,128)(2,1)}, bf16[160,2048]{1,0:T(8,128)(2,1)S(1)}) custom-call(bf16[160,2048]{1,0:T(8,128)(2,1)S(1)} %pad_maximum_fusion.3.refs_0_, ...), custom_call_target="tpu_custom_call", output_to_operand_aliasing={{0}: (11, {}), {1}: (12, {}), {2}: (13, {}), {3}: (14, {})} | custom-call | flops 120000000 | tf_op jit(solution)/shard_map/feed/pallas_call | solution.py:560
  256.9 10.0 %tn_blocks.15 = (bf16[512,1024]{1,0:T(8,128)(2,1)S(1)}, bf16[512,1024]{1,0:T(8,128)(2,1)S(1)}, bf16[512,1024]{1,0:T(8,128)(2,1)S(1)}, bf16[512,1024]{1,0:T(8,128)(2,1)S(1)}) custom-call(bf16[1280,2048]{1,0:T(8,128)(2,1)S(1)} %copy-done, bf16[1280,2048]{1,0:T(8,128)(2,1)S(1)} %copy-done.1), custom_call_target="tpu_custom_call" | custom-call | flops 100000000 | tf_op jit(solution)/shard_map/tn_blocks/pallas_call | solution.py:693
  273.3 7.6 %tn_blocks.16 = (bf16[256,1024]{1,0:T(8,128)(2,1)}, bf16[256,1024]{1,0:T(8,128)(2,1)}, bf16[256,1024]{1,0:T(8,128)(2,1)}, bf16[256,1024]{1,0:T(8,128)(2,1)}) custom-call(bf16[1280,1024]{1,0:T(8,128)(2,1)S(1)} %copy-done.5, bf16[1280,2048]{1,0:T(8,128)(2,1)S(1)} %copy-done.3), custom_call_target="tpu_custom_call" | custom-call | flops 60000000 | tf_op jit(solution)/shard_map/tn_blocks/pallas_call | solution.py:693
  280.9 5.7 tn_blocks.17
  291.5 6.1 %down_rows.1 = bf16[1280,2048]{1,0:T(8,128)(2,1)S(1)} custom-call(bf16[1280,1024]{1,0:T(8,128)(2,1)S(1)} %copy-done.5, bf16[1024,2048]{1,0:T(8,128)(2,1)S(1)} %copy-done.4), custom_call_target="tpu_custom_call" | custom-call | flops 80000000 | tf_op jit(solution)/shard_map/down_rows/pallas_call | solution.py:590
  311.8 11.5 %collective-permute-done.68.rest_1_ = bf16[160,2048]{1,0:T(8,128)(2,1)S(1)} collective-permute-done((bf16[160,2048]{1,0:T(8,128)(2,1)S(1)}, bf16[160,2048]{1,0:T(8,128)(2,1)S(1)}, u32[]{:S(2)}, u32[]{:S(2)}) %collective-permute-start.68) | collective-permute-done | bytes 655392 | tf_op jit(solution)/shard_map/ppermute | solution.py:777
  334.0 6.5 %tn_blocks.19 = bf16[512,2048]{1,0:T(8,128)(2,1)S(1)} custom-call(bf16[1280,2048]{1,0:T(8,128)(2,1)S(1)} %bitcast.17, bf16[1280,2048]{1,0:T(8,128)(2,1)S(1)} %copy-done.2, bf16[512,1024]{1,0:T(8,128)(2,1)} %collective-permute-done.70.refs_0_, bf16[512,1024]{1,0:T(8,128)(2,1)} %collective-permute-done.71.refs_1_, ...), custom_call_target="tpu_custom_call" | custom-call | flops 50000000 | tf_op jit(solution)/shard_map/tn_blocks/pallas_call | solution.py:693
  346.9 5.6 tn_blocks.20
  353.0 13.5 %attention_backward.2 = (bf16[160,1024]{1,0:T(8,128)(2,1)}, bf16[1280,512]{1,0:T(8,128)(2,1)}) custom-call(s32[23]{0:T(128)} %copy-done.84, bf16[160,2048]{1,0:T(8,128)(2,1)} %copy-done.12, bf16[160,2048]{1,0:T(8,128)(2,1)} %copy-done.35, f32[160,128]{1,0:T(8,128)} %copy-done.77, f32[160,128]{1,0:T(8,128)} %copy-done.64, f32[160,128]{1,0:T(8,128)} %copy-done.33, ...), custom_call_target="tpu_custom_call" | custom-call | flops 260000000 | tf_op jit(solution)/shard_map/attention_backward/pallas_call | solution.py:236
  370.2 14.0 %attention_backward.3 = (bf16[160,1024]{1,0:T(8,128)(2,1)}, bf16[1280,512]{1,0:T(8,128)(2,1)}) custom-call(s32[23]{0:T(128)} %copy-done.84, bf16[160,2048]{1,0:T(8,128)(2,1)} %copy-done.12, bf16[160,2048]{1,0:T(8,128)(2,1)} %copy-done.35, f32[160,128]{1,0:T(8,128)} %copy-done.77, f32[160,128]{1,0:T(8,128)} %copy-done.64, f32[160,128]{1,0:T(8,128)} %copy-done.33, ...), custom_call_target="tpu_custom_call" | custom-call | flops 260000000 | tf_op jit(solution)/shard_map/attention_backward/pallas_call | solution.py:236
  418.8 5.8 %collective-permute-done.81 = bf16[160,1024]{1,0:T(8,128)(2,1)} collective-permute-done((bf16[160,1024]{1,0:T(8,128)(2,1)S(1)}, bf16[160,1024]{1,0:T(8,128)(2,1)}, u32[]{:S(2)}, u32[]{:S(2)}) %collective-permute-start.81) | collective-permute-done | bytes 327712 | tf_op jit(solution)/shard_map/ppermute | solution.py:777
  462.8 6.2 %spread.1 = (f32[64,8192]{1,0:T(8,128)}, f32[64,8192]{1,0:T(8,128)}) custom-call(s32[23]{0:T(128)S(1)} %copy-done.85, bf16[8,64,2048]{2,1,0:T(8,128)(2,1)} %all-to-all-done.all_ref), custom_call_target="tpu_custom_call" | custom-call | flops 40000000 | tf_op jit(solution)/shard_map/spread/pallas_call | solution.py:726
  529.3 7.0 %collective-permute-done.114.refs_2_ = bf16[512,1024]{1,0:T(8,128)(2,1)} collective-permute-done((bf16[512,1024]{1,0:T(8,128)(2,1)}, bf16[512,1024]{1,0:T(8,128)(2,1)}, u32[]{:S(2)}, u32[]{:S(2)}) %collective-permute-start.114) | collective-permute-done | bytes 1048608 | tf_op jit(solution)/shard_map/ppermute | solution.py:739
  (636 shorter events, 342.4 us)
Async XLA Ops:
  8.1 29.3 %collective-permute-start.4 = (bf16[512,512]{1,0:T(8,128)(2,1)}, bf16[512,512]{1,0:T(8,128)(2,1)}, u32[]{:S(2)}, u32[]{:S(2)}) collective-permute-start(bf16[512,512]{1,0:T(8,128)(2,1)} %refs_6_), channel_id=1, source_target_pairs={{0,16},{8,24},{16,0},{24,8},{1,17},{9,25},{17,1},{25,9},{2,18},{10... | collective-permute-start | bytes 1572872 | tf_op jit(solution)/shard_map/ppermute | solution.py:739
  12.1 30.1 %collective-permute-start.18 = (bf16[160,2048]{1,0:T(8,128)(2,1)}, bf16[160,2048]{1,0:T(8,128)(2,1)}, u32[]{:S(2)}, u32[]{:S(2)}) collective-permute-start(bf16[160,2048]{1,0:T(8,128)(2,1)} %base_ref), channel_id=1, source_target_pairs={{0,2},{2,4},{4,6},{6,7},{7,5},{5,3},{3,1},{1,0},{8,10},{10,12},{12... | collective-permute-start | bytes 1966088 | tf_op jit(solution)/shard_map/ppermute | solution.py:777
  37.4 47.5 %collective-permute-start.9 = (bf16[512,2048]{1,0:T(8,128)(2,1)}, bf16[512,2048]{1,0:T(8,128)(2,1)S(1)}, u32[]{:S(2)}, u32[]{:S(2)}) collective-permute-start(bf16[512,2048]{1,0:T(8,128)(2,1)} %refs_1_.1), channel_id=1, source_target_pairs={{0,16},{8,24},{16,0},{24,8},{1,17},{9,25},{17,1},{25,9},{2,18},{10... | collective-permute-start | bytes 6291464 | tf_op jit(solution)/shard_map/ppermute | solution.py:739
  79.4 26.3 %collective-permute-start.3 = (bf16[512,2048]{1,0:T(8,128)(2,1)S(1)}, bf16[512,2048]{1,0:T(8,128)(2,1)S(1)}, u32[]{:S(2)}, u32[]{:S(2)}) collective-permute-start(bf16[512,2048]{1,0:T(8,128)(2,1)S(1)} %copy-done.18), channel_id=1, source_target_pairs={{0,8},{8,0},{16,24},{24,16},{1,9},{9,1},{17,25},{25,17},{2,10},{10... | collective-permute-start | bytes 6291464 | tf_op jit(solution)/shard_map/ppermute | solution.py:739
  86.2 27.0 %collective-permute-start.31 = (bf16[512,1024]{1,0:T(8,128)(2,1)S(1)}, bf16[512,1024]{1,0:T(8,128)(2,1)S(1)}, u32[]{:S(2)}, u32[]{:S(2)}) collective-permute-start(bf16[512,1024]{1,0:T(8,128)(2,1)S(1)} %pad_maximum_fusion.1.refs_6_.refs_4_.refs_2_), channel_id=1, source_target_pairs={{0,16},{8,24},{16,0},{24,8},{1,17},{9,25},{17,1},{25,9},{2,18},{10... | collective-permute-start | bytes 3145736 | tf_op jit(solution)/shard_map/ppermute | solution.py:739
  105.7 35.1 %collective-permute-start.32 = (bf16[512,2048]{1,0:T(8,128)(2,1)S(1)}, bf16[512,2048]{1,0:T(8,128)(2,1)}, u32[]{:S(2)}, u32[]{:S(2)}) collective-permute-start(bf16[512,2048]{1,0:T(8,128)(2,1)S(1)} %copy-done.16), channel_id=1, source_target_pairs={{0,8},{8,0},{16,24},{24,16},{1,9},{9,1},{17,25},{25,17},{2,10},{10... | collective-permute-start | bytes 6291464 | tf_op jit(solution)/shard_map/ppermute | solution.py:739
  113.9 26.9 %collective-permute-start.33 = (bf16[512,2048]{1,0:T(8,128)(2,1)S(1)}, bf16[512,2048]{1,0:T(8,128)(2,1)S(1)}, u32[]{:S(2)}, u32[]{:S(2)}) collective-permute-start(bf16[512,2048]{1,0:T(8,128)(2,1)S(1)} %place_rows.1.w2.refs_3_), channel_id=1, source_target_pairs={{0,8},{8,0},{16,24},{24,16},{1,9},{9,1},{17,25},{25,17},{2,10},{10... | collective-permute-start | bytes 6291464 | tf_op jit(solution)/shard_map/ppermute | solution.py:739
  139.7 28.5 %collective-permute-start.46 = (bf16[256,2048]{1,0:T(8,128)(2,1)}, bf16[256,2048]{1,0:T(8,128)(2,1)S(1)}, u32[]{:S(2)}, u32[]{:S(2)}) collective-permute-start(bf16[256,2048]{1,0:T(8,128)(2,1)} %constant_dynamic-slice_fusion.6), channel_id=1, source_target_pairs={{0,16},{8,24},{16,0},{24,8},{1,17},{9,25},{17,1},{25,9},{2,18},{10... | collective-permute-start | bytes 3145736 | tf_op jit(solution)/shard_map/ppermute | solution.py:739
  168.8 27.5 %collective-permute-start.39 = (bf16[160,2048]{1,0:T(8,128)(2,1)S(1)}, bf16[160,2048]{1,0:T(8,128)(2,1)S(1)}, u32[]{:S(2)}, u32[]{:S(2)}) collective-permute-start(bf16[160,2048]{1,0:T(8,128)(2,1)S(1)} %collective-permute-done.37.refs_0_), channel_id=1, source_target_pairs={{0,2},{2,4},{4,6},{6,7},{7,5},{5,3},{3,1},{1,0},{8,10},{10,12},{12... | collective-permute-start | bytes 1966088 | tf_op jit(solution)/shard_map/ppermute | solution.py:777
  170.4 25.9 %collective-permute-start.40 = (bf16[160,2048]{1,0:T(8,128)(2,1)S(1)}, bf16[160,2048]{1,0:T(8,128)(2,1)S(1)}, u32[]{:S(2)}, u32[]{:S(2)}) collective-permute-start(bf16[160,2048]{1,0:T(8,128)(2,1)S(1)} %collective-permute-done.38.refs_2_), channel_id=1, source_target_pairs={{0,1},{2,0},{4,2},{6,4},{7,6},{5,7},{3,5},{1,3},{8,9},{10,8},{12,1... | collective-permute-start | bytes 1966088 | tf_op jit(solution)/shard_map/ppermute | solution.py:777
  170.9 29.5 %collective-permute-start.50 = (bf16[160,2048]{1,0:T(8,128)(2,1)S(1)}, bf16[160,2048]{1,0:T(8,128)(2,1)S(1)}, u32[]{:S(2)}, u32[]{:S(2)}) collective-permute-start(bf16[160,2048]{1,0:T(8,128)(2,1)S(1)} %copy-done.75), channel_id=1, source_target_pairs={{0,2},{2,4},{4,6},{6,7},{7,5},{5,3},{3,1},{1,0},{8,10},{10,12},{12... | collective-permute-start | bytes 1966088 | tf_op jit(solution)/shard_map/ppermute | solution.py:777
  173.9 28.2 %collective-permute-start.51 = (bf16[160,2048]{1,0:T(8,128)(2,1)}, bf16[160,2048]{1,0:T(8,128)(2,1)S(1)}, u32[]{:S(2)}, u32[]{:S(2)}) collective-permute-start(bf16[160,2048]{1,0:T(8,128)(2,1)} %collective-permute-done.35.refs_3_), channel_id=1, source_target_pairs={{0,1},{2,0},{4,2},{6,4},{7,6},{5,7},{3,5},{1,3},{8,9},{10,8},{12,1... | collective-permute-start | bytes 1966088 | tf_op jit(solution)/shard_map/ppermute | solution.py:777
  286.7 47.4 %collective-permute-start.72 = (bf16[512,2048]{1,0:T(8,128)(2,1)}, bf16[512,2048]{1,0:T(8,128)(2,1)}, u32[]{:S(2)}, u32[]{:S(2)}) collective-permute-start(bf16[512,2048]{1,0:T(8,128)(2,1)} %tn_blocks.17), channel_id=1, source_target_pairs={{0,16},{8,24},{16,0},{24,8},{1,17},{9,25},{17,1},{25,9},{2,18},{10... | collective-permute-start | bytes 6291464 | tf_op jit(solution)/shard_map/ppermute | solution.py:739
  297.7 36.4 %collective-permute-start.70 = (bf16[512,1024]{1,0:T(8,128)(2,1)}, bf16[512,1024]{1,0:T(8,128)(2,1)}, u32[]{:S(2)}, u32[]{:S(2)}) collective-permute-start(bf16[512,1024]{1,0:T(8,128)(2,1)} %copy-done.91), channel_id=1, source_target_pairs={{0,8},{8,0},{16,24},{24,16},{1,9},{9,1},{17,25},{25,17},{2,10},{10... | collective-permute-start | bytes 3145736 | tf_op jit(solution)/shard_map/ppermute | solution.py:739
  297.8 36.3 %collective-permute-start.71 = (bf16[512,1024]{1,0:T(8,128)(2,1)}, bf16[512,1024]{1,0:T(8,128)(2,1)}, u32[]{:S(2)}, u32[]{:S(2)}) collective-permute-start(bf16[512,1024]{1,0:T(8,128)(2,1)} %copy-done.90), channel_id=1, source_target_pairs={{0,8},{8,0},{16,24},{24,16},{1,9},{9,1},{17,25},{25,17},{2,10},{10... | collective-permute-start | bytes 3145736 | tf_op jit(solution)/shard_map/ppermute | solution.py:739
  341.9 59.4 %all-to-all-start = ((bf16[8,64,2048]{2,1,0:T(8,128)(2,1)}), bf16[8,64,2048]{2,1,0:T(8,128)(2,1)}, u32[]{:S(2)}, u32[]{:S(2)}) async-start(bf16[8,64,2048]{2,1,0:T(8,128)(2,1)} %bitcast.22), calls=%async_computation | async-start | bytes 4194304 | tf_op jit(solution)/shard_map/all_to_all | solution.py:1105
  352.5 37.2 %collective-permute-start.76 = (bf16[512,1024]{1,0:T(8,128)(2,1)S(1)}, bf16[512,1024]{1,0:T(8,128)(2,1)S(1)}, u32[]{:S(2)}, u32[]{:S(2)}) collective-permute-start(bf16[512,1024]{1,0:T(8,128)(2,1)S(1)} %get-tuple-element.637), channel_id=1, source_target_pairs={{0,8},{8,0},{16,24},{24,16},{1,9},{9,1},{17,25},{25,17},{2,10},{10... | collective-permute-start | bytes 3145736 | tf_op jit(solution)/shard_map/ppermute | solution.py:739
  352.5 37.2 %collective-permute-start.77 = (bf16[512,1024]{1,0:T(8,128)(2,1)S(1)}, bf16[512,1024]{1,0:T(8,128)(2,1)S(1)}, u32[]{:S(2)}, u32[]{:S(2)}) collective-permute-start(bf16[512,1024]{1,0:T(8,128)(2,1)S(1)} %get-tuple-element.638), channel_id=1, source_target_pairs={{0,8},{8,0},{16,24},{24,16},{1,9},{9,1},{17,25},{25,17},{2,10},{10... | collective-permute-start | bytes 3145736 | tf_op jit(solution)/shard_map/ppermute | solution.py:739
  392.8 51.0 %collective-permute-start.88 = (bf16[512,2048]{1,0:T(8,128)(2,1)}, bf16[512,2048]{1,0:T(8,128)(2,1)}, u32[]{:S(2)}, u32[]{:S(2)}) collective-permute-start(bf16[512,2048]{1,0:T(8,128)(2,1)} %tn_blocks.21), channel_id=1, source_target_pairs={{0,16},{8,24},{16,0},{24,8},{1,17},{9,25},{17,1},{25,9},{2,18},{10... | collective-permute-start | bytes 6291464 | tf_op jit(solution)/shard_map/ppermute | solution.py:739
  418.3 26.4 %collective-permute-start.86 = (bf16[512,1024]{1,0:T(8,128)(2,1)}, bf16[512,1024]{1,0:T(8,128)(2,1)}, u32[]{:S(2)}, u32[]{:S(2)}) collective-permute-start(bf16[512,1024]{1,0:T(8,128)(2,1)} %get-tuple-element.635), channel_id=1, source_target_pairs={{0,8},{8,0},{16,24},{24,16},{1,9},{9,1},{17,25},{25,17},{2,10},{10... | collective-permute-start | bytes 3145736 | tf_op jit(solution)/shard_map/ppermute | solution.py:739
  418.3 27.6 %collective-permute-start.87 = (bf16[512,1024]{1,0:T(8,128)(2,1)}, bf16[512,1024]{1,0:T(8,128)(2,1)}, u32[]{:S(2)}, u32[]{:S(2)}) collective-permute-start(bf16[512,1024]{1,0:T(8,128)(2,1)} %get-tuple-element.636), channel_id=1, source_target_pairs={{0,8},{8,0},{16,24},{24,16},{1,9},{9,1},{17,25},{25,17},{2,10},{10... | collective-permute-start | bytes 3145736 | tf_op jit(solution)/shard_map/ppermute | solution.py:739
  445.9 64.0 %collective-permute-start.105 = (bf16[512,2048]{1,0:T(8,128)(2,1)}, bf16[512,2048]{1,0:T(8,128)(2,1)}, u32[]{:S(2)}, u32[]{:S(2)}) collective-permute-start(bf16[512,2048]{1,0:T(8,128)(2,1)} %tn_blocks.23), channel_id=1, source_target_pairs={{0,16},{8,24},{16,0},{24,8},{1,17},{9,25},{17,1},{25,9},{2,18},{10... | collective-permute-start | bytes 6291464 | tf_op jit(solution)/shard_map/ppermute | solution.py:739
  509.9 26.4 %collective-permute-start.112 = (bf16[512,512]{1,0:T(8,128)(2,1)}, bf16[512,512]{1,0:T(8,128)(2,1)}, u32[]{:S(2)}, u32[]{:S(2)}) collective-permute-start(bf16[512,512]{1,0:T(8,128)(2,1)} %copy-done.93), channel_id=1, source_target_pairs={{0,8},{8,0},{16,24},{24,16},{1,9},{9,1},{17,25},{25,17},{2,10},{10... | collective-permute-start | bytes 1572872 | tf_op jit(solution)/shard_map/ppermute | solution.py:739
  510.3 26.0 %collective-permute-start.113 = (bf16[512,512]{1,0:T(8,128)(2,1)}, bf16[512,512]{1,0:T(8,128)(2,1)}, u32[]{:S(2)}, u32[]{:S(2)}) collective-permute-start(bf16[512,512]{1,0:T(8,128)(2,1)} %copy-done.92), channel_id=1, source_target_pairs={{0,8},{8,0},{16,24},{24,16},{1,9},{9,1},{17,25},{25,17},{2,10},{10... | collective-permute-start | bytes 1572872 | tf_op jit(solution)/shard_map/ppermute | solution.py:739
  (228 other events, 2822.0 us)

commit v6 on v5

--- a/solution.py
+++ b/solution.py
@@ -345,14 +345,15 @@
 def project(rows, cosine, sine, weights, turned_tiles, scale, micros):
     count, depth = rows.shape
     size, width = weights[0][0].shape
-    part = 256 // len(weights)
+    run = 512 // len(weights)
+    part = run // len(weights)
     whole = lambda a: pl.BlockSpec(a.shape, lambda j: (0, 0))
     return pl.pallas_call(
         functools.partial(project_kernel, scale, turned_tiles),
         grid=(width // part,),
         in_specs=[whole(rows), whole(cosine), whole(sine)]
         + [pl.BlockSpec((size, part), lambda j: (0, j))] * (4 * len(weights)),
-        out_specs=pl.BlockSpec((count, 256), lambda j: (0, j)),
+        out_specs=pl.BlockSpec((count, run), lambda j: (0, j)),
         out_shape=jax.ShapeDtypeStruct((count, width * len(weights)), BF),
         compiler_params=params(32),
         cost_estimate=cost(micros),
@@ -380,9 +381,9 @@
     whole = lambda a: pl.BlockSpec(a.shape, lambda j: (0, 0))
     return pl.pallas_call(
         out_kernel,
-        grid=(width // 256,),
+        grid=(width // 512,),
         in_specs=[smem(), whole(mixed), whole(tokens), whole(gain)]
-        + [pl.BlockSpec((size, 256), lambda j: (0, j))] * 4,
+        + [pl.BlockSpec((size, 512), lambda j: (0, j))] * 4,
         out_specs=[whole(tokens), whole(tokens)],
         out_shape=[
             jax.ShapeDtypeStruct((count, width), F32),
@@ -992,7 +993,7 @@
     out_parts.send()
     kv_chunks = [kv.chunks[r] for r in rel]
 
-    queries = order.run(project, hidden_one, cosine, sine, [weight_q], turned_tiles=2, scale=0.125, micros=7)
+    queries = order.run(project, hidden_one, cosine, sine, [weight_q], turned_tiles=4, scale=0.125, micros=7)
     out_parts.rest()
     out_parts.take()
     gate = shards(gate_own, gate_core, order.take(gate_across))

time: 584 us -> 581 us (level)
  transfers between devices with their start and end apart: 131 -> 131, of which waited for: 49 -> 48; matrix products, arithmetic and copies ran while one was open for 9% -> 9% of each run, Pallas kernels for 35% -> 35%
where the time goes in v6:
time: 581 us; the launch traced here: 573 us
  Pallas kernels  218 us (38%)
  waiting for transfers between devices  139 us (24%)
  starting transfers between devices  114 us (20%)
  local copies, waits for them, and re-layouts  60.7 us (10%)
  other arithmetic  38.5 us (7%)
    ppermute x80, waiting for transfers between devices, ring_shift(): lax.ppermute(value, 'ctx', [(order[i], order[(i + step) % n]) for i in ra...  116 us
    ppermute x80, starting transfers between devices, ring_shift(): lax.ppermute(value, 'ctx', [(order[i], order[(i + step) % n]) for i in ra...  86.7 us
    pallas_call x15, Pallas kernels, tn_blocks(): pl.pallas_call(functools.partial(tn_kernel, windows, outs), grid=(len(blo...  71.8 us
    pallas_call x4, Pallas kernels, feed(): pl.pallas_call(functools.partial(feed_kernel, m, len(kept), crossed), gri...  59.4 us
    unnamed x246, local copies, waits for them, and re-layouts  41.6 us
    pallas_call x2, Pallas kernels, attention_backward(): pl.pallas_call(functools.partial(backward_kernel, n, group, ends, first),...  27.4 us
    ppermute x49, waiting for transfers between devices, swap_fsdp(): return lax.ppermute(value, 'fsdp', [(i, i ^ d) for i in range(4)])  22.8 us
    ppermute x49, starting transfers between devices, swap_fsdp(): return lax.ppermute(value, 'fsdp', [(i, i ^ d) for i in range(4)])  20.2 us
  transfers between devices with their start and end apart: 131, of which 48 were waited for; matrix products, arithmetic and copies ran while one was open for 9% of the time, Pallas kernels for 35%

profile of v6, /device:TPU:0, one launch (start us, length us, event | category | flops | bytes accessed | tf_op | source)
XLA Modules:
  0.0 573.5 jit_solution(12093086937817426960)
XLA Ops:
  19.7 6.7 %collective-permute-done.8.refs_2_.refs_4_ = bf16[512,512]{1,0:T(8,128)(2,1)S(1)} collective-permute-done((bf16[512,512]{1,0:T(8,128)(2,1)}, bf16[512,512]{1,0:T(8,128)(2,1)S(1)}, u32[]{:S(2)}, u32[]{:S(2)}) %collective-permute-start.8) | collective-permute-done | bytes 524320 | tf_op jit(solution)/shard_map/ppermute | solution.py:740
  27.9 7.4 %collective-permute-done.6.refs_2_ = bf16[64,2048]{1,0:T(8,128)(2,1)S(1)} collective-permute-done((bf16[64,2048]{1,0:T(8,128)(2,1)S(1)}, bf16[64,2048]{1,0:T(8,128)(2,1)S(1)}, u32[]{:S(2)}, u32[]{:S(2)}) %collective-permute-start.6) | collective-permute-done | bytes 262176 | tf_op jit(solution)/shard_map/ppermute | solution.py:778
  59.4 8.1 %collective-permute-done.20.rest_2_ = bf16[160,1024]{1,0:T(8,128)(2,1)S(1)} collective-permute-done((bf16[160,1024]{1,0:T(8,128)(2,1)S(1)}, bf16[160,1024]{1,0:T(8,128)(2,1)S(1)}, u32[]{:S(2)}, u32[]{:S(2)}) %collective-permute-start.20) | collective-permute-done | bytes 327712 | tf_op jit(solution)/shard_map/ppermute | solution.py:778
  72.8 6.6 %collective-permute-done.22.rest_1_ = bf16[160,1024]{1,0:T(8,128)(2,1)S(1)} collective-permute-done((bf16[160,1024]{1,0:T(8,128)(2,1)S(1)}, bf16[160,1024]{1,0:T(8,128)(2,1)S(1)}, u32[]{:S(2)}, u32[]{:S(2)}) %collective-permute-start.22) | collective-permute-done | bytes 327712 | tf_op jit(solution)/shard_map/ppermute | solution.py:778
  89.2 7.8 %collective-permute-done.25.rest_0_ = bf16[160,1024]{1,0:T(8,128)(2,1)S(1)} collective-permute-done((bf16[160,1024]{1,0:T(8,128)(2,1)S(1)}, bf16[160,1024]{1,0:T(8,128)(2,1)S(1)}, u32[]{:S(2)}, u32[]{:S(2)}) %collective-permute-start.25) | collective-permute-done | bytes 327712 | tf_op jit(solution)/shard_map/ppermute | solution.py:778
  116.4 16.0 %attention_forward.1 = (bf16[160,2048]{1,0:T(8,128)(2,1)S(1)}, f32[160,128]{1,0:T(8,128)S(1)}) custom-call(s32[23]{0:T(128)S(1)} %pad_add_fusion.f_ref.sc, bf16[160,2048]{1,0:T(8,128)(2,1)S(1)} %project.3.q_ref, bf16[160,1024]{1,0:T(8,128)(2,1)S(1)} %collective-permute-done.25.rest_0_, bf16[160,1024]{1,0:T(8,128)(2,1)S(1)} %collective-permute-done.22.rest_1_, ...), custom_call_target="tpu_custom_call" | custom-call | flops 180000000 | tf_op jit(solution)/shard_map/attention_forward/pallas_call | solution.py:131
  149.3 12.9 %collective-permute-done.37.refs_0_ = bf16[160,2048]{1,0:T(8,128)(2,1)S(1)} collective-permute-done((bf16[160,2048]{1,0:T(8,128)(2,1)S(1)}, bf16[160,2048]{1,0:T(8,128)(2,1)S(1)}, u32[]{:S(2)}, u32[]{:S(2)}) %collective-permute-start.37) | collective-permute-done | bytes 655392 | tf_op jit(solution)/shard_map/ppermute | solution.py:778
  173.5 19.5 %feed.4 = (bf16[1280,2048]{1,0:T(8,128)(2,1)}, bf16[1280,2048]{1,0:T(8,128)(2,1)}, bf16[1280,1024]{1,0:T(8,128)(2,1)}, bf16[1280,2048]{1,0:T(8,128)(2,1)}, bf16[480,2048]{1,0:T(8,128)(2,1)}) custom-call(bf16[160,2048]{1,0:T(8,128)(2,1)S(1)} %collective-permute-done.37.refs_0_, bf16[160,2048]{1,0:T(8,128)(2,1)S(1)} %copy-done.73, ...), custom_call_target="tpu_custom_call" | custom-call | flops 200000000 | tf_op jit(solution)/shard_map/feed/pallas_call | solution.py:561
  201.0 14.5 %feed.5 = (bf16[1280,2048]{1,0:T(8,128)(2,1)}, bf16[1280,2048]{1,0:T(8,128)(2,1)}, bf16[1280,1024]{1,0:T(8,128)(2,1)}, bf16[1280,2048]{1,0:T(8,128)(2,1)}, bf16[320,2048]{1,0:T(8,128)(2,1)}) custom-call(bf16[160,2048]{1,0:T(8,128)(2,1)S(1)} %collective-permute-done.39.refs_0_, ...), custom_call_target="tpu_custom_call", output_to_operand_aliasing={{0}: (13, {}), {1}: (14, {}), {2}: (15, {}), {3}: (16, {})} | custom-call | flops 160000000 | tf_op jit(solution)/shard_map/feed/pallas_call | solution.py:561
  219.8 14.5 %feed.6 = (bf16[1280,2048]{1,0:T(8,128)(2,1)}, bf16[1280,2048]{1,0:T(8,128)(2,1)}, bf16[1280,1024]{1,0:T(8,128)(2,1)}, bf16[1280,2048]{1,0:T(8,128)(2,1)}, bf16[320,2048]{1,0:T(8,128)(2,1)}) custom-call(bf16[160,2048]{1,0:T(8,128)(2,1)S(1)} %collective-permute-done.48.refs_0_, ...), custom_call_target="tpu_custom_call", output_to_operand_aliasing={{0}: (13, {}), {1}: (14, {}), {2}: (15, {}), {3}: (16, {})} | custom-call | flops 160000000 | tf_op jit(solution)/shard_map/feed/pallas_call | solution.py:561
  235.5 11.0 %feed.7 = (bf16[1280,2048]{1,0:T(8,128)(2,1)}, bf16[1280,2048]{1,0:T(8,128)(2,1)}, bf16[1280,1024]{1,0:T(8,128)(2,1)}, bf16[1280,2048]{1,0:T(8,128)(2,1)}, bf16[160,2048]{1,0:T(8,128)(2,1)S(1)}) custom-call(bf16[160,2048]{1,0:T(8,128)(2,1)S(1)} %pad_maximum_fusion.3.refs_0_, ...), custom_call_target="tpu_custom_call", output_to_operand_aliasing={{0}: (11, {}), {1}: (12, {}), {2}: (13, {}), {3}: (14, {})} | custom-call | flops 120000000 | tf_op jit(solution)/shard_map/feed/pallas_call | solution.py:561
  253.7 10.0 %tn_blocks.15 = (bf16[512,1024]{1,0:T(8,128)(2,1)S(1)}, bf16[512,1024]{1,0:T(8,128)(2,1)S(1)}, bf16[512,1024]{1,0:T(8,128)(2,1)S(1)}, bf16[512,1024]{1,0:T(8,128)(2,1)S(1)}) custom-call(bf16[1280,2048]{1,0:T(8,128)(2,1)S(1)} %copy-done, bf16[1280,2048]{1,0:T(8,128)(2,1)S(1)} %copy-done.1), custom_call_target="tpu_custom_call" | custom-call | flops 100000000 | tf_op jit(solution)/shard_map/tn_blocks/pallas_call | solution.py:694
  270.0 7.6 %tn_blocks.16 = (bf16[256,1024]{1,0:T(8,128)(2,1)}, bf16[256,1024]{1,0:T(8,128)(2,1)}, bf16[256,1024]{1,0:T(8,128)(2,1)}, bf16[256,1024]{1,0:T(8,128)(2,1)}) custom-call(bf16[1280,1024]{1,0:T(8,128)(2,1)S(1)} %copy-done.5, bf16[1280,2048]{1,0:T(8,128)(2,1)S(1)} %copy-done.3), custom_call_target="tpu_custom_call" | custom-call | flops 60000000 | tf_op jit(solution)/shard_map/tn_blocks/pallas_call | solution.py:694
  277.7 5.7 tn_blocks.17
  288.5 6.1 %down_rows.1 = bf16[1280,2048]{1,0:T(8,128)(2,1)S(1)} custom-call(bf16[1280,1024]{1,0:T(8,128)(2,1)S(1)} %copy-done.5, bf16[1024,2048]{1,0:T(8,128)(2,1)S(1)} %copy-done.4), custom_call_target="tpu_custom_call" | custom-call | flops 80000000 | tf_op jit(solution)/shard_map/down_rows/pallas_call | solution.py:591
  309.0 11.5 %collective-permute-done.68.rest_1_ = bf16[160,2048]{1,0:T(8,128)(2,1)S(1)} collective-permute-done((bf16[160,2048]{1,0:T(8,128)(2,1)S(1)}, bf16[160,2048]{1,0:T(8,128)(2,1)S(1)}, u32[]{:S(2)}, u32[]{:S(2)}) %collective-permute-start.68) | collective-permute-done | bytes 655392 | tf_op jit(solution)/shard_map/ppermute | solution.py:778
  330.8 6.5 %tn_blocks.19 = bf16[512,2048]{1,0:T(8,128)(2,1)S(1)} custom-call(bf16[1280,2048]{1,0:T(8,128)(2,1)S(1)} %bitcast.17, bf16[1280,2048]{1,0:T(8,128)(2,1)S(1)} %copy-done.2, bf16[512,1024]{1,0:T(8,128)(2,1)} %collective-permute-done.70.refs_0_, bf16[512,1024]{1,0:T(8,128)(2,1)} %collective-permute-done.71.refs_1_, ...), custom_call_target="tpu_custom_call" | custom-call | flops 50000000 | tf_op jit(solution)/shard_map/tn_blocks/pallas_call | solution.py:694
  343.9 5.6 tn_blocks.20
  350.0 13.5 %attention_backward.2 = (bf16[160,1024]{1,0:T(8,128)(2,1)}, bf16[1280,512]{1,0:T(8,128)(2,1)}) custom-call(s32[23]{0:T(128)} %copy-done.84, bf16[160,2048]{1,0:T(8,128)(2,1)} %copy-done.12, bf16[160,2048]{1,0:T(8,128)(2,1)} %copy-done.35, f32[160,128]{1,0:T(8,128)} %copy-done.77, f32[160,128]{1,0:T(8,128)} %copy-done.64, f32[160,128]{1,0:T(8,128)} %copy-done.33, ...), custom_call_target="tpu_custom_call" | custom-call | flops 260000000 | tf_op jit(solution)/shard_map/attention_backward/pallas_call | solution.py:236
  366.9 13.9 %attention_backward.3 = (bf16[160,1024]{1,0:T(8,128)(2,1)}, bf16[1280,512]{1,0:T(8,128)(2,1)}) custom-call(s32[23]{0:T(128)} %copy-done.84, bf16[160,2048]{1,0:T(8,128)(2,1)} %copy-done.12, bf16[160,2048]{1,0:T(8,128)(2,1)} %copy-done.35, f32[160,128]{1,0:T(8,128)} %copy-done.77, f32[160,128]{1,0:T(8,128)} %copy-done.64, f32[160,128]{1,0:T(8,128)} %copy-done.33, ...), custom_call_target="tpu_custom_call" | custom-call | flops 260000000 | tf_op jit(solution)/shard_map/attention_backward/pallas_call | solution.py:236
  390.8 5.3 tn_blocks.22
  416.1 5.8 %collective-permute-done.81 = bf16[160,1024]{1,0:T(8,128)(2,1)} collective-permute-done((bf16[160,1024]{1,0:T(8,128)(2,1)S(1)}, bf16[160,1024]{1,0:T(8,128)(2,1)}, u32[]{:S(2)}, u32[]{:S(2)}) %collective-permute-start.81) | collective-permute-done | bytes 327712 | tf_op jit(solution)/shard_map/ppermute | solution.py:778
  459.6 6.2 %spread.1 = (f32[64,8192]{1,0:T(8,128)}, f32[64,8192]{1,0:T(8,128)}) custom-call(s32[23]{0:T(128)S(1)} %copy-done.85, bf16[8,64,2048]{2,1,0:T(8,128)(2,1)} %all-to-all-done.all_ref), custom_call_target="tpu_custom_call" | custom-call | flops 40000000 | tf_op jit(solution)/shard_map/spread/pallas_call | solution.py:727
  525.9 7.0 %collective-permute-done.114.refs_2_ = bf16[512,1024]{1,0:T(8,128)(2,1)} collective-permute-done((bf16[512,1024]{1,0:T(8,128)(2,1)}, bf16[512,1024]{1,0:T(8,128)(2,1)}, u32[]{:S(2)}, u32[]{:S(2)}) %collective-permute-start.114) | collective-permute-done | bytes 1048608 | tf_op jit(solution)/shard_map/ppermute | solution.py:740
  (636 shorter events, 341.2 us)
Async XLA Ops:
  8.1 29.3 %collective-permute-start.4 = (bf16[512,512]{1,0:T(8,128)(2,1)}, bf16[512,512]{1,0:T(8,128)(2,1)}, u32[]{:S(2)}, u32[]{:S(2)}) collective-permute-start(bf16[512,512]{1,0:T(8,128)(2,1)} %refs_6_), channel_id=1, source_target_pairs={{0,16},{8,24},{16,0},{24,8},{1,17},{9,25},{17,1},{25,9},{2,18},{10... | collective-permute-start | bytes 1572872 | tf_op jit(solution)/shard_map/ppermute | solution.py:740
  12.1 30.1 %collective-permute-start.18 = (bf16[160,2048]{1,0:T(8,128)(2,1)}, bf16[160,2048]{1,0:T(8,128)(2,1)}, u32[]{:S(2)}, u32[]{:S(2)}) collective-permute-start(bf16[160,2048]{1,0:T(8,128)(2,1)} %base_ref), channel_id=1, source_target_pairs={{0,2},{2,4},{4,6},{6,7},{7,5},{5,3},{3,1},{1,0},{8,10},{10,12},{12... | collective-permute-start | bytes 1966088 | tf_op jit(solution)/shard_map/ppermute | solution.py:778
  37.4 47.5 %collective-permute-start.9 = (bf16[512,2048]{1,0:T(8,128)(2,1)}, bf16[512,2048]{1,0:T(8,128)(2,1)S(1)}, u32[]{:S(2)}, u32[]{:S(2)}) collective-permute-start(bf16[512,2048]{1,0:T(8,128)(2,1)} %refs_1_.1), channel_id=1, source_target_pairs={{0,16},{8,24},{16,0},{24,8},{1,17},{9,25},{17,1},{25,9},{2,18},{10... | collective-permute-start | bytes 6291464 | tf_op jit(solution)/shard_map/ppermute | solution.py:740
  79.4 26.3 %collective-permute-start.3 = (bf16[512,2048]{1,0:T(8,128)(2,1)S(1)}, bf16[512,2048]{1,0:T(8,128)(2,1)S(1)}, u32[]{:S(2)}, u32[]{:S(2)}) collective-permute-start(bf16[512,2048]{1,0:T(8,128)(2,1)S(1)} %copy-done.18), channel_id=1, source_target_pairs={{0,8},{8,0},{16,24},{24,16},{1,9},{9,1},{17,25},{25,17},{2,10},{10... | collective-permute-start | bytes 6291464 | tf_op jit(solution)/shard_map/ppermute | solution.py:740
  105.7 33.7 %collective-permute-start.32 = (bf16[512,2048]{1,0:T(8,128)(2,1)S(1)}, bf16[512,2048]{1,0:T(8,128)(2,1)}, u32[]{:S(2)}, u32[]{:S(2)}) collective-permute-start(bf16[512,2048]{1,0:T(8,128)(2,1)S(1)} %copy-done.16), channel_id=1, source_target_pairs={{0,8},{8,0},{16,24},{24,16},{1,9},{9,1},{17,25},{25,17},{2,10},{10... | collective-permute-start | bytes 6291464 | tf_op jit(solution)/shard_map/ppermute | solution.py:740
  112.5 26.9 %collective-permute-start.33 = (bf16[512,2048]{1,0:T(8,128)(2,1)S(1)}, bf16[512,2048]{1,0:T(8,128)(2,1)S(1)}, u32[]{:S(2)}, u32[]{:S(2)}) collective-permute-start(bf16[512,2048]{1,0:T(8,128)(2,1)S(1)} %place_rows.1.w2.refs_3_), channel_id=1, source_target_pairs={{0,8},{8,0},{16,24},{24,16},{1,9},{9,1},{17,25},{25,17},{2,10},{10... | collective-permute-start | bytes 6291464 | tf_op jit(solution)/shard_map/ppermute | solution.py:740
  138.3 26.8 %collective-permute-start.46 = (bf16[256,2048]{1,0:T(8,128)(2,1)}, bf16[256,2048]{1,0:T(8,128)(2,1)S(1)}, u32[]{:S(2)}, u32[]{:S(2)}) collective-permute-start(bf16[256,2048]{1,0:T(8,128)(2,1)} %constant_dynamic-slice_fusion.6), channel_id=1, source_target_pairs={{0,16},{8,24},{16,0},{24,8},{1,17},{9,25},{17,1},{25,9},{2,18},{10... | collective-permute-start | bytes 3145736 | tf_op jit(solution)/shard_map/ppermute | solution.py:740
  165.6 27.4 %collective-permute-start.39 = (bf16[160,2048]{1,0:T(8,128)(2,1)S(1)}, bf16[160,2048]{1,0:T(8,128)(2,1)S(1)}, u32[]{:S(2)}, u32[]{:S(2)}) collective-permute-start(bf16[160,2048]{1,0:T(8,128)(2,1)S(1)} %collective-permute-done.37.refs_0_), channel_id=1, source_target_pairs={{0,2},{2,4},{4,6},{6,7},{7,5},{5,3},{3,1},{1,0},{8,10},{10,12},{12... | collective-permute-start | bytes 1966088 | tf_op jit(solution)/shard_map/ppermute | solution.py:778
  167.1 25.9 %collective-permute-start.40 = (bf16[160,2048]{1,0:T(8,128)(2,1)S(1)}, bf16[160,2048]{1,0:T(8,128)(2,1)S(1)}, u32[]{:S(2)}, u32[]{:S(2)}) collective-permute-start(bf16[160,2048]{1,0:T(8,128)(2,1)S(1)} %collective-permute-done.38.refs_2_), channel_id=1, source_target_pairs={{0,1},{2,0},{4,2},{6,4},{7,6},{5,7},{3,5},{1,3},{8,9},{10,8},{12,1... | collective-permute-start | bytes 1966088 | tf_op jit(solution)/shard_map/ppermute | solution.py:778
  167.7 29.5 %collective-permute-start.50 = (bf16[160,2048]{1,0:T(8,128)(2,1)S(1)}, bf16[160,2048]{1,0:T(8,128)(2,1)S(1)}, u32[]{:S(2)}, u32[]{:S(2)}) collective-permute-start(bf16[160,2048]{1,0:T(8,128)(2,1)S(1)} %copy-done.75), channel_id=1, source_target_pairs={{0,2},{2,4},{4,6},{6,7},{7,5},{5,3},{3,1},{1,0},{8,10},{10,12},{12... | collective-permute-start | bytes 1966088 | tf_op jit(solution)/shard_map/ppermute | solution.py:778
  170.7 28.1 %collective-permute-start.51 = (bf16[160,2048]{1,0:T(8,128)(2,1)}, bf16[160,2048]{1,0:T(8,128)(2,1)S(1)}, u32[]{:S(2)}, u32[]{:S(2)}) collective-permute-start(bf16[160,2048]{1,0:T(8,128)(2,1)} %collective-permute-done.35.refs_3_), channel_id=1, source_target_pairs={{0,1},{2,0},{4,2},{6,4},{7,6},{5,7},{3,5},{1,3},{8,9},{10,8},{12,1... | collective-permute-start | bytes 1966088 | tf_op jit(solution)/shard_map/ppermute | solution.py:778
  283.4 47.4 %collective-permute-start.72 = (bf16[512,2048]{1,0:T(8,128)(2,1)}, bf16[512,2048]{1,0:T(8,128)(2,1)}, u32[]{:S(2)}, u32[]{:S(2)}) collective-permute-start(bf16[512,2048]{1,0:T(8,128)(2,1)} %tn_blocks.17), channel_id=1, source_target_pairs={{0,16},{8,24},{16,0},{24,8},{1,17},{9,25},{17,1},{25,9},{2,18},{10... | collective-permute-start | bytes 6291464 | tf_op jit(solution)/shard_map/ppermute | solution.py:740
  294.7 36.1 %collective-permute-start.70 = (bf16[512,1024]{1,0:T(8,128)(2,1)}, bf16[512,1024]{1,0:T(8,128)(2,1)}, u32[]{:S(2)}, u32[]{:S(2)}) collective-permute-start(bf16[512,1024]{1,0:T(8,128)(2,1)} %copy-done.91), channel_id=1, source_target_pairs={{0,8},{8,0},{16,24},{24,16},{1,9},{9,1},{17,25},{25,17},{2,10},{10... | collective-permute-start | bytes 3145736 | tf_op jit(solution)/shard_map/ppermute | solution.py:740
  294.8 36.0 %collective-permute-start.71 = (bf16[512,1024]{1,0:T(8,128)(2,1)}, bf16[512,1024]{1,0:T(8,128)(2,1)}, u32[]{:S(2)}, u32[]{:S(2)}) collective-permute-start(bf16[512,1024]{1,0:T(8,128)(2,1)} %copy-done.90), channel_id=1, source_target_pairs={{0,8},{8,0},{16,24},{24,16},{1,9},{9,1},{17,25},{25,17},{2,10},{10... | collective-permute-start | bytes 3145736 | tf_op jit(solution)/shard_map/ppermute | solution.py:740
  338.6 60.1 %all-to-all-start = ((bf16[8,64,2048]{2,1,0:T(8,128)(2,1)}), bf16[8,64,2048]{2,1,0:T(8,128)(2,1)}, u32[]{:S(2)}, u32[]{:S(2)}) async-start(bf16[8,64,2048]{2,1,0:T(8,128)(2,1)} %bitcast.22), calls=%async_computation | async-start | bytes 4194304 | tf_op jit(solution)/shard_map/all_to_all | solution.py:1106
  349.5 37.3 %collective-permute-start.76 = (bf16[512,1024]{1,0:T(8,128)(2,1)S(1)}, bf16[512,1024]{1,0:T(8,128)(2,1)S(1)}, u32[]{:S(2)}, u32[]{:S(2)}) collective-permute-start(bf16[512,1024]{1,0:T(8,128)(2,1)S(1)} %get-tuple-element.637), channel_id=1, source_target_pairs={{0,8},{8,0},{16,24},{24,16},{1,9},{9,1},{17,25},{25,17},{2,10},{10... | collective-permute-start | bytes 3145736 | tf_op jit(solution)/shard_map/ppermute | solution.py:740
  349.5 37.3 %collective-permute-start.77 = (bf16[512,1024]{1,0:T(8,128)(2,1)S(1)}, bf16[512,1024]{1,0:T(8,128)(2,1)S(1)}, u32[]{:S(2)}, u32[]{:S(2)}) collective-permute-start(bf16[512,1024]{1,0:T(8,128)(2,1)S(1)} %get-tuple-element.638), channel_id=1, source_target_pairs={{0,8},{8,0},{16,24},{24,16},{1,9},{9,1},{17,25},{25,17},{2,10},{10... | collective-permute-start | bytes 3145736 | tf_op jit(solution)/shard_map/ppermute | solution.py:740
  390.0 51.0 %collective-permute-start.88 = (bf16[512,2048]{1,0:T(8,128)(2,1)}, bf16[512,2048]{1,0:T(8,128)(2,1)}, u32[]{:S(2)}, u32[]{:S(2)}) collective-permute-start(bf16[512,2048]{1,0:T(8,128)(2,1)} %tn_blocks.21), channel_id=1, source_target_pairs={{0,16},{8,24},{16,0},{24,8},{1,17},{9,25},{17,1},{25,9},{2,18},{10... | collective-permute-start | bytes 6291464 | tf_op jit(solution)/shard_map/ppermute | solution.py:740
  415.6 26.4 %collective-permute-start.86 = (bf16[512,1024]{1,0:T(8,128)(2,1)}, bf16[512,1024]{1,0:T(8,128)(2,1)}, u32[]{:S(2)}, u32[]{:S(2)}) collective-permute-start(bf16[512,1024]{1,0:T(8,128)(2,1)} %get-tuple-element.635), channel_id=1, source_target_pairs={{0,8},{8,0},{16,24},{24,16},{1,9},{9,1},{17,25},{25,17},{2,10},{10... | collective-permute-start | bytes 3145736 | tf_op jit(solution)/shard_map/ppermute | solution.py:740
  415.6 27.4 %collective-permute-start.87 = (bf16[512,1024]{1,0:T(8,128)(2,1)}, bf16[512,1024]{1,0:T(8,128)(2,1)}, u32[]{:S(2)}, u32[]{:S(2)}) collective-permute-start(bf16[512,1024]{1,0:T(8,128)(2,1)} %get-tuple-element.636), channel_id=1, source_target_pairs={{0,8},{8,0},{16,24},{24,16},{1,9},{9,1},{17,25},{25,17},{2,10},{10... | collective-permute-start | bytes 3145736 | tf_op jit(solution)/shard_map/ppermute | solution.py:740
  442.9 63.5 %collective-permute-start.105 = (bf16[512,2048]{1,0:T(8,128)(2,1)}, bf16[512,2048]{1,0:T(8,128)(2,1)}, u32[]{:S(2)}, u32[]{:S(2)}) collective-permute-start(bf16[512,2048]{1,0:T(8,128)(2,1)} %tn_blocks.23), channel_id=1, source_target_pairs={{0,16},{8,24},{16,0},{24,8},{1,17},{9,25},{17,1},{25,9},{2,18},{10... | collective-permute-start | bytes 6291464 | tf_op jit(solution)/shard_map/ppermute | solution.py:740
  506.5 26.4 %collective-permute-start.112 = (bf16[512,512]{1,0:T(8,128)(2,1)}, bf16[512,512]{1,0:T(8,128)(2,1)}, u32[]{:S(2)}, u32[]{:S(2)}) collective-permute-start(bf16[512,512]{1,0:T(8,128)(2,1)} %copy-done.93), channel_id=1, source_target_pairs={{0,8},{8,0},{16,24},{24,16},{1,9},{9,1},{17,25},{25,17},{2,10},{10... | collective-permute-start | bytes 1572872 | tf_op jit(solution)/shard_map/ppermute | solution.py:740
  506.9 26.0 %collective-permute-start.113 = (bf16[512,512]{1,0:T(8,128)(2,1)}, bf16[512,512]{1,0:T(8,128)(2,1)}, u32[]{:S(2)}, u32[]{:S(2)}) collective-permute-start(bf16[512,512]{1,0:T(8,128)(2,1)} %copy-done.92), channel_id=1, source_target_pairs={{0,8},{8,0},{16,24},{24,16},{1,9},{9,1},{17,25},{25,17},{2,10},{10... | collective-permute-start | bytes 1572872 | tf_op jit(solution)/shard_map/ppermute | solution.py:740
  507.1 25.9 %collective-permute-start.114 = (bf16[512,1024]{1,0:T(8,128)(2,1)}, bf16[512,1024]{1,0:T(8,128)(2,1)}, u32[]{:S(2)}, u32[]{:S(2)}) collective-permute-start(bf16[512,1024]{1,0:T(8,128)(2,1)} %tn_blocks.27), channel_id=1, source_target_pairs={{0,16},{8,24},{16,0},{24,8},{1,17},{9,25},{17,1},{25,9},{2,18},{10... | collective-permute-start | bytes 3145736 | tf_op jit(solution)/shard_map/ppermute | solution.py:740
  (228 other events, 2794.6 us)
